TPU v7x, 256 devices: a whole 4x4x8 slice. The times are simulated.
256 devices in a mesh: tile: 8 (over z), frame: 32 (over y, x, core).
Axes of the slice: x: 4, y: 4, z: 8, core: 2. Of those that a mesh axis runs over, the one named last changes fastest.
Arguments:
- movie: bfloat16 [8, 32, 1024, 5760], P('tile', 'frame'), may hold values from -6 to 6
- frame_shift: int32 [8, 32, 2], P('tile', 'frame'), may hold values from -4 to 4
- intersection: int32 [8], replicated, may hold values from 0 to 512, as said below
- seam_shift: int32 [8], replicated, may hold values from 0 to 127
Outputs:
- micrograph: bfloat16 [8, 1024, 5760], P('tile', 'frame')
- seam_score: float32 [8, 128], P('tile')
Inputs may be any that keep to these rules, and one draw needn't show every extreme that they name: intersection[t] is 0 exactly where t % 8 == 8 - 1 (the last tile of a grid row), else between 128 and 512.
All inputs are finite; a program needn't handle non-finite values.
Results may differ from a plain program's by a relative error of at most 0.0048.
Values may be sent and summed in bfloat16 or wider, within the bound.
No kernel may reach another device: no remote copies, remote signals or barrier semaphores. Data moves between devices by JAX's collectives and lax.ppermute only.
A program may use at most 128 MiB of HBM per device.

v0:
```python
import math

import jax
import jax.numpy as jnp
from jax import lax
from jax.sharding import PartitionSpec as P

SHIFT = 4
STRIP = 512
LAGS = 128


def from_behind(array, axis, by):
    count = lax.axis_size(axis)
    pairs = [(i, i + by) for i in range(count) if 0 <= i + by < count]
    return lax.ppermute(array, axis, pairs)


def right_seam(own_right, next_left, seam_width, shift_now):
    strip_cols = own_right.shape[1]
    lag_count = next_left.shape[1] - strip_cols
    padded = jnp.pad(next_left, ((0, 0), (strip_cols, 0)))
    aligned = lax.dynamic_slice_in_dim(padded, seam_width, strip_cols + lag_count, 1)
    column = jnp.arange(strip_cols, dtype=jnp.int32)
    inside = column >= strip_cols - seam_width
    masked = jnp.where(inside[None, :], own_right, jnp.zeros_like(own_right))
    correlated = lax.conv_general_dilated(
        aligned[None],
        masked[None],
        (1,),
        "VALID",
        dimension_numbers=("NCH", "OIH", "NCH"),
        preferred_element_type=jnp.float32,
    )
    products = correlated[0, 0, :lag_count]
    shifted = lax.dynamic_slice_in_dim(padded, seam_width + shift_now, strip_cols, 1).astype(
        jnp.float32
    )
    feather = ((strip_cols - column).astype(jnp.float32) - 0.5) / jnp.maximum(seam_width, 1).astype(
        jnp.float32
    )
    own_value = own_right.astype(jnp.float32)
    blended = jnp.where(
        inside[None, :],
        feather[None, :] * own_value + (1.0 - feather[None, :]) * shifted,
        own_value,
    )
    return (products, blended)


def left_seam(own_left, prev_right, width_left, shift_left):
    strip_cols = prev_right.shape[1]
    lag_count = own_left.shape[1] - strip_cols
    padded = jnp.pad(prev_right, ((0, 0), (lag_count, strip_cols + lag_count)))
    previous = lax.dynamic_slice_in_dim(
        padded, lag_count + strip_cols - width_left - shift_left, strip_cols + lag_count, 1
    ).astype(jnp.float32)
    column = jnp.arange(strip_cols + lag_count, dtype=jnp.int32)
    inside = (column >= shift_left) & (column < shift_left + width_left)
    feather = ((width_left - column + shift_left).astype(jnp.float32) - 0.5) / jnp.maximum(
        width_left, 1
    ).astype(jnp.float32)
    own_value = own_left.astype(jnp.float32)
    return jnp.where(
        inside[None, :],
        feather[None, :] * previous + (1.0 - feather[None, :]) * own_value,
        own_value,
    )


def body(movie, frame_shift, intersection, seam_shift):
    frames = movie[0]
    moves = frame_shift[0]
    frame_count = frames.shape[0]
    rows_all = frames.shape[1]
    cols_all = frames.shape[2]
    devices_frame = lax.axis_size("frame")
    frames_all = frame_count * devices_frame

    def add_frame(running, element):
        one_frame, frame_move = element
        padded = jnp.pad(one_frame.astype(jnp.float32), ((SHIFT, SHIFT), (SHIFT, SHIFT)))
        moved = lax.dynamic_slice(
            padded, (SHIFT - frame_move[0], SHIFT - frame_move[1]), (rows_all, cols_all)
        )
        return (running + moved, None)

    partial_image, _ = lax.scan(
        add_frame, jnp.zeros((rows_all, cols_all), jnp.float32), (frames, moves)
    )
    band = lax.psum_scatter(partial_image, "frame", scatter_dimension=0, tiled=True)
    summed = (band * (1.0 / math.sqrt(frames_all))).astype(jnp.bfloat16)
    tile_index = lax.axis_index("tile")
    seam_width = intersection[tile_index]
    shift_now = seam_shift[tile_index]
    earlier = jnp.maximum(tile_index - 1, 0)
    width_left = jnp.where(tile_index > 0, intersection[earlier], 0)
    shift_left = jnp.where(tile_index > 0, seam_shift[earlier], 0)
    next_piece = from_behind(summed[:, : STRIP + LAGS], "tile", -1)
    prev_piece = from_behind(summed[:, cols_all - STRIP :], "tile", 1)
    products, right_part = right_seam(
        summed[:, cols_all - STRIP :], next_piece, seam_width, shift_now
    )
    left_part = left_seam(summed[:, : STRIP + LAGS], prev_piece, width_left, shift_left)
    products = lax.psum(products, "frame")
    middle = summed[:, STRIP + LAGS : cols_all - STRIP]
    tile_image = jnp.concatenate(
        [left_part.astype(jnp.bfloat16), middle, right_part.astype(jnp.bfloat16)], 1
    )
    score = products / jnp.sqrt((rows_all * jnp.maximum(seam_width, 1)).astype(jnp.float32))
    return (tile_image[None], score[None])


def solution(mesh):
    placed = (P("tile", "frame", None, None), P("tile", "frame", None), P(), P())
    return jax.shard_map(
        body,
        mesh=mesh,
        in_specs=placed,
        out_specs=(P("tile", "frame", None), P("tile", None)),
        check_vma=False,
    )
```

profile of v0, /device:TPU:96, one launch (start us, length us, event | category | flops | bytes accessed | tf_op | source)
XLA Modules:
  0.0 284.6 jit_solution(5914414440484258071)
XLA Ops:
  7.2 0.0 reduce-scatter.2.cloned.1.call-start
  7.2 1.3 fusion.9
  11.1 15.2 %fusion = f32[1024,5760]{1,0:T(8,128)} fusion(s32[]{:T(128)S(6)} %select_n.44, s32[]{:T(128)S(6)} %select_n.45, bf16[1024,5760]{1,0:T(8,128)(2,1)} %bitcast.19), kind=kLoop, calls=%fused_computation.1 | loop fusion | flops 5898240 | bytes 35389448 | tf_op jit(solution)/shard_map/while/body/eval_jaxpr/jit(_pad)/pad | solution.py:82
  26.3 0.0 copy-start
  26.3 0.0 copy-start.1
  26.3 0.0 reduce-scatter.2.cloned.1.call-update
  26.3 0.6 copy-done
  27.0 0.0 copy-done.1
  27.0 0.7 fusion.7
  30.4 140.7 %reduce-scatter.2.cloned.1.call-done = f32[32,5760]{1,0:T(8,128)} async-done(((f32[1024,5760]{1,0:T(8,128)}), f32[32,5760]{1,0:T(8,128)}) %reduce-scatter.2.cloned.1.call-update) | async-done | bytes 737296 | tf_op jit(solution)/shard_map/reduce_scatter | solution.py:91
  171.1 1.2 multiply_convert_fusion
  172.3 4.6 %collective-permute-start = (bf16[32,512]{1,0:T(8,128)(2,1)S(1)}, bf16[32,512]{1,0:T(8,128)(2,1)S(1)}, u32[]{:S(2)}, u32[]{:S(2)}) collective-permute-start(bf16[32,512]{1,0:T(8,128)(2,1)S(1)} %get-tuple-element.11), channel_id=1, source_target_pairs={{0,32},{32,64},{64,96},{96,128},{128,160},{160,192},{192,224},{1,3... | collective-permute-start | bytes 98312 | tf_op jit(solution)/shard_map/ppermute | solution.py:16
  180.4 1.9 collective-permute-start.1
  182.4 0.2 copy.9
  182.5 0.0 collective-permute-done
  182.5 0.1 fusion.2
  182.7 4.9 %collective-permute-done.1 = bf16[32,640]{1,0:T(8,128)(2,1)S(1)} collective-permute-done((bf16[32,640]{1,0:T(8,128)(2,1)S(1)}, bf16[32,640]{1,0:T(8,128)(2,1)S(1)}, u32[]{:S(2)}, u32[]{:S(2)}) %collective-permute-start.1) | collective-permute-done | bytes 40992 | tf_op jit(solution)/shard_map/ppermute | solution.py:16
  187.5 0.1 fusion.5
  187.6 0.2 copy.8
  187.9 25.4 %convolution_reduce_fusion = f32[128]{0:T(128)S(1)} fusion(bf16[1,32,640]{1,0,2:T(2,128)(2,1)S(1)} %copy.8, bf16[1,32,512]{1,0,2:T(2,128)(2,1)S(1)} %copy.9), kind=kOutput, calls=%fused_computation.2 | convolution fusion | flops 4194304 | bytes 74240 | tf_op jit(solution)/shard_map/slice | solution.py:35
  213.3 63.1 %psum.7 = f32[128]{0:T(128)S(1)} all-reduce(f32[128]{0:T(128)S(1)} %convolution_reduce_fusion), channel_id=1, replica_groups=mesh['tile'=8,'frame'=32] {'frame'}, use_global_device_ids=true, to_apply=%region_1.2 | all-reduce | flops 128 | bytes 1024 | tf_op jit(solution)/shard_map/psum | solution.py:105
  276.4 0.5 divide_bitcast_fusion
  276.9 0.1 fusion.4
  277.0 0.8 maximum_bitcast_fusion
  (9 shorter events, 0.1 us)
Async XLA Ops:
  7.2 163.9 %reduce-scatter.2.cloned.1.call-start = ((), (), s32[]{:S(2)}) async-start(), calls=%async_computation.1 | async-start | bytes 24330240 | tf_op jit(solution)/shard_map/reduce_scatter | solution.py:91
  26.3 0.7 copy-start
  26.3 0.7 copy-start.1
  172.3 10.3 %collective-permute-start = (bf16[32,512]{1,0:T(8,128)(2,1)S(1)}, bf16[32,512]{1,0:T(8,128)(2,1)S(1)}, u32[]{:S(2)}, u32[]{:S(2)}) collective-permute-start(bf16[32,512]{1,0:T(8,128)(2,1)S(1)} %get-tuple-element.11), channel_id=1, source_target_pairs={{0,32},{32,64},{64,96},{96,128},{128,160},{160,192},{192,224},{1,3... | collective-permute-start | bytes 98312 | tf_op jit(solution)/shard_map/ppermute | solution.py:16
  180.4 7.1 %collective-permute-start.1 = (bf16[32,640]{1,0:T(8,128)(2,1)S(1)}, bf16[32,640]{1,0:T(8,128)(2,1)S(1)}, u32[]{:S(2)}, u32[]{:S(2)}) collective-permute-start(bf16[32,640]{1,0:T(8,128)(2,1)S(1)} %slice.31), channel_id=1, source_target_pairs={{32,0},{64,32},{96,64},{128,96},{160,128},{192,160},{224,192},{33,... | collective-permute-start | bytes 122888 | tf_op jit(solution)/shard_map/ppermute | solution.py:16
Sparse Core Ops, SparseCore 0:
  26.5 144.5 reduce-scatter.1
where the time goes:
time: 285 us
  waiting for transfers between devices  146 us (51%)
  blocking collectives  63.1 us (22%)
  matrix products  25.4 us (9%)
  between operations  22.9 us (8%)
  other arithmetic  17.9 us (6%)
  starting transfers between devices  6.6 us (2%)
  local copies, waits for them, and re-layouts  3.11 us (1%)
    reduce_scatter x1, waiting for transfers between devices, body(): lax.psum_scatter(partial_image, 'frame', scatter_dimension=0, tiled=True)  141 us
    psum x1, blocking collectives, body(): products = lax.psum(products, 'frame')  63.1 us
    slice x1, matrix products, right_seam(): products = correlated[0, 0, :lag_count]  25.4 us
    pad x1, other arithmetic, add_frame(): jnp.pad(one_frame.astype(jnp.float32), ((SHIFT, SHIFT), (SHIFT, SHIFT)))  15.2 us
    ppermute x2, starting transfers between devices, from_behind(): return lax.ppermute(array, axis, pairs)  6.56 us
  transfers between devices with their start and end apart: 3, of which 2 were waited for; matrix products, arithmetic and copies ran while one was open for 0% of the time, Pallas kernels for 0%

commit v1 on v0

v1 whole, which is shorter than its diff:
```python
import functools
import math

import jax
import jax.numpy as jnp
from jax import lax
from jax.experimental import pallas as pl
from jax.experimental.pallas import tpu as pltpu
from jax.sharding import PartitionSpec as P

SHIFT = 4
STRIP = 512
LAGS = 128
LANES = 128
EDGE = STRIP + LAGS
SIDE = 4
BAND = 32
HALO = 16
WINDOW = 2 * BAND + 2 * HALO
PAD = 8
VMEM = 48 * 1024 * 1024


def device_at(y, x, core):
    return (y * SIDE + x) * 2 + core


def moved_by(array, y=0, x=0, core=0):
    pairs = [
        (device_at(i, j, k), device_at((i + y) % SIDE, (j + x) % SIDE, (k + core) % 2))
        for i in range(SIDE)
        for j in range(SIDE)
        for k in range(2)
    ]
    return lax.ppermute(array, "frame", pairs)


def from_behind(array, axis, by):
    count = lax.axis_size(axis)
    pairs = [(i, i + by) for i in range(count) if 0 <= i + by < count]
    return lax.ppermute(array, axis, pairs)


def window_start(step, rows):
    return jnp.clip(2 * BAND * step - HALO, 0, rows - WINDOW)


def shift_kernel(pieces, cols, rows, meta, *refs):
    count = len(pieces)
    sources, outs, scratch = refs[:count], refs[count : count + 2], refs[count + 2 :]
    step = pl.program_id(0)
    core, down, right = meta[2], meta[3], meta[4]
    inside = 2 * BAND * step - window_start(step, rows)
    over = jnp.where(right < 0, 1, 0)
    turn = jnp.where(right < 0, LANES + right, right)
    lane = lax.broadcasted_iota(jnp.int32, (BAND, LANES), 1)
    place = 0
    for (first, width), source, held in zip(pieces, sources, scratch):
        low = 0 if first > 0 else 1

        @pl.when(step == 0)
        def _():
            held[...] = jnp.zeros_like(held)

        for k in range(source.shape[1] // LANES):
            held[low + k, PAD : PAD + WINDOW, :] = source[
                :, k * LANES : (k + 1) * LANES
            ].astype(jnp.float32)
        for which, out in ((core, outs[0]), (1 - core, outs[1])):
            top = PAD + inside + BAND * which - down
            before = None
            for k in range(width // LANES + 1):
                now = pltpu.roll(held[k + over, pl.ds(top, BAND), :], turn, 1)
                if k > 0:
                    value = jnp.where(lane < turn, before, now)
                    begin = place + (k - 1) * LANES
                    out[0, 0, :, begin : begin + LANES] = value.astype(jnp.bfloat16)
                before = now
        place += width


def shifted(frame, meta, pieces, x_first):
    rows, cols = frame.shape
    total = sum(width for _, width in pieces)
    in_specs, scratch = [], []
    for first, width in pieces:
        begin = max(first - LANES, 0)
        end = min(first + width + LANES, cols)
        in_specs.append(
            pl.BlockSpec(
                (pl.Element(WINDOW), pl.Element(end - begin)),
                functools.partial(
                    lambda start, i, m: (pl.multiple_of(window_start(i, rows), HALO), start), begin
                ),
            )
        )
        scratch.append(pltpu.VMEM((width // LANES + 2, WINDOW + 2 * PAD, LANES), jnp.float32))

    def place(i, m):
        by_y = lax.rem(i // SIDE - m[0] + SIDE, SIDE)
        by_x = lax.rem(lax.rem(i, SIDE) - m[1] + SIDE, SIDE)
        return (by_x, by_y, 0, 0) if x_first else (by_y, by_x, 0, 0)

    out_spec = pl.BlockSpec((1, 1, BAND, total), place)
    out = jax.ShapeDtypeStruct((SIDE, SIDE, BAND, total), jnp.bfloat16)
    return pl.pallas_call(
        functools.partial(shift_kernel, pieces, cols, rows),
        grid_spec=pltpu.PrefetchScalarGridSpec(
            num_scalar_prefetch=1,
            grid=(SIDE * SIDE,),
            in_specs=in_specs,
            out_specs=[out_spec, out_spec],
            scratch_shapes=scratch,
        ),
        out_shape=[out, out],
        compiler_params=pltpu.CompilerParams(vmem_limit_bytes=VMEM),
        cost_estimate=pl.CostEstimate(
            flops=4 * rows * total, bytes_accessed=5 * rows * total, transcendentals=0
        ),
    )(meta, *[frame] * len(pieces))


def wide(array):
    return array.astype(jnp.float32)


def ahead(array, axis, by):
    return moved_by(array, x=by) if axis == "x" else moved_by(array, y=by)


def reduced(mine, theirs, axes):
    other = moved_by(theirs, core=1)

    def pair(j):
        return wide(mine[j]) + wide(other[j])

    first = [ahead(pair(j).astype(jnp.bfloat16), axes[0], j) for j in (1, 3, 2)]

    def row(j):
        return (wide(mine[0, j]) + wide(other[0, j])) + (
            (wide(first[0][j]) + wide(first[1][j])) + wide(first[2][j])
        )

    second = [ahead(row(j).astype(jnp.bfloat16), axes[1], j) for j in (1, 3, 2)]
    return row(0) + ((wide(second[0]) + wide(second[1])) + wide(second[2]))


def seam_kernel(meta, own_left, own_right, next_left, prev_right, left_out, right_out, score_out):
    width_now, shift_now, width_left, shift_left = meta[0], meta[1], meta[2], meta[3]
    rows = own_left.shape[0]
    mine = own_right[...].astype(jnp.float32)
    after = next_left[...].astype(jnp.float32)
    column = lax.broadcasted_iota(jnp.int32, (rows, STRIP), 1)
    inside = column >= STRIP - width_now
    aligned = pltpu.roll(after, lax.rem(STRIP - width_now - shift_now + EDGE, EDGE), 1)[:, :STRIP]
    feather = ((STRIP - column).astype(jnp.float32) - 0.5) / jnp.maximum(width_now, 1).astype(
        jnp.float32
    )
    right_out[...] = jnp.where(inside, feather * mine + (1.0 - feather) * aligned, mine).astype(
        right_out.dtype
    )
    own = own_left[...].astype(jnp.float32)
    before = jnp.concatenate(
        [prev_right[...].astype(jnp.float32), jnp.zeros((rows, LAGS), jnp.float32)], 1
    )
    before = pltpu.roll(before, lax.rem(shift_left + width_left - STRIP + EDGE, EDGE), 1)
    place = lax.broadcasted_iota(jnp.int32, (rows, EDGE), 1)
    within = (place >= shift_left) & (place < shift_left + width_left)
    weight = ((width_left - place + shift_left).astype(jnp.float32) - 0.5) / jnp.maximum(
        width_left, 1
    ).astype(jnp.float32)
    left_out[...] = jnp.where(within, weight * before + (1.0 - weight) * own, own).astype(
        left_out.dtype
    )
    masked = jnp.where(inside, mine, 0.0)
    masked = pltpu.roll(masked, lax.rem(width_now, STRIP), 1).astype(jnp.bfloat16)
    after = next_left[...]
    gram = jnp.zeros((LANES, 2 * LANES), jnp.float32)
    for t in range(STRIP // LANES):
        gram += lax.dot_general(
            masked[:, t * LANES : (t + 1) * LANES],
            after[:, t * LANES : (t + 2) * LANES],
            (((0,), (0,)), ((), ())),
            preferred_element_type=jnp.float32,
        )
    line = lax.broadcasted_iota(jnp.int32, gram.shape, 0)
    step = 1
    while step < LANES:
        gram = jnp.where((line & step) != 0, pltpu.roll(gram, 2 * LANES - step, 1), gram)
        step *= 2
    scale = lax.rsqrt(
        jnp.full((8, LANES), 1, jnp.int32).astype(jnp.float32)
        * (meta[4] * jnp.maximum(width_now, 1)).astype(jnp.float32)
    )
    total = jnp.sum(gram[:, :LANES], axis=0, keepdims=True)
    score_out[...] = jnp.broadcast_to(total, (8, LANES)) * scale


def seams(meta, own_left, own_right, next_left, prev_right):
    rows = own_left.shape[0]
    return pl.pallas_call(
        seam_kernel,
        in_specs=[pl.BlockSpec(memory_space=pltpu.SMEM)]
        + [pl.BlockSpec(memory_space=pltpu.VMEM)] * 4,
        out_specs=[pl.BlockSpec(memory_space=pltpu.VMEM)] * 3,
        out_shape=[
            jax.ShapeDtypeStruct((rows, EDGE), jnp.bfloat16),
            jax.ShapeDtypeStruct((rows, STRIP), jnp.bfloat16),
            jax.ShapeDtypeStruct((8, LANES), jnp.float32),
        ],
        cost_estimate=pl.CostEstimate(
            flops=2 * rows * STRIP * 2 * LANES, bytes_accessed=10 * rows * EDGE, transcendentals=0
        ),
    )(meta, own_left, own_right, next_left, prev_right)


FIRST_TILES = 14


def body(movie, frame_shift, intersection, seam_shift):
    frame = movie[0, 0]
    rows, cols = frame.shape
    frames = lax.axis_size("frame")
    position = lax.axis_index("frame")
    tile = lax.axis_index("tile")
    y, x, core = position // (2 * SIDE), (position // 2) % SIDE, position % 2
    meta = jnp.concatenate([jnp.stack([y, x, core]).astype(jnp.int32), frame_shift[0, 0]])

    cut = EDGE + FIRST_TILES * LANES
    strips = [(0, EDGE), (cols - STRIP, STRIP)]
    parts = [
        (strips, ("x", "y")),
        ([(cut, cols - STRIP - cut)], ("y", "x")),
        ([(EDGE, cut - EDGE)], ("x", "y")),
    ]
    scale = 1.0 / math.sqrt(frames)
    sums = []
    for pieces, axes in parts:
        mine, theirs = shifted(frame, meta, pieces, axes[0] == "x")
        sums.append((reduced(mine, theirs, axes) * scale).astype(jnp.bfloat16))
    strip, middle_b, middle_a = sums
    own_left, own_right = strip[:, :EDGE], strip[:, EDGE:]

    next_left = from_behind(own_left, "tile", -1)
    prev_right = from_behind(own_right, "tile", 1)
    earlier = jnp.maximum(tile - 1, 0)
    seam_meta = jnp.stack(
        [
            intersection[tile],
            seam_shift[tile],
            jnp.where(tile > 0, intersection[earlier], 0),
            jnp.where(tile > 0, seam_shift[earlier], 0),
            jnp.int32(rows),
        ]
    )
    left_part, right_part, products = seams(seam_meta, own_left, own_right, next_left, prev_right)
    spread_out = jnp.broadcast_to(products[None, :1], (frames, 1, LAGS))
    score = jnp.sum(lax.all_to_all(spread_out, "frame", 0, 0), axis=0)
    image = jnp.concatenate([left_part, middle_a, middle_b, right_part], 1)
    return (image[None], score)


def solution(mesh):
    placed = (P("tile", "frame", None, None), P("tile", "frame", None), P(), P())
    return jax.shard_map(
        body,
        mesh=mesh,
        in_specs=placed,
        out_specs=(P("tile", "frame", None), P("tile", None)),
        check_vma=False,
    )
```

time: 285 us -> 134 us (0.47)
  the two profiles are of different devices: /device:TPU:96 before, /device:TPU:102 now
where the time goes in v1:
time: 134 us; the launch traced here: 132 us
  Pallas kernels  35.5 us (26%)
  starting transfers between devices  33.6 us (25%)
  waiting for transfers between devices  28.7 us (21%)
  blocking collectives  17.3 us (13%)
  other arithmetic  11.8 us (9%)
  local copies, waits for them, and re-layouts  3.11 us (2%)
  between operations  2.16 us (2%)
    pallas_call x3, Pallas kernels, shifted(): pl.pallas_call(functools.partial(shift_kernel, pieces, cols, rows), grid_...  33.2 us
    ppermute x21, waiting for transfers between devices, moved_by(): return lax.ppermute(array, 'frame', pairs)  28.7 us
    ppermute x21, starting transfers between devices, moved_by(): return lax.ppermute(array, 'frame', pairs)  26.5 us
    all_to_all x1, blocking collectives, body(): score = jnp.sum(lax.all_to_all(spread_out, 'frame', 0, 0), axis=0)  17.3 us
    ppermute x2, starting transfers between devices, from_behind(): return lax.ppermute(array, axis, pairs)  7.05 us
    convert_element_type x3, other arithmetic, reduced(): second = [ahead(row(j).astype(jnp.bfloat16), axes[1], j) for j in (1, 3, 2)]  3.71 us
    convert_element_type x3, other arithmetic, reduced(): first = [ahead(pair(j).astype(jnp.bfloat16), axes[0], j) for j in (1, 3, 2)]  3.41 us
    convert_element_type x3, other arithmetic, body(): sums.append((reduced(mine, theirs, axes) * scale).astype(jnp.bfloat16))  2.69 us
  transfers between devices with their start and end apart: 23, of which 8 were waited for; matrix products, arithmetic and copies ran while one was open for 9% of the time, Pallas kernels for 19%

profile of v1, /device:TPU:102, one launch (start us, length us, event | category | flops | bytes accessed | tf_op | source)
XLA Modules:
  0.0 132.2 jit_solution(7834738932136287170)
XLA Ops:
  1.4 10.8 %shard_map.59 = (bf16[4,4,32,1152]{3,2,1,0:T(8,128)(2,1)S(1)}, bf16[4,4,32,1152]{3,2,1,0:T(8,128)(2,1)S(1)}) custom-call(s32[5]{0:T(128)S(1)} %pad_add_fusion.meta, bf16[1024,5760]{1,0:T(8,128)(2,1)} %bitcast.117, bf16[1024,5760]{1,0:T(8,128)(2,1)} %bitcast.118), custom_call_target="tpu_custom_call" | custom-call | flops 4718592 | bytes 5898240 | tf_op jit(solution)/shard_map/pallas_call | solution.py:106
  12.3 11.8 %shard_map.62 = (bf16[4,4,32,2816]{3,2,1,0:T(8,128)(2,1)S(1)}, bf16[4,4,32,2816]{3,2,1,0:T(8,128)(2,1)S(1)}) custom-call(s32[5]{0:T(128)S(1)} %pad_add_fusion.meta, bf16[1024,5760]{1,0:T(8,128)(2,1)} %bitcast.119), custom_call_target="tpu_custom_call" | custom-call | flops 11534336 | bytes 14417920 | tf_op jit(solution)/shard_map/pallas_call | solution.py:106
  24.7 10.6 %shard_map.61 = (bf16[4,4,32,1792]{3,2,1,0:T(8,128)(2,1)S(1)}, bf16[4,4,32,1792]{3,2,1,0:T(8,128)(2,1)S(1)}) custom-call(s32[5]{0:T(128)S(1)} %pad_add_fusion.meta, bf16[1024,5760]{1,0:T(8,128)(2,1)} %bitcast.120), custom_call_target="tpu_custom_call" | custom-call | flops 7340032 | bytes 9175040 | tf_op jit(solution)/shard_map/pallas_call | solution.py:106
  37.2 3.2 %collective-permute-start.1 = (bf16[4,32,1152]{2,1,0:T(8,128)(2,1)S(1)}, bf16[4,32,1152]{2,1,0:T(8,128)(2,1)S(1)}, u32[]{:S(2)}, u32[]{:S(2)}) collective-permute-start(bf16[4,32,1152]{2,1,0:T(8,128)(2,1)S(1)} %get-tuple-element.35), channel_id=1, source_target_pairs={{0,2},{1,3},{2,4},{3,5},{4,6},{5,7},{6,0},{7,1},{8,10},{9,11},{10,... | collective-permute-start | bytes 884744 | tf_op jit(solution)/shard_map/ppermute | solution.py:35
  40.4 6.7 %collective-permute-done.3 = bf16[4,32,1152]{2,1,0:T(8,128)(2,1)S(1)} collective-permute-done((bf16[4,32,1152]{2,1,0:T(8,128)(2,1)S(1)}, bf16[4,32,1152]{2,1,0:T(8,128)(2,1)S(1)}, u32[]{:S(2)}, u32[]{:S(2)}) %collective-permute-start.3) | collective-permute-done | bytes 294944 | tf_op jit(solution)/shard_map/ppermute | solution.py:35
  47.1 5.9 %collective-permute-done.2 = bf16[4,32,1152]{2,1,0:T(8,128)(2,1)S(1)} collective-permute-done((bf16[4,32,1152]{2,1,0:T(8,128)(2,1)S(1)}, bf16[4,32,1152]{2,1,0:T(8,128)(2,1)S(1)}, u32[]{:S(2)}, u32[]{:S(2)}) %collective-permute-start.2) | collective-permute-done | bytes 294944 | tf_op jit(solution)/shard_map/ppermute | solution.py:35
  53.1 3.3 %collective-permute-start.6 = (bf16[32,1152]{1,0:T(8,128)(2,1)S(1)}, bf16[32,1152]{1,0:T(8,128)(2,1)S(1)}, u32[]{:S(2)}, u32[]{:S(2)}) collective-permute-start(bf16[32,1152]{1,0:T(8,128)(2,1)S(1)} %get-tuple-element.33), channel_id=1, source_target_pairs={{0,16},{1,17},{2,18},{3,19},{4,20},{5,21},{6,22},{7,23},{8,24},{9,... | collective-permute-start | bytes 221192 | tf_op jit(solution)/shard_map/ppermute | solution.py:35
  59.1 1.9 %collective-permute-done.5 = bf16[32,1152]{1,0:T(8,128)(2,1)S(1)} collective-permute-done((bf16[32,1152]{1,0:T(8,128)(2,1)S(1)}, bf16[32,1152]{1,0:T(8,128)(2,1)S(1)}, u32[]{:S(2)}, u32[]{:S(2)}) %collective-permute-start.5) | collective-permute-done | bytes 73760 | tf_op jit(solution)/shard_map/ppermute | solution.py:35
  61.0 2.0 %collective-permute-done.4 = bf16[32,1152]{1,0:T(8,128)(2,1)S(1)} collective-permute-done((bf16[32,1152]{1,0:T(8,128)(2,1)S(1)}, bf16[32,1152]{1,0:T(8,128)(2,1)S(1)}, u32[]{:S(2)}, u32[]{:S(2)}) %collective-permute-start.4) | collective-permute-done | bytes 73760 | tf_op jit(solution)/shard_map/ppermute | solution.py:35
  63.2 2.0 %collective-permute-start.7 = (bf16[32,640]{1,0:T(8,128)(2,1)S(1)}, bf16[32,640]{1,0:T(8,128)(2,1)S(1)}, u32[]{:S(2)}, u32[]{:S(2)}) collective-permute-start(bf16[32,640]{1,0:T(8,128)(2,1)S(1)} %slice.343.own_left), channel_id=1, source_target_pairs={{32,0},{64,32},{96,64},{128,96},{160,128},{192,160},{224,192},{33,... | collective-permute-start | bytes 122888 | tf_op jit(solution)/shard_map/ppermute | solution.py:41
  65.2 5.0 %collective-permute-start.8 = (bf16[32,512]{1,0:T(8,128)(2,1)S(1)}, bf16[32,512]{1,0:T(8,128)(2,1)S(1)}, u32[]{:S(2)}, u32[]{:S(2)}) collective-permute-start(bf16[32,512]{1,0:T(8,128)(2,1)S(1)} %slice.344.own_right), channel_id=1, source_target_pairs={{0,32},{32,64},{64,96},{96,128},{128,160},{160,192},{192,224},{1,3... | collective-permute-start | bytes 98312 | tf_op jit(solution)/shard_map/ppermute | solution.py:41
  73.4 3.2 %collective-permute-start.10 = (bf16[4,32,1792]{2,1,0:T(8,128)(2,1)}, bf16[4,32,1792]{2,1,0:T(8,128)(2,1)}, u32[]{:S(2)}, u32[]{:S(2)}) collective-permute-start(bf16[4,32,1792]{2,1,0:T(8,128)(2,1)} %get-tuple-element.29), channel_id=1, source_target_pairs={{0,2},{1,3},{2,4},{3,5},{4,6},{5,7},{6,0},{7,1},{8,10},{9,11},{10,... | collective-permute-start | bytes 1376264 | tf_op jit(solution)/shard_map/ppermute | solution.py:35
  76.7 1.6 %fusion = (bf16[4,32,2816]{2,1,0:T(8,128)(2,1)}, bf16[4,32,2816]{2,1,0:T(8,128)(2,1)}, bf16[4,32,2816]{2,1,0:T(8,128)(2,1)}) fusion(bf16[4,4,32,2816]{3,2,1,0:T(8,128)(2,1)S(1)} %collective-permute-done.16, bf16[4,4,32,2816]{3,2,1,0:T(8,128)(2,1)S(1)} %get-tuple-element.16), kind=kLoop, calls=%fused_computation.6 | loop fusion | flops 4325376 | bytes 6488064 | tf_op jit(solution)/shard_map/convert_element_type | solution.py:137
  79.0 1.8 %collective-permute-start.18 = (bf16[4,32,2816]{2,1,0:T(8,128)(2,1)}, bf16[4,32,2816]{2,1,0:T(8,128)(2,1)}, u32[]{:S(2)}, u32[]{:S(2)}) collective-permute-start(bf16[4,32,2816]{2,1,0:T(8,128)(2,1)} %get-tuple-element.25), channel_id=1, source_target_pairs={{0,24},{1,25},{2,26},{3,27},{4,28},{5,29},{6,30},{7,31},{8,0},{9,1... | collective-permute-start | bytes 2162696 | tf_op jit(solution)/shard_map/ppermute | solution.py:35
  80.8 6.1 %collective-permute-done.12 = bf16[4,32,1792]{2,1,0:T(8,128)(2,1)S(1)} collective-permute-done((bf16[4,32,1792]{2,1,0:T(8,128)(2,1)S(1)}, bf16[4,32,1792]{2,1,0:T(8,128)(2,1)S(1)}, u32[]{:S(2)}, u32[]{:S(2)}) %collective-permute-start.12) | collective-permute-done | bytes 458784 | tf_op jit(solution)/shard_map/ppermute | solution.py:35
  88.9 1.7 %stack.20.meta = s32[5]{0:T(128)} concatenate(s32[1]{0:T(128)} %get-tuple-element.42, s32[1]{0:T(128)} %get-tuple-element.39, s32[1]{0:T(128)} %bitcast.1, s32[1]{0:T(128)} %bitcast.3, s32[1]{0:T(128)} %constant.57.clone.1), dimensions={0} | concatenate | bytes 40 | tf_op jit(solution)/shard_map/stack | solution.py:247
  90.6 2.3 %shard_map.60 = (bf16[32,640]{1,0:T(8,128)(2,1)}, bf16[32,512]{1,0:T(8,128)(2,1)}, f32[8,128]{1,0:T(8,128)}) custom-call(s32[5]{0:T(128)} %stack.20.meta, bf16[32,640]{1,0:T(8,128)(2,1)} %copy-done.3, bf16[32,512]{1,0:T(8,128)(2,1)} %copy-done.4, bf16[32,640]{1,0:T(8,128)(2,1)} %copy-done.6, bf16[32,512]{1,0:T(8,128)(2,1)} %copy-done.8), custom_call_target="tpu_custom_call" | custom-call | flops 8388608 | bytes 204800 | tf_op jit(solution)/shard_map/pallas_call | solution.py:201
  93.6 17.3 %all_to_all.5 = f32[32,1,128]{2,1,0:T(1,128)S(1)} all-to-all(f32[32,1,128]{2,1,0:T(1,128)S(1)} %broadcast_in_dim.13), channel_id=1, replica_groups=mesh['tile'=8,'frame'=32] {'frame'}, dimensions={0} | all-to-all | bytes 32768 | tf_op jit(solution)/shard_map/all_to_all | solution.py:258
  111.4 1.6 %fusion.17 = (bf16[32,1792]{1,0:T(8,128)(2,1)S(1)}, bf16[32,1792]{1,0:T(8,128)(2,1)S(1)}, bf16[32,1792]{1,0:T(8,128)(2,1)S(1)}) fusion(bf16[4,32,1792]{2,1,0:T(8,128)(2,1)S(1)} %collective-permute-done.12, bf16[4,32,1792]{2,1,0:T(8,128)(2,1)} %collective-permute-done.11, bf16[4,32,1792]{2,1,0:T(8,128)(2,1)} %collective-permute-done.10, ...), kind=kLoop, calls=%fused_computation.34 | loop fusion | flops 1720320 | bytes 2064384 | tf_op jit(solution)/shard_map/convert_element_type | solution.py:144
  113.0 1.8 %collective-permute-start.15 = (bf16[32,1792]{1,0:T(8,128)(2,1)S(1)}, bf16[32,1792]{1,0:T(8,128)(2,1)S(1)}, u32[]{:S(2)}, u32[]{:S(2)}) collective-permute-start(bf16[32,1792]{1,0:T(8,128)(2,1)S(1)} %get-tuple-element.27), channel_id=1, source_target_pairs={{0,16},{1,17},{2,18},{3,19},{4,20},{5,21},{6,22},{7,23},{8,24},{9,... | collective-permute-start | bytes 344072 | tf_op jit(solution)/shard_map/ppermute | solution.py:35
  116.9 2.0 %fusion.8 = (bf16[32,2816]{1,0:T(8,128)(2,1)S(1)}, bf16[32,2816]{1,0:T(8,128)(2,1)S(1)}, bf16[32,2816]{1,0:T(8,128)(2,1)S(1)}) fusion(bf16[4,32,2816]{2,1,0:T(8,128)(2,1)} %collective-permute-done.19, bf16[4,32,2816]{2,1,0:T(8,128)(2,1)} %collective-permute-done.18, bf16[4,32,2816]{2,1,0:T(8,128)(2,1)} %collective-permute-done.17, ...), kind=kLoop, calls=%fused_computation.21 | loop fusion | flops 2703360 | bytes 3244032 | tf_op jit(solution)/shard_map/convert_element_type | solution.py:144
  120.8 2.7 %collective-permute-start.20 = (bf16[32,2816]{1,0:T(8,128)(2,1)S(1)}, bf16[32,2816]{1,0:T(8,128)(2,1)S(1)}, u32[]{:S(2)}, u32[]{:S(2)}) collective-permute-start(bf16[32,2816]{1,0:T(8,128)(2,1)S(1)} %get-tuple-element.20), channel_id=1, source_target_pairs={{0,2},{1,3},{2,4},{3,5},{4,6},{5,7},{6,0},{7,1},{8,10},{9,11},{10,... | collective-permute-start | bytes 540680 | tf_op jit(solution)/shard_map/ppermute | solution.py:35
  124.7 3.3 %collective-permute-done.22 = bf16[32,2816]{1,0:T(8,128)(2,1)S(1)} collective-permute-done((bf16[32,2816]{1,0:T(8,128)(2,1)S(1)}, bf16[32,2816]{1,0:T(8,128)(2,1)S(1)}, u32[]{:S(2)}, u32[]{:S(2)}) %collective-permute-start.22) | collective-permute-done | bytes 180256 | tf_op jit(solution)/shard_map/ppermute | solution.py:35
  128.0 2.1 %collective-permute-done.21 = bf16[32,2816]{1,0:T(8,128)(2,1)S(1)} collective-permute-done((bf16[32,2816]{1,0:T(8,128)(2,1)S(1)}, bf16[32,2816]{1,0:T(8,128)(2,1)S(1)}, u32[]{:S(2)}, u32[]{:S(2)}) %collective-permute-start.21) | collective-permute-done | bytes 180256 | tf_op jit(solution)/shard_map/ppermute | solution.py:35
  (67 shorter events, 19.2 us)
Async XLA Ops:
  12.2 23.2 %collective-permute-start = (bf16[4,4,32,1152]{3,2,1,0:T(8,128)(2,1)S(1)}, bf16[4,4,32,1152]{3,2,1,0:T(8,128)(2,1)S(1)}, u32[]{:S(2)}, u32[]{:S(2)}) collective-permute-start(bf16[4,4,32,1152]{3,2,1,0:T(8,128)(2,1)S(1)} %get-tuple-element.12), channel_id=1, source_target_pairs={{0,1},{1,0},{2,3},{3,2},{4,5},{5,4},{6,7},{7,6},{8,9},{9,8},{10,11... | collective-permute-start | bytes 3538952 | tf_op jit(solution)/shard_map/ppermute | solution.py:35
  24.1 49.3 %collective-permute-start.16 = (bf16[4,4,32,2816]{3,2,1,0:T(8,128)(2,1)S(1)}, bf16[4,4,32,2816]{3,2,1,0:T(8,128)(2,1)S(1)}, u32[]{:S(2)}, u32[]{:S(2)}) collective-permute-start(bf16[4,4,32,2816]{3,2,1,0:T(8,128)(2,1)S(1)} %get-tuple-element.17), channel_id=1, source_target_pairs={{0,1},{1,0},{2,3},{3,2},{4,5},{5,4},{6,7},{7,6},{8,9},{9,8},{10,11... | collective-permute-start | bytes 8650760 | tf_op jit(solution)/shard_map/ppermute | solution.py:35
  35.3 35.0 %copy-start = (bf16[4,4,32,1792]{3,2,1,0:T(8,128)(2,1)}, bf16[4,4,32,1792]{3,2,1,0:T(8,128)(2,1)S(1)}, u32[]{:S(2)}) copy-start(bf16[4,4,32,1792]{3,2,1,0:T(8,128)(2,1)S(1)} %get-tuple-element.14) | copy-start | bytes 5505028
  35.3 34.9 %collective-permute-start.9 = (bf16[4,4,32,1792]{3,2,1,0:T(8,128)(2,1)S(1)}, bf16[4,4,32,1792]{3,2,1,0:T(8,128)(2,1)S(1)}, u32[]{:S(2)}, u32[]{:S(2)}) collective-permute-start(bf16[4,4,32,1792]{3,2,1,0:T(8,128)(2,1)S(1)} %get-tuple-element.15), channel_id=1, source_target_pairs={{0,1},{1,0},{2,3},{3,2},{4,5},{5,4},{6,7},{7,6},{8,9},{9,8},{10,11... | collective-permute-start | bytes 5505032 | tf_op jit(solution)/shard_map/ppermute | solution.py:35
  35.7 11.4 %collective-permute-start.3 = (bf16[4,32,1152]{2,1,0:T(8,128)(2,1)S(1)}, bf16[4,32,1152]{2,1,0:T(8,128)(2,1)S(1)}, u32[]{:S(2)}, u32[]{:S(2)}) collective-permute-start(bf16[4,32,1152]{2,1,0:T(8,128)(2,1)S(1)} %get-tuple-element.36), channel_id=1, source_target_pairs={{0,4},{1,5},{2,6},{3,7},{4,0},{5,1},{6,2},{7,3},{8,12},{9,13},{10,... | collective-permute-start | bytes 884744 | tf_op jit(solution)/shard_map/ppermute | solution.py:35
  37.2 15.8 %collective-permute-start.2 = (bf16[4,32,1152]{2,1,0:T(8,128)(2,1)S(1)}, bf16[4,32,1152]{2,1,0:T(8,128)(2,1)S(1)}, u32[]{:S(2)}, u32[]{:S(2)}) collective-permute-start(bf16[4,32,1152]{2,1,0:T(8,128)(2,1)S(1)} %get-tuple-element.37), channel_id=1, source_target_pairs={{0,6},{1,7},{2,0},{3,1},{4,2},{5,3},{6,4},{7,5},{8,14},{9,15},{10,... | collective-permute-start | bytes 884744 | tf_op jit(solution)/shard_map/ppermute | solution.py:35
  37.2 15.8 %collective-permute-start.1 = (bf16[4,32,1152]{2,1,0:T(8,128)(2,1)S(1)}, bf16[4,32,1152]{2,1,0:T(8,128)(2,1)S(1)}, u32[]{:S(2)}, u32[]{:S(2)}) collective-permute-start(bf16[4,32,1152]{2,1,0:T(8,128)(2,1)S(1)} %get-tuple-element.35), channel_id=1, source_target_pairs={{0,2},{1,3},{2,4},{3,5},{4,6},{5,7},{6,0},{7,1},{8,10},{9,11},{10,... | collective-permute-start | bytes 884744 | tf_op jit(solution)/shard_map/ppermute | solution.py:35
  53.1 5.9 %collective-permute-start.6 = (bf16[32,1152]{1,0:T(8,128)(2,1)S(1)}, bf16[32,1152]{1,0:T(8,128)(2,1)S(1)}, u32[]{:S(2)}, u32[]{:S(2)}) collective-permute-start(bf16[32,1152]{1,0:T(8,128)(2,1)S(1)} %get-tuple-element.33), channel_id=1, source_target_pairs={{0,16},{1,17},{2,18},{3,19},{4,20},{5,21},{6,22},{7,23},{8,24},{9,... | collective-permute-start | bytes 221192 | tf_op jit(solution)/shard_map/ppermute | solution.py:35
  56.4 4.6 %collective-permute-start.5 = (bf16[32,1152]{1,0:T(8,128)(2,1)S(1)}, bf16[32,1152]{1,0:T(8,128)(2,1)S(1)}, u32[]{:S(2)}, u32[]{:S(2)}) collective-permute-start(bf16[32,1152]{1,0:T(8,128)(2,1)S(1)} %get-tuple-element.34), channel_id=1, source_target_pairs={{0,24},{1,25},{2,26},{3,27},{4,28},{5,29},{6,30},{7,31},{8,0},{9,1... | collective-permute-start | bytes 221192 | tf_op jit(solution)/shard_map/ppermute | solution.py:35
  57.5 5.6 %collective-permute-start.4 = (bf16[32,1152]{1,0:T(8,128)(2,1)S(1)}, bf16[32,1152]{1,0:T(8,128)(2,1)S(1)}, u32[]{:S(2)}, u32[]{:S(2)}) collective-permute-start(bf16[32,1152]{1,0:T(8,128)(2,1)S(1)} %get-tuple-element.32), channel_id=1, source_target_pairs={{0,8},{1,9},{2,10},{3,11},{4,12},{5,13},{6,14},{7,15},{8,16},{9,17... | collective-permute-start | bytes 221192 | tf_op jit(solution)/shard_map/ppermute | solution.py:35
  63.2 15.8 %collective-permute-start.7 = (bf16[32,640]{1,0:T(8,128)(2,1)S(1)}, bf16[32,640]{1,0:T(8,128)(2,1)S(1)}, u32[]{:S(2)}, u32[]{:S(2)}) collective-permute-start(bf16[32,640]{1,0:T(8,128)(2,1)S(1)} %slice.343.own_left), channel_id=1, source_target_pairs={{32,0},{64,32},{96,64},{128,96},{160,128},{192,160},{224,192},{33,... | collective-permute-start | bytes 122888 | tf_op jit(solution)/shard_map/ppermute | solution.py:41
  65.2 13.1 %collective-permute-start.8 = (bf16[32,512]{1,0:T(8,128)(2,1)S(1)}, bf16[32,512]{1,0:T(8,128)(2,1)S(1)}, u32[]{:S(2)}, u32[]{:S(2)}) collective-permute-start(bf16[32,512]{1,0:T(8,128)(2,1)S(1)} %slice.344.own_right), channel_id=1, source_target_pairs={{0,32},{32,64},{64,96},{96,128},{128,160},{160,192},{192,224},{1,3... | collective-permute-start | bytes 98312 | tf_op jit(solution)/shard_map/ppermute | solution.py:41
  71.9 15.0 %collective-permute-start.12 = (bf16[4,32,1792]{2,1,0:T(8,128)(2,1)S(1)}, bf16[4,32,1792]{2,1,0:T(8,128)(2,1)S(1)}, u32[]{:S(2)}, u32[]{:S(2)}) collective-permute-start(bf16[4,32,1792]{2,1,0:T(8,128)(2,1)S(1)} %get-tuple-element.30), channel_id=1, source_target_pairs={{0,4},{1,5},{2,6},{3,7},{4,0},{5,1},{6,2},{7,3},{8,12},{9,13},{10,... | collective-permute-start | bytes 1376264 | tf_op jit(solution)/shard_map/ppermute | solution.py:35
  73.4 38.0 %collective-permute-start.11 = (bf16[4,32,1792]{2,1,0:T(8,128)(2,1)}, bf16[4,32,1792]{2,1,0:T(8,128)(2,1)}, u32[]{:S(2)}, u32[]{:S(2)}) collective-permute-start(bf16[4,32,1792]{2,1,0:T(8,128)(2,1)} %get-tuple-element.31), channel_id=1, source_target_pairs={{0,6},{1,7},{2,0},{3,1},{4,2},{5,3},{6,4},{7,5},{8,14},{9,15},{10,... | collective-permute-start | bytes 1376264 | tf_op jit(solution)/shard_map/ppermute | solution.py:35
  73.4 38.0 %collective-permute-start.10 = (bf16[4,32,1792]{2,1,0:T(8,128)(2,1)}, bf16[4,32,1792]{2,1,0:T(8,128)(2,1)}, u32[]{:S(2)}, u32[]{:S(2)}) collective-permute-start(bf16[4,32,1792]{2,1,0:T(8,128)(2,1)} %get-tuple-element.29), channel_id=1, source_target_pairs={{0,2},{1,3},{2,4},{3,5},{4,6},{5,7},{6,0},{7,1},{8,10},{9,11},{10,... | collective-permute-start | bytes 1376264 | tf_op jit(solution)/shard_map/ppermute | solution.py:35
  78.3 37.9 %collective-permute-start.19 = (bf16[4,32,2816]{2,1,0:T(8,128)(2,1)}, bf16[4,32,2816]{2,1,0:T(8,128)(2,1)}, u32[]{:S(2)}, u32[]{:S(2)}) collective-permute-start(bf16[4,32,2816]{2,1,0:T(8,128)(2,1)} %get-tuple-element.24), channel_id=1, source_target_pairs={{0,16},{1,17},{2,18},{3,19},{4,20},{5,21},{6,22},{7,23},{8,24},{9,... | collective-permute-start | bytes 2162696 | tf_op jit(solution)/shard_map/ppermute | solution.py:35
  79.0 37.9 %collective-permute-start.18 = (bf16[4,32,2816]{2,1,0:T(8,128)(2,1)}, bf16[4,32,2816]{2,1,0:T(8,128)(2,1)}, u32[]{:S(2)}, u32[]{:S(2)}) collective-permute-start(bf16[4,32,2816]{2,1,0:T(8,128)(2,1)} %get-tuple-element.25), channel_id=1, source_target_pairs={{0,24},{1,25},{2,26},{3,27},{4,28},{5,29},{6,30},{7,31},{8,0},{9,1... | collective-permute-start | bytes 2162696 | tf_op jit(solution)/shard_map/ppermute | solution.py:35
  86.9 30.0 %collective-permute-start.17 = (bf16[4,32,2816]{2,1,0:T(8,128)(2,1)}, bf16[4,32,2816]{2,1,0:T(8,128)(2,1)}, u32[]{:S(2)}, u32[]{:S(2)}) collective-permute-start(bf16[4,32,2816]{2,1,0:T(8,128)(2,1)} %get-tuple-element.23), channel_id=1, source_target_pairs={{0,8},{1,9},{2,10},{3,11},{4,12},{5,13},{6,14},{7,15},{8,16},{9,17... | collective-permute-start | bytes 2162696 | tf_op jit(solution)/shard_map/ppermute | solution.py:35
  113.0 7.7 %collective-permute-start.15 = (bf16[32,1792]{1,0:T(8,128)(2,1)S(1)}, bf16[32,1792]{1,0:T(8,128)(2,1)S(1)}, u32[]{:S(2)}, u32[]{:S(2)}) collective-permute-start(bf16[32,1792]{1,0:T(8,128)(2,1)S(1)} %get-tuple-element.27), channel_id=1, source_target_pairs={{0,16},{1,17},{2,18},{3,19},{4,20},{5,21},{6,22},{7,23},{8,24},{9,... | collective-permute-start | bytes 344072 | tf_op jit(solution)/shard_map/ppermute | solution.py:35
  114.9 8.6 %collective-permute-start.14 = (bf16[32,1792]{1,0:T(8,128)(2,1)S(1)}, bf16[32,1792]{1,0:T(8,128)(2,1)S(1)}, u32[]{:S(2)}, u32[]{:S(2)}) collective-permute-start(bf16[32,1792]{1,0:T(8,128)(2,1)S(1)} %get-tuple-element.28), channel_id=1, source_target_pairs={{0,24},{1,25},{2,26},{3,27},{4,28},{5,29},{6,30},{7,31},{8,0},{9,1... | collective-permute-start | bytes 344072 | tf_op jit(solution)/shard_map/ppermute | solution.py:35
  116.2 7.3 %collective-permute-start.13 = (bf16[32,1792]{1,0:T(8,128)(2,1)S(1)}, bf16[32,1792]{1,0:T(8,128)(2,1)S(1)}, u32[]{:S(2)}, u32[]{:S(2)}) collective-permute-start(bf16[32,1792]{1,0:T(8,128)(2,1)S(1)} %get-tuple-element.26), channel_id=1, source_target_pairs={{0,8},{1,9},{2,10},{3,11},{4,12},{5,13},{6,14},{7,15},{8,16},{9,17... | collective-permute-start | bytes 344072 | tf_op jit(solution)/shard_map/ppermute | solution.py:35
  118.9 9.1 %collective-permute-start.22 = (bf16[32,2816]{1,0:T(8,128)(2,1)S(1)}, bf16[32,2816]{1,0:T(8,128)(2,1)S(1)}, u32[]{:S(2)}, u32[]{:S(2)}) collective-permute-start(bf16[32,2816]{1,0:T(8,128)(2,1)S(1)} %get-tuple-element.21), channel_id=1, source_target_pairs={{0,4},{1,5},{2,6},{3,7},{4,0},{5,1},{6,2},{7,3},{8,12},{9,13},{10,... | collective-permute-start | bytes 540680 | tf_op jit(solution)/shard_map/ppermute | solution.py:35
  120.2 9.8 %collective-permute-start.21 = (bf16[32,2816]{1,0:T(8,128)(2,1)S(1)}, bf16[32,2816]{1,0:T(8,128)(2,1)S(1)}, u32[]{:S(2)}, u32[]{:S(2)}) collective-permute-start(bf16[32,2816]{1,0:T(8,128)(2,1)S(1)} %get-tuple-element.22), channel_id=1, source_target_pairs={{0,6},{1,7},{2,0},{3,1},{4,2},{5,3},{6,4},{7,5},{8,14},{9,15},{10,... | collective-permute-start | bytes 540680 | tf_op jit(solution)/shard_map/ppermute | solution.py:35
  120.8 9.3 %collective-permute-start.20 = (bf16[32,2816]{1,0:T(8,128)(2,1)S(1)}, bf16[32,2816]{1,0:T(8,128)(2,1)S(1)}, u32[]{:S(2)}, u32[]{:S(2)}) collective-permute-start(bf16[32,2816]{1,0:T(8,128)(2,1)S(1)} %get-tuple-element.20), channel_id=1, source_target_pairs={{0,2},{1,3},{2,4},{3,5},{4,6},{5,7},{6,0},{7,1},{8,10},{9,11},{10,... | collective-permute-start | bytes 540680 | tf_op jit(solution)/shard_map/ppermute | solution.py:35
  (10 other events, 93.3 us)

commit v2 on v0

v2 whole, which is shorter than its diff:
```python
import functools
import math

import jax
import jax.numpy as jnp
from jax import lax
from jax.experimental import pallas as pl
from jax.experimental.pallas import tpu as pltpu
from jax.sharding import PartitionSpec as P

STRIP = 512
LAGS = 128
LANES = 128
EDGE = STRIP + LAGS
SIDE = 4
BAND = 32
HALO = 16
PAD = 8
VMEM = 16 * 1024 * 1024
GATE = 1024 * 1024
LOADING = 36 * 1024 * 1024


def device_at(y, x, core):
    return (y * SIDE + x) * 2 + core


def permuted(array, target):
    places = [(y, x, core) for y in range(SIDE) for x in range(SIDE) for core in range(2)]
    return lax.ppermute(
        array, "frame", [(device_at(*place), device_at(*target(*place))) for place in places]
    )


def to_other_core(array):
    return permuted(array, lambda y, x, core: (y, x, 1 - core))


def ahead(array, stage, by):
    def target(y, x, core):
        if (core == 0) == (stage == 1):
            return (y, (x + by) % SIDE, core)
        return ((y + by) % SIDE, x, core)

    return permuted(array, target)


def from_behind(array, axis, by):
    count = lax.axis_size(axis)
    pairs = [(i, i + by) for i in range(count) if 0 <= i + by < count]
    return lax.ppermute(array, axis, pairs)


def wide(array):
    return array.astype(jnp.float32)


def call(kernel, out_shape, operands, scalars=(), after=(), scratch=()):
    vmem = pl.BlockSpec(memory_space=pltpu.VMEM)
    anywhere = pl.BlockSpec(memory_space=pl.ANY)
    first, last = len(scalars) + len(operands), len(scalars) + len(operands) + len(after)

    def run(*refs):
        kernel(*refs[:first], *refs[last:])

    return pl.pallas_call(
        run,
        in_specs=[pl.BlockSpec(memory_space=pltpu.SMEM)] * len(scalars)
        + [vmem] * len(operands)
        + [anywhere] * len(after),
        out_specs=[vmem] * len(out_shape),
        out_shape=[jax.ShapeDtypeStruct(shape, dtype) for shape, dtype in out_shape],
        scratch_shapes=list(scratch),
        compiler_params=pltpu.CompilerParams(vmem_limit_bytes=VMEM),
        cost_estimate=pl.CostEstimate(flops=1024, bytes_accessed=1024, transcendentals=0),
    )(*scalars, *operands, *after)


def gated(arrays, after):
    anywhere = pl.BlockSpec(memory_space=pl.ANY)
    return pl.pallas_call(
        lambda *refs: None,
        in_specs=[anywhere] * (len(arrays) + len(after)),
        out_specs=[anywhere] * len(arrays),
        out_shape=[jax.ShapeDtypeStruct(array.shape, array.dtype) for array in arrays],
        input_output_aliases={i: i for i in range(len(arrays))},
        compiler_params=pltpu.CompilerParams(vmem_limit_bytes=GATE),
        cost_estimate=pl.CostEstimate(flops=1024, bytes_accessed=1024, transcendentals=0),
    )(*arrays, *after)


class Mover:
    def __init__(self, moves, pieces, rows, cols, held, theirs):
        position = lax.axis_index("frame")
        self.y, self.x = position // (2 * SIDE), (position // 2) % SIDE
        core = position % 2
        self.core = 1 - core if theirs else core
        self.down, right = moves[0], moves[1]
        self.over = jnp.where(right < 0, 1, 0)
        self.turn = jnp.where(right < 0, LANES + right, right)
        self.rows, self.held, self.pieces = rows, held, []
        base = 0
        for source, origin, first, width in pieces:
            begin, end = max(first - LANES, 0), min(first + width + LANES, cols)
            blank = jnp.zeros(held.shape[2:], held.dtype)
            for slot in range(2):
                if begin == first:
                    held[slot, base] = blank
                if end == first + width:
                    held[slot, base + width // LANES + 1] = blank
            low = base + (1 if begin == first else 0)
            self.pieces.append((source, begin - origin, (end - begin) // LANES, base, low, width))
            base += width // LANES + 2

    def band(self, slot, j, d, write):
        by_x = jnp.where(self.core == 0, j, d)
        by_y = jnp.where(self.core == 0, d, j)
        chip = lax.rem(self.y + by_y, SIDE) * SIDE + lax.rem(self.x + by_x, SIDE)
        top = pl.multiple_of((chip * 2 + self.core) * BAND, BAND)
        above = pl.multiple_of(jnp.maximum(top - HALO, 0), HALO)
        below = pl.multiple_of(jnp.minimum(top + BAND, self.rows - HALO), HALO)
        has_above = jnp.where(top > 0, 1.0, 0.0).astype(jnp.float32)
        has_below = jnp.where(top + BAND < self.rows, 1.0, 0.0).astype(jnp.float32)
        lane = lax.broadcasted_iota(jnp.int32, (BAND, LANES), 1)
        held, out = self.held, 0
        for source, begin, tiles, base, low, width in self.pieces:
            for k in range(tiles):
                at = pl.ds(begin + k * LANES, LANES)
                held[slot, low + k, :PAD] = wide(source[pl.ds(above, HALO), at])[PAD:] * has_above
                held[slot, low + k, PAD : PAD + BAND] = wide(source[pl.ds(top, BAND), at])
                held[slot, low + k, PAD + BAND :] = (
                    wide(source[pl.ds(below, HALO), at])[:PAD] * has_below
                )
            before = None
            for k in range(width // LANES + 1):
                value = held[slot, base + k + self.over, pl.ds(PAD - self.down, BAND), :]
                now = pltpu.roll(value, self.turn, 1)
                if k > 0:
                    write(out, jnp.where(lane < self.turn, before, now))
                    out += LANES
                before = now


def held_for(widths):
    tiles = sum(width // LANES + 2 for width in widths)
    return pltpu.VMEM((2, tiles, BAND + 2 * PAD, LANES), jnp.float32)


def each_band(mover, count, where, write):
    @pl.loop(0, count // 2)
    def _(pair):
        for slot in range(2):
            n = 2 * pair + slot
            j, d = where(n)
            mover.band(slot, j, d, functools.partial(write, n))


def forward(n):
    return 1 + n // 2, n


def backward(n):
    return 2 + n // 2, n


def own(n):
    return 0, n


def both_ways(n):
    return jnp.where(n < 4, forward(n)[0], backward(n - 4)[0]), lax.rem(n, SIDE)


def later(n):
    return jnp.where(n < 2, 1, jnp.where(n < 4, 3, 0)), lax.rem(jnp.where(n < 4, n + 2, n), SIDE)


def every(n):
    return n // SIDE, lax.rem(n, SIDE)


class Columns:
    def __init__(self, moves, rows, cols, arrays, places):
        self.moves, self.rows, self.cols, self.arrays, self.places = moves, rows, cols, arrays, places
        self.total = sum(width for _, _, width in places)
        self.scratch = [held_for([width for _, _, width in places])]

    def mover(self, moves, sources, held, theirs):
        pieces = [(source, *place) for source, place in zip(sources, self.places)]
        return Mover(moves, pieces, self.rows, self.cols, held, theirs)

    def run(self, body, out_shape, operands, after=(), theirs=False):
        count = len(self.arrays)

        def kernel(moves, *refs):
            mover = self.mover(moves, [refs[0]] * len(self.places), refs[-1], theirs)
            body(mover, *refs[count:-1])

        return call(
            kernel,
            out_shape,
            [*self.arrays, *operands],
            [self.moves],
            after,
            self.scratch,
        )

    def theirs(self, count, where, after=()):
        def body(mover, out):
            def write(n, begin, value):
                out[n, :, begin : begin + LANES] = value.astype(jnp.bfloat16)

            each_band(mover, count, where, write)

        shape = ((count, BAND, self.total), jnp.bfloat16)
        return self.run(body, [shape], [], after, True)[0]

    def loaded(self, frame, parts):
        def kernel(moves, frame, out, bands, held, sems):
            copies = [
                pltpu.make_async_copy(
                    frame.at[:, begin:end], out.at[:, begin:end], sems.at[p]
                )
                for p, (begin, end) in enumerate(parts)
            ]
            for copy in copies:
                copy.start()
            mover = self.mover(moves, [out] * len(self.places), held, True)
            for copy in copies[:-1]:
                copy.wait()

            def write(n, begin, value):
                bands[n, :, begin : begin + LANES] = value.astype(jnp.bfloat16)

            each_band(mover, SIDE * SIDE, every, write)
            copies[-1].wait()

        vmem = pl.BlockSpec(memory_space=pltpu.VMEM)
        return pl.pallas_call(
            kernel,
            in_specs=[
                pl.BlockSpec(memory_space=pltpu.SMEM),
                pl.BlockSpec(memory_space=pltpu.HBM),
            ],
            out_specs=[vmem, vmem],
            out_shape=[
                jax.ShapeDtypeStruct(frame.shape, frame.dtype),
                jax.ShapeDtypeStruct((SIDE * SIDE, BAND, self.total), jnp.bfloat16),
            ],
            scratch_shapes=[*self.scratch, pltpu.SemaphoreType.DMA((len(parts),))],
            compiler_params=pltpu.CompilerParams(vmem_limit_bytes=LOADING),
            cost_estimate=pl.CostEstimate(flops=1024, bytes_accessed=1024, transcendentals=0),
        )(self.moves, frame)

    def pairs(self, other, after=()):
        def body(mover, other, *outs):
            for way, where in enumerate((forward, backward)):

                def write(n, begin, value, way=way):
                    at = slice(begin, begin + LANES)
                    value = value + wide(other[way * SIDE + n, :, at])
                    outs[way][n, :, at] = value.astype(jnp.bfloat16)

                each_band(mover, SIDE, where, write)

        shape = ((SIDE, BAND, self.total), jnp.bfloat16)
        return self.run(body, [shape, shape], [other], after)

    def every_pair(self, other, after=()):
        def body(mover, other, *outs):
            for j in range(SIDE):

                def write(n, begin, value, j=j):
                    at = slice(begin, begin + LANES)
                    value = value + wide(other[j * SIDE + n, :, at])
                    outs[j][n, :, at] = value.astype(outs[j].dtype)

                each_band(mover, SIDE, lambda n, j=j: (j, n), write)

        quarter = (SIDE, BAND, self.total)
        shapes = [(quarter, jnp.float32)] + [(quarter, jnp.bfloat16)] * (SIDE - 1)
        return self.run(body, shapes, [other], after)

    def passed(self, forth, other, got, after=()):
        first, j, d0 = (0, 1, 2) if forth else (2, 3, 0)

        def body(mover, other, got, out):
            def write(n, begin, value):
                at = slice(begin, begin + LANES)
                value = (value + wide(other[first + n, :, at])) + wide(got[d0 + n, :, at])
                out[n, :, at] = value.astype(jnp.bfloat16)

            each_band(mover, 2, lambda n: (j, d0 + n), write)

        shape = ((2, BAND, self.total), jnp.bfloat16)
        return self.run(body, [shape], [other, got], after)[0]

    def rows_of_chip(self, other, forth, back, forth_far, back_far, scores, after=()):
        total = self.total

        def body(mover, other, forth, back, forth_far, back_far, *refs):
            score_refs, outs = refs[:SIDE], refs[SIDE:]
            for n in range(SIDE):
                near = forth if n < 2 else back
                far = back_far if n < 2 else forth_far

                def write(begin, value, n=n, near=near, far=far):
                    at = slice(begin, begin + LANES)
                    value = value + wide(other[SIDE + n, :, at])
                    value = value + (wide(near[n, :, at]) + wide(far[n % 2, :, at]))
                    outs[n][:, at] = value.astype(outs[n].dtype)

                mover.band(n % 2, 0, n, write)
            score = (score_refs[0][...] + score_refs[1][...]) + (
                score_refs[2][...] + score_refs[3][...]
            )
            high = wide(score.astype(jnp.bfloat16))
            middle = wide((score - high).astype(jnp.bfloat16))
            low = (score - high) - middle
            line = lax.broadcasted_iota(jnp.int32, score.shape, 0)
            three = jnp.where(line == 0, high, jnp.where(line == 1, middle, low))
            three = jnp.where(line < 3, three, 0.0)
            three = jnp.concatenate([three, jnp.zeros((BAND - PAD, LANES), jnp.float32)], 0)
            for out in outs:
                out[:, total:] = three.astype(out.dtype)

        wider = (BAND, total + LANES)
        shapes = [(wider, jnp.float32)] + [(wider, jnp.bfloat16)] * (SIDE - 1)
        operands = [other, forth, back, forth_far, back_far, *scores]
        return self.run(body, shapes, operands, after)


def row_kernel(mine, a, b, c, *outs):
    for d in range(SIDE):
        value = mine[d] + ((wide(a[d]) + wide(b[d])) + wide(c[d]))
        outs[d][...] = value.astype(outs[d].dtype)


def edge_kernel(scale, mine, a, b, c, left, right, right_sent):
    value = mine[...] + ((wide(a[...]) + wide(b[...])) + wide(c[...]))
    value = value * scale
    left[...] = value[:, :EDGE]
    right[...] = value[:, EDGE:]
    right_sent[...] = value[:, EDGE:].astype(jnp.bfloat16)


def image_kernel(scale, left, right, mine, a, b, c, out, score):
    total = mine.shape[1] - LANES
    out[:, :EDGE] = left[...]
    for begin in range(0, total, LANES):
        at = slice(begin, begin + LANES)
        value = mine[:, at] + ((wide(a[:, at]) + wide(b[:, at])) + wide(c[:, at]))
        out[:, EDGE + begin : EDGE + begin + LANES] = (value * scale).astype(jnp.bfloat16)
    out[:, EDGE + total :] = right[...]
    at = slice(total, total + LANES)
    value = mine[:PAD, at] + ((wide(a[:, at]) + wide(b[:, at])) + wide(c[:, at]))[:PAD]
    score[...] = jnp.sum(value, axis=0, keepdims=True)


def seam_kernel(
    widths, shifts, all_rows, own_left, own_right, next_left, prev_right, left_out, right_out, score_out
):
    tile = lax.axis_index("tile")
    earlier = jnp.maximum(tile - 1, 0)
    width_now, shift_now = widths[tile], shifts[tile]
    width_left = jnp.where(tile > 0, widths[earlier], 0)
    shift_left = jnp.where(tile > 0, shifts[earlier], 0)
    rows = own_left.shape[0]

    def rounded(ref):
        return wide(ref[...].astype(jnp.bfloat16))

    mine, after = rounded(own_right), rounded(next_left)
    column = lax.broadcasted_iota(jnp.int32, (rows, STRIP), 1)
    inside = column >= STRIP - width_now
    aligned = pltpu.roll(after, lax.rem(STRIP - width_now - shift_now + EDGE, EDGE), 1)[:, :STRIP]
    feather = ((STRIP - column).astype(jnp.float32) - 0.5) / jnp.maximum(width_now, 1).astype(
        jnp.float32
    )
    right_out[...] = jnp.where(inside, feather * mine + (1.0 - feather) * aligned, mine).astype(
        right_out.dtype
    )
    mine = rounded(own_left)
    before = jnp.concatenate(
        [prev_right[...].astype(jnp.float32), jnp.zeros((rows, LAGS), jnp.float32)], 1
    )
    before = pltpu.roll(before, lax.rem(shift_left + width_left - STRIP + EDGE, EDGE), 1)
    place = lax.broadcasted_iota(jnp.int32, (rows, EDGE), 1)
    within = (place >= shift_left) & (place < shift_left + width_left)
    weight = ((width_left - place + shift_left).astype(jnp.float32) - 0.5) / jnp.maximum(
        width_left, 1
    ).astype(jnp.float32)
    left_out[...] = jnp.where(within, weight * before + (1.0 - weight) * mine, mine).astype(
        left_out.dtype
    )
    masked = jnp.where(inside, own_right[...], 0.0)
    masked = pltpu.roll(masked, lax.rem(width_now, STRIP), 1)
    after = next_left[...]
    mine_high, after_high = masked.astype(jnp.bfloat16), after.astype(jnp.bfloat16)
    mine_low = (masked - wide(mine_high)).astype(jnp.bfloat16)
    after_low = (after - wide(after_high)).astype(jnp.bfloat16)
    gram = jnp.zeros((LANES, 2 * LANES), jnp.float32)
    for t in range(STRIP // LANES):
        for one, two in ((mine_high, after_high), (mine_high, after_low), (mine_low, after_high)):
            gram += lax.dot_general(
                one[:, t * LANES : (t + 1) * LANES],
                two[:, t * LANES : (t + 2) * LANES],
                (((0,), (0,)), ((), ())),
                preferred_element_type=jnp.float32,
            )
    line = lax.broadcasted_iota(jnp.int32, gram.shape, 0)
    step = 1
    while step < LANES:
        gram = jnp.where((line & step) != 0, pltpu.roll(gram, 2 * LANES - step, 1), gram)
        step *= 2
    total = jnp.sum(gram[:, :LANES], axis=0, keepdims=True)
    terms = jnp.full((PAD, LANES), all_rows * jnp.maximum(width_now, 1), jnp.int32)
    score_out[...] = jnp.broadcast_to(total, (PAD, LANES)) / jnp.sqrt(terms.astype(jnp.float32))


def body(movie, frame_shift, intersection, seam_shift):
    frame = movie[0, 0]
    rows, cols = frame.shape
    scale = 1.0 / math.sqrt(lax.axis_size("frame"))
    moves = frame_shift[0, 0]

    low, high = EDGE + LANES, cols - STRIP - LANES
    places = [(0, 0, EDGE), (0, cols - STRIP, STRIP)]
    frame, theirs_s = Columns(moves, rows, cols, [], places).loaded(
        frame, [(0, low), (high, cols), (low, high)]
    )
    strips = Columns(moves, rows, cols, [frame], places)
    middle = Columns(moves, rows, cols, [frame], [(0, EDGE, cols - STRIP - EDGE)])

    other_s = to_other_core(theirs_s)
    theirs_m = middle.theirs(2 * SIDE, both_ways, [theirs_s])
    other_m = to_other_core(*gated([theirs_m], [other_s]))
    pair_s = strips.every_pair(other_s, [theirs_m])
    got_s = [ahead(pair_s[j], 1, j) for j in (1, 2, 3)]
    theirs_l = middle.theirs(2 * SIDE, later, [pair_s[0]])
    other_l = to_other_core(theirs_l)
    pair_m = middle.pairs(other_m, [theirs_l])
    pair_f, pair_b = gated(pair_m, got_s)
    got_f, got_b = ahead(pair_f, 1, 1), ahead(pair_b, 1, -1)

    band = (BAND, EDGE + STRIP)
    row_s = call(
        row_kernel,
        [(band, jnp.float32)] + [(band, jnp.bfloat16)] * (SIDE - 1),
        [pair_s[0], *got_s],
        after=[pair_f, other_l],
    )
    own_left, own_right, sent_right = call(
        functools.partial(edge_kernel, scale),
        [((BAND, EDGE), jnp.float32), ((BAND, STRIP), jnp.float32), ((BAND, STRIP), jnp.bfloat16)],
        [row_s[0], *[ahead(row_s[j], 2, j) for j in (1, 2, 3)]],
    )
    next_left = from_behind(own_left, "tile", -1)
    prev_right = from_behind(sent_right, "tile", 1)
    left_part, right_part, score = call(
        lambda widths, shifts, *refs: seam_kernel(widths, shifts, rows, *refs),
        [((BAND, EDGE), jnp.bfloat16), ((BAND, STRIP), jnp.bfloat16), ((PAD, LANES), jnp.float32)],
        [own_left, own_right, next_left, prev_right],
        [intersection, seam_shift],
    )
    far_f = ahead(middle.passed(True, other_l, got_f, [score]), 1, 1)
    far_b = ahead(middle.passed(False, other_l, got_b, [score]), 1, -1)
    score = score + to_other_core(score)
    scores = [score, *[ahead(score, 1, j) for j in (1, 2, 3)]]
    row_m = middle.rows_of_chip(other_l, got_f, got_b, far_f, far_b, scores)
    image, score = call(
        functools.partial(image_kernel, scale),
        [((BAND, cols), jnp.bfloat16), ((1, LAGS), jnp.float32)],
        [left_part, right_part, row_m[0], *[ahead(row_m[j], 2, j) for j in (1, 2, 3)]],
    )
    return (image[None], score)


def solution(mesh):
    placed = (P("tile", "frame", None, None), P("tile", "frame", None), P(), P())
    return jax.shard_map(
        body,
        mesh=mesh,
        in_specs=placed,
        out_specs=(P("tile", "frame", None), P("tile", None)),
        check_vma=False,
    )
```

time: 285 us -> 79 us (0.28)
  the two profiles are of different devices: /device:TPU:96 before, /device:TPU:102 now
where the time goes in v2:
time: 79 us; the launch traced here: 78.3 us
  starting transfers between devices  30.1 us (38%)
  waiting for transfers between devices  27 us (34%)
  Pallas kernels  19.8 us (25%)
    ppermute x20, waiting for transfers between devices, permuted(): lax.ppermute(array, 'frame', [(device_at(*place), device_at(*target(*plac...  25.4 us
    ppermute x20, starting transfers between devices, permuted(): lax.ppermute(array, 'frame', [(device_at(*place), device_at(*target(*plac...  23 us
    pallas_call x11, Pallas kernels, call(): pl.pallas_call(run, in_specs=[pl.BlockSpec(memory_space=pltpu.SMEM)] * le...  14.8 us
    ppermute x2, starting transfers between devices, from_behind(): return lax.ppermute(array, axis, pairs)  7.05 us
    pallas_call x1, Pallas kernels, loaded(): pl.pallas_call(kernel, in_specs=[pl.BlockSpec(memory_space=pltpu.SMEM), p...  5 us
  transfers between devices with their start and end apart: 22, of which 15 were waited for; matrix products, arithmetic and copies ran while one was open for 0% of the time, Pallas kernels for 13%

profile of v2, /device:TPU:102, one launch (start us, length us, event | category | flops | bytes accessed | tf_op | source)
XLA Modules:
  0.0 78.3 jit_solution(1603369581164730449)
XLA Ops:
  1.3 5.0 %shard_map.59 = (bf16[1024,5760]{1,0:T(8,128)(2,1)S(1)}, bf16[16,32,1152]{2,1,0:T(8,128)(2,1)S(1)}) custom-call(s32[2]{0:T(128)S(1)} %bitcast.3, bf16[1024,5760]{1,0:T(8,128)(2,1)} %bitcast.11), custom_call_target="tpu_custom_call" | custom-call | flops 1024 | bytes 1024 | tf_op jit(solution)/shard_map/pallas_call | solution.py:239
  6.4 1.9 %shard_map.60.refs_3_.refs_0_ = bf16[8,32,4608]{2,1,0:T(8,128)(2,1)S(1)} custom-call(s32[2]{0:T(128)S(1)} %bitcast.4, bf16[1024,5760]{1,0:T(8,128)(2,1)S(1)} %get-tuple-element.28.refs_1_, bf16[16,32,1152]{2,1,0:T(8,128)(2,1)S(1)} %get-tuple-element.29.refs_2_), custom_call_target="tpu_custom_call" | custom-call | flops 1024 | bytes 1024 | tf_op jit(solution)/shard_map/pallas_call | solution.py:66
  9.2 2.1 %shard_map.61 = (f32[4,32,1152]{2,1,0:T(8,128)S(1)}, bf16[4,32,1152]{2,1,0:T(8,128)(2,1)S(1)}, bf16[4,32,1152]{2,1,0:T(8,128)(2,1)S(1)}, bf16[4,32,1152]{2,1,0:T(8,128)(2,1)S(1)}) custom-call(s32[2]{0:T(128)S(1)} %bitcast.5, bf16[1024,5760]{1,0:T(8,128)(2,1)S(1)} %get-tuple-element.28.refs_1_, ...), custom_call_target="tpu_custom_call" | custom-call | flops 1024 | bytes 1024 | tf_op jit(solution)/shard_map/pallas_call | solution.py:66
  11.6 1.9 %shard_map.63.refs_3_ = bf16[8,32,4608]{2,1,0:T(8,128)(2,1)S(1)} custom-call(s32[2]{0:T(128)S(1)} %bitcast.6, bf16[1024,5760]{1,0:T(8,128)(2,1)S(1)} %get-tuple-element.28.refs_1_, f32[4,32,1152]{2,1,0:T(8,128)S(1)} %get-tuple-element.30.refs_2_.refs_0_), custom_call_target="tpu_custom_call" | custom-call | flops 1024 | bytes 1024 | tf_op jit(solution)/shard_map/pallas_call | solution.py:66
  14.4 2.4 %collective-permute-start.2 = (bf16[4,32,1152]{2,1,0:T(8,128)(2,1)S(1)}, bf16[4,32,1152]{2,1,0:T(8,128)(2,1)S(1)}, u32[]{:S(2)}, u32[]{:S(2)}) collective-permute-start(bf16[4,32,1152]{2,1,0:T(8,128)(2,1)S(1)} %get-tuple-element.32), channel_id=1, source_target_pairs={{0,4},{1,17},{2,6},{3,19},{4,0},{5,21},{6,2},{7,23},{8,12},{9,25},... | collective-permute-start | bytes 884744 | tf_op jit(solution)/shard_map/ppermute | solution.py:30
  16.8 2.5 %shard_map.64 = (bf16[4,32,4608]{2,1,0:T(8,128)(2,1)S(1)}, bf16[4,32,4608]{2,1,0:T(8,128)(2,1)S(1)}) custom-call(s32[2]{0:T(128)S(1)} %bitcast.7, bf16[1024,5760]{1,0:T(8,128)(2,1)S(1)} %get-tuple-element.28.refs_1_, bf16[8,32,4608]{2,1,0:T(8,128)(2,1)S(1)} %collective-permute-done.4.refs_2_, bf16[8,32,4608]{2,1,0:T(8,128)(2,1)S(1)} %shard_map.63.refs_3_), custom_call_target="tpu_custom_call" | custom-call | flops 1024 | bytes 1024 | tf_op jit(solution)/shard_map/pallas_call | solution.py:66
  20.6 2.1 %collective-permute-done.2.refs_3_.refs_2_ = bf16[4,32,1152]{2,1,0:T(8,128)(2,1)S(1)} collective-permute-done((bf16[4,32,1152]{2,1,0:T(8,128)(2,1)S(1)}, bf16[4,32,1152]{2,1,0:T(8,128)(2,1)S(1)}, u32[]{:S(2)}, u32[]{:S(2)}) %collective-permute-start.2) | collective-permute-done | bytes 294944 | tf_op jit(solution)/shard_map/ppermute | solution.py:30
  22.7 3.1 %collective-permute-done.3.refs_4_.refs_3_ = bf16[4,32,1152]{2,1,0:T(8,128)(2,1)S(1)} collective-permute-done((bf16[4,32,1152]{2,1,0:T(8,128)(2,1)S(1)}, bf16[4,32,1152]{2,1,0:T(8,128)(2,1)S(1)}, u32[]{:S(2)}, u32[]{:S(2)}) %collective-permute-start.3) | collective-permute-done | bytes 294944 | tf_op jit(solution)/shard_map/ppermute | solution.py:30
  28.0 1.6 %collective-permute-start.6 = (bf16[32,1152]{1,0:T(8,128)(2,1)S(1)}, bf16[32,1152]{1,0:T(8,128)(2,1)S(1)}, u32[]{:S(2)}, u32[]{:S(2)}) collective-permute-start(bf16[32,1152]{1,0:T(8,128)(2,1)S(1)} %get-tuple-element.38), channel_id=1, source_target_pairs={{0,8},{1,3},{2,10},{3,5},{4,12},{5,7},{6,14},{7,1},{8,16},{9,11},{... | collective-permute-start | bytes 221192 | tf_op jit(solution)/shard_map/ppermute | solution.py:30
  29.6 2.9 %collective-permute-start.7 = (bf16[32,1152]{1,0:T(8,128)(2,1)S(1)}, bf16[32,1152]{1,0:T(8,128)(2,1)S(1)}, u32[]{:S(2)}, u32[]{:S(2)}) collective-permute-start(bf16[32,1152]{1,0:T(8,128)(2,1)S(1)} %get-tuple-element.39), channel_id=1, source_target_pairs={{0,16},{1,5},{2,18},{3,7},{4,20},{5,1},{6,22},{7,3},{8,24},{9,13},... | collective-permute-start | bytes 221192 | tf_op jit(solution)/shard_map/ppermute | solution.py:30
  32.5 1.3 %collective-permute-start.8 = (bf16[32,1152]{1,0:T(8,128)(2,1)S(1)}, bf16[32,1152]{1,0:T(8,128)(2,1)S(1)}, u32[]{:S(2)}, u32[]{:S(2)}) collective-permute-start(bf16[32,1152]{1,0:T(8,128)(2,1)S(1)} %get-tuple-element.40), channel_id=1, source_target_pairs={{0,24},{1,7},{2,26},{3,1},{4,28},{5,3},{6,30},{7,5},{8,0},{9,15},{... | collective-permute-start | bytes 221192 | tf_op jit(solution)/shard_map/ppermute | solution.py:30
  34.5 2.8 %collective-permute-done.7.refs_2_ = bf16[32,1152]{1,0:T(8,128)(2,1)S(1)} collective-permute-done((bf16[32,1152]{1,0:T(8,128)(2,1)S(1)}, bf16[32,1152]{1,0:T(8,128)(2,1)S(1)}, u32[]{:S(2)}, u32[]{:S(2)}) %collective-permute-start.7) | collective-permute-done | bytes 73760 | tf_op jit(solution)/shard_map/ppermute | solution.py:30
  37.8 2.0 %collective-permute-start.9 = (f32[32,640]{1,0:T(8,128)S(1)}, f32[32,640]{1,0:T(8,128)S(1)}, u32[]{:S(2)}, u32[]{:S(2)}) collective-permute-start(f32[32,640]{1,0:T(8,128)S(1)} %get-tuple-element.41.refs_2_), channel_id=1, source_target_pairs={{32,0},{64,32},{96,64},{128,96},{160,128},{192,160},{224,192},{33,... | collective-permute-start | bytes 245768 | tf_op jit(solution)/shard_map/ppermute | solution.py:51
  39.8 5.0 %collective-permute-start.10 = (bf16[32,512]{1,0:T(8,128)(2,1)S(1)}, bf16[32,512]{1,0:T(8,128)(2,1)S(1)}, u32[]{:S(2)}, u32[]{:S(2)}) collective-permute-start(bf16[32,512]{1,0:T(8,128)(2,1)S(1)} %get-tuple-element.43), channel_id=1, source_target_pairs={{0,32},{32,64},{64,96},{96,128},{128,160},{160,192},{192,224},{1,3... | collective-permute-start | bytes 98312 | tf_op jit(solution)/shard_map/ppermute | solution.py:51
  44.8 1.6 %collective-permute-done.10.refs_5_ = bf16[32,512]{1,0:T(8,128)(2,1)S(1)} collective-permute-done((bf16[32,512]{1,0:T(8,128)(2,1)S(1)}, bf16[32,512]{1,0:T(8,128)(2,1)S(1)}, u32[]{:S(2)}, u32[]{:S(2)}) %collective-permute-start.10) | collective-permute-done | bytes 32800 | tf_op jit(solution)/shard_map/ppermute | solution.py:51
  46.4 1.5 %shard_map.68 = (bf16[32,640]{1,0:T(8,128)(2,1)S(1)}, bf16[32,512]{1,0:T(8,128)(2,1)S(1)}, f32[8,128]{1,0:T(8,128)S(1)}) custom-call(s32[8]{0:T(128)S(1)} %copy-done.1, s32[8]{0:T(128)S(1)} %copy-done.2, f32[32,640]{1,0:T(8,128)S(1)} %get-tuple-element.41.refs_2_, f32[32,512]{1,0:T(8,128)S(1)} %get-tuple-element.42.refs_3_, ...), custom_call_target="tpu_custom_call" | custom-call | flops 1024 | bytes 1024 | tf_op jit(solution)/shard_map/pallas_call | solution.py:66
  49.1 2.2 %collective-permute-start.13 = (bf16[2,32,4608]{2,1,0:T(8,128)(2,1)S(1)}, bf16[2,32,4608]{2,1,0:T(8,128)(2,1)S(1)}, u32[]{:S(2)}, u32[]{:S(2)}) collective-permute-start(bf16[2,32,4608]{2,1,0:T(8,128)(2,1)S(1)} %shard_map.69), channel_id=1, source_target_pairs={{0,2},{1,9},{2,4},{3,11},{4,6},{5,13},{6,0},{7,15},{8,10},{9,17},{... | collective-permute-start | bytes 1769480 | tf_op jit(solution)/shard_map/ppermute | solution.py:30
  53.7 3.1 %collective-permute-start.16 = (f32[8,128]{1,0:T(8,128)S(1)}, f32[8,128]{1,0:T(8,128)S(1)}, u32[]{:S(2)}, u32[]{:S(2)}) collective-permute-start(f32[8,128]{1,0:T(8,128)S(1)} %add.3.refs_7_), channel_id=1, source_target_pairs={{0,2},{1,9},{2,4},{3,11},{4,6},{5,13},{6,0},{7,15},{8,10},{9,17},{... | collective-permute-start | bytes 12296 | tf_op jit(solution)/shard_map/ppermute | solution.py:30
  57.7 1.6 %collective-permute-done.16.refs_8_ = f32[8,128]{1,0:T(8,128)S(1)} collective-permute-done((f32[8,128]{1,0:T(8,128)S(1)}, f32[8,128]{1,0:T(8,128)S(1)}, u32[]{:S(2)}, u32[]{:S(2)}) %collective-permute-start.16) | collective-permute-done | bytes 4128 | tf_op jit(solution)/shard_map/ppermute | solution.py:30
  59.2 3.3 %collective-permute-done.17.refs_9_ = f32[8,128]{1,0:T(8,128)S(1)} collective-permute-done((f32[8,128]{1,0:T(8,128)S(1)}, f32[8,128]{1,0:T(8,128)S(1)}, u32[]{:S(2)}, u32[]{:S(2)}) %collective-permute-start.17) | collective-permute-done | bytes 4128 | tf_op jit(solution)/shard_map/ppermute | solution.py:30
  63.6 1.5 %shard_map.71 = (f32[32,4736]{1,0:T(8,128)S(1)}, bf16[32,4736]{1,0:T(8,128)(2,1)S(1)}, bf16[32,4736]{1,0:T(8,128)(2,1)S(1)}, bf16[32,4736]{1,0:T(8,128)(2,1)S(1)}) custom-call(s32[2]{0:T(128)S(1)} %bitcast.10, bf16[1024,5760]{1,0:T(8,128)(2,1)S(1)} %get-tuple-element.28.refs_1_, bf16[8,32,4608]{2,1,0:T(8,128)(2,1)S(1)} %collective-permute-done.5.refs_5_.refs_2_, ...), custom_call_target="tpu_custom_call" | custom-call | flops 1024 | bytes 1024 | tf_op jit(solution)/shard_map/pallas_call | solution.py:66
  65.6 3.6 %collective-permute-start.20 = (bf16[32,4736]{1,0:T(8,128)(2,1)S(1)}, bf16[32,4736]{1,0:T(8,128)(2,1)S(1)}, u32[]{:S(2)}, u32[]{:S(2)}) collective-permute-start(bf16[32,4736]{1,0:T(8,128)(2,1)S(1)} %get-tuple-element.50), channel_id=1, source_target_pairs={{0,16},{1,5},{2,18},{3,7},{4,20},{5,1},{6,22},{7,3},{8,24},{9,13},... | collective-permute-start | bytes 909320 | tf_op jit(solution)/shard_map/ppermute | solution.py:30
  70.2 3.0 %collective-permute-done.19.refs_3_ = bf16[32,4736]{1,0:T(8,128)(2,1)S(1)} collective-permute-done((bf16[32,4736]{1,0:T(8,128)(2,1)S(1)}, bf16[32,4736]{1,0:T(8,128)(2,1)S(1)}, u32[]{:S(2)}, u32[]{:S(2)}) %collective-permute-start.19) | collective-permute-done | bytes 303136 | tf_op jit(solution)/shard_map/ppermute | solution.py:30
  73.2 4.0 %collective-permute-done.20.refs_4_ = bf16[32,4736]{1,0:T(8,128)(2,1)S(1)} collective-permute-done((bf16[32,4736]{1,0:T(8,128)(2,1)S(1)}, bf16[32,4736]{1,0:T(8,128)(2,1)S(1)}, u32[]{:S(2)}, u32[]{:S(2)}) %collective-permute-start.20) | collective-permute-done | bytes 303136 | tf_op jit(solution)/shard_map/ppermute | solution.py:30
  (41 shorter events, 15.2 us)
Async XLA Ops:
  6.3 2.9 %collective-permute-start = (bf16[16,32,1152]{2,1,0:T(8,128)(2,1)S(1)}, bf16[16,32,1152]{2,1,0:T(8,128)(2,1)S(1)}, u32[]{:S(2)}, u32[]{:S(2)}) collective-permute-start(bf16[16,32,1152]{2,1,0:T(8,128)(2,1)S(1)} %get-tuple-element.29.refs_2_), channel_id=1, source_target_pairs={{0,1},{1,0},{2,3},{3,2},{4,5},{5,4},{6,7},{7,6},{8,9},{9,8},{10,11... | collective-permute-start | bytes 3538952 | tf_op jit(solution)/shard_map/ppermute | solution.py:30
  11.3 5.5 %collective-permute-start.4 = (bf16[8,32,4608]{2,1,0:T(8,128)(2,1)S(1)}, bf16[8,32,4608]{2,1,0:T(8,128)(2,1)S(1)}, u32[]{:S(2)}, u32[]{:S(2)}) collective-permute-start(bf16[8,32,4608]{2,1,0:T(8,128)(2,1)S(1)} %shard_map.62), channel_id=1, source_target_pairs={{0,1},{1,0},{2,3},{3,2},{4,5},{5,4},{6,7},{7,6},{8,9},{9,8},{10,11... | collective-permute-start | bytes 7077896 | tf_op jit(solution)/shard_map/ppermute | solution.py:30
  13.5 14.4 %collective-permute-start.5 = (bf16[8,32,4608]{2,1,0:T(8,128)(2,1)S(1)}, bf16[8,32,4608]{2,1,0:T(8,128)(2,1)S(1)}, u32[]{:S(2)}, u32[]{:S(2)}) collective-permute-start(bf16[8,32,4608]{2,1,0:T(8,128)(2,1)S(1)} %shard_map.63.refs_3_), channel_id=1, source_target_pairs={{0,1},{1,0},{2,3},{3,2},{4,5},{5,4},{6,7},{7,6},{8,9},{9,8},{10,11... | collective-permute-start | bytes 7077896 | tf_op jit(solution)/shard_map/ppermute | solution.py:30
  13.9 6.7 %collective-permute-start.1 = (bf16[4,32,1152]{2,1,0:T(8,128)(2,1)S(1)}, bf16[4,32,1152]{2,1,0:T(8,128)(2,1)S(1)}, u32[]{:S(2)}, u32[]{:S(2)}) collective-permute-start(bf16[4,32,1152]{2,1,0:T(8,128)(2,1)S(1)} %get-tuple-element.31), channel_id=1, source_target_pairs={{0,2},{1,9},{2,4},{3,11},{4,6},{5,13},{6,0},{7,15},{8,10},{9,17},{... | collective-permute-start | bytes 884744 | tf_op jit(solution)/shard_map/ppermute | solution.py:30
  14.4 8.3 %collective-permute-start.2 = (bf16[4,32,1152]{2,1,0:T(8,128)(2,1)S(1)}, bf16[4,32,1152]{2,1,0:T(8,128)(2,1)S(1)}, u32[]{:S(2)}, u32[]{:S(2)}) collective-permute-start(bf16[4,32,1152]{2,1,0:T(8,128)(2,1)S(1)} %get-tuple-element.32), channel_id=1, source_target_pairs={{0,4},{1,17},{2,6},{3,19},{4,0},{5,21},{6,2},{7,23},{8,12},{9,25},... | collective-permute-start | bytes 884744 | tf_op jit(solution)/shard_map/ppermute | solution.py:30
  16.8 9.0 %collective-permute-start.3 = (bf16[4,32,1152]{2,1,0:T(8,128)(2,1)S(1)}, bf16[4,32,1152]{2,1,0:T(8,128)(2,1)S(1)}, u32[]{:S(2)}, u32[]{:S(2)}) collective-permute-start(bf16[4,32,1152]{2,1,0:T(8,128)(2,1)S(1)} %get-tuple-element.33), channel_id=1, source_target_pairs={{0,6},{1,25},{2,0},{3,27},{4,2},{5,29},{6,4},{7,31},{8,14},{9,1},{... | collective-permute-start | bytes 884744 | tf_op jit(solution)/shard_map/ppermute | solution.py:30
  25.8 22.2 %collective-permute-start.11 = (bf16[4,32,4608]{2,1,0:T(8,128)(2,1)S(1)}, bf16[4,32,4608]{2,1,0:T(8,128)(2,1)S(1)}, u32[]{:S(2)}, u32[]{:S(2)}) collective-permute-start(bf16[4,32,4608]{2,1,0:T(8,128)(2,1)S(1)} %get-tuple-element.36.refs_4_), channel_id=1, source_target_pairs={{0,2},{1,9},{2,4},{3,11},{4,6},{5,13},{6,0},{7,15},{8,10},{9,17},{... | collective-permute-start | bytes 3538952 | tf_op jit(solution)/shard_map/ppermute | solution.py:30
  26.5 19.9 %copy-start.1 = (s32[8]{0:T(128)S(1)}, s32[8]{0:T(128)}, u32[]{:S(2)}) copy-start(s32[8]{0:T(128)} %refs_0_.1) | copy-start | bytes 100
  26.5 19.9 %copy-start.2 = (s32[8]{0:T(128)S(1)}, s32[8]{0:T(128)}, u32[]{:S(2)}) copy-start(s32[8]{0:T(128)} %refs_1_.1) | copy-start | bytes 100
  26.5 24.8 %collective-permute-start.12 = (bf16[4,32,4608]{2,1,0:T(8,128)(2,1)S(1)}, bf16[4,32,4608]{2,1,0:T(8,128)(2,1)S(1)}, u32[]{:S(2)}, u32[]{:S(2)}) collective-permute-start(bf16[4,32,4608]{2,1,0:T(8,128)(2,1)S(1)} %get-tuple-element.46), channel_id=1, source_target_pairs={{0,6},{1,25},{2,0},{3,27},{4,2},{5,29},{6,4},{7,31},{8,14},{9,1},{... | collective-permute-start | bytes 3538952 | tf_op jit(solution)/shard_map/ppermute | solution.py:30
  28.0 6.5 %collective-permute-start.6 = (bf16[32,1152]{1,0:T(8,128)(2,1)S(1)}, bf16[32,1152]{1,0:T(8,128)(2,1)S(1)}, u32[]{:S(2)}, u32[]{:S(2)}) collective-permute-start(bf16[32,1152]{1,0:T(8,128)(2,1)S(1)} %get-tuple-element.38), channel_id=1, source_target_pairs={{0,8},{1,3},{2,10},{3,5},{4,12},{5,7},{6,14},{7,1},{8,16},{9,11},{... | collective-permute-start | bytes 221192 | tf_op jit(solution)/shard_map/ppermute | solution.py:30
  29.6 7.7 %collective-permute-start.7 = (bf16[32,1152]{1,0:T(8,128)(2,1)S(1)}, bf16[32,1152]{1,0:T(8,128)(2,1)S(1)}, u32[]{:S(2)}, u32[]{:S(2)}) collective-permute-start(bf16[32,1152]{1,0:T(8,128)(2,1)S(1)} %get-tuple-element.39), channel_id=1, source_target_pairs={{0,16},{1,5},{2,18},{3,7},{4,20},{5,1},{6,22},{7,3},{8,24},{9,13},... | collective-permute-start | bytes 221192 | tf_op jit(solution)/shard_map/ppermute | solution.py:30
  32.5 5.2 %collective-permute-start.8 = (bf16[32,1152]{1,0:T(8,128)(2,1)S(1)}, bf16[32,1152]{1,0:T(8,128)(2,1)S(1)}, u32[]{:S(2)}, u32[]{:S(2)}) collective-permute-start(bf16[32,1152]{1,0:T(8,128)(2,1)S(1)} %get-tuple-element.40), channel_id=1, source_target_pairs={{0,24},{1,7},{2,26},{3,1},{4,28},{5,3},{6,30},{7,5},{8,0},{9,15},{... | collective-permute-start | bytes 221192 | tf_op jit(solution)/shard_map/ppermute | solution.py:30
  37.8 8.6 %collective-permute-start.9 = (f32[32,640]{1,0:T(8,128)S(1)}, f32[32,640]{1,0:T(8,128)S(1)}, u32[]{:S(2)}, u32[]{:S(2)}) collective-permute-start(f32[32,640]{1,0:T(8,128)S(1)} %get-tuple-element.41.refs_2_), channel_id=1, source_target_pairs={{32,0},{64,32},{96,64},{128,96},{160,128},{192,160},{224,192},{33,... | collective-permute-start | bytes 245768 | tf_op jit(solution)/shard_map/ppermute | solution.py:51
  39.8 6.6 %collective-permute-start.10 = (bf16[32,512]{1,0:T(8,128)(2,1)S(1)}, bf16[32,512]{1,0:T(8,128)(2,1)S(1)}, u32[]{:S(2)}, u32[]{:S(2)}) collective-permute-start(bf16[32,512]{1,0:T(8,128)(2,1)S(1)} %get-tuple-element.43), channel_id=1, source_target_pairs={{0,32},{32,64},{64,96},{96,128},{128,160},{160,192},{192,224},{1,3... | collective-permute-start | bytes 98312 | tf_op jit(solution)/shard_map/ppermute | solution.py:51
  49.1 14.5 %collective-permute-start.13 = (bf16[2,32,4608]{2,1,0:T(8,128)(2,1)S(1)}, bf16[2,32,4608]{2,1,0:T(8,128)(2,1)S(1)}, u32[]{:S(2)}, u32[]{:S(2)}) collective-permute-start(bf16[2,32,4608]{2,1,0:T(8,128)(2,1)S(1)} %shard_map.69), channel_id=1, source_target_pairs={{0,2},{1,9},{2,4},{3,11},{4,6},{5,13},{6,0},{7,15},{8,10},{9,17},{... | collective-permute-start | bytes 1769480 | tf_op jit(solution)/shard_map/ppermute | solution.py:30
  52.3 11.3 %collective-permute-start.14 = (bf16[2,32,4608]{2,1,0:T(8,128)(2,1)S(1)}, bf16[2,32,4608]{2,1,0:T(8,128)(2,1)S(1)}, u32[]{:S(2)}, u32[]{:S(2)}) collective-permute-start(bf16[2,32,4608]{2,1,0:T(8,128)(2,1)S(1)} %shard_map.70), channel_id=1, source_target_pairs={{0,6},{1,25},{2,0},{3,27},{4,2},{5,29},{6,4},{7,31},{8,14},{9,1},{... | collective-permute-start | bytes 1769480 | tf_op jit(solution)/shard_map/ppermute | solution.py:30
  52.5 1.2 %collective-permute-start.15 = (f32[8,128]{1,0:T(8,128)S(1)}, f32[8,128]{1,0:T(8,128)S(1)}, u32[]{:S(2)}, u32[]{:S(2)}) collective-permute-start(f32[8,128]{1,0:T(8,128)S(1)} %get-tuple-element.47.refs_4_), channel_id=1, source_target_pairs={{0,1},{1,0},{2,3},{3,2},{4,5},{5,4},{6,7},{7,6},{8,9},{9,8},{10,11... | collective-permute-start | bytes 12296 | tf_op jit(solution)/shard_map/ppermute | solution.py:30
  53.7 5.5 %collective-permute-start.16 = (f32[8,128]{1,0:T(8,128)S(1)}, f32[8,128]{1,0:T(8,128)S(1)}, u32[]{:S(2)}, u32[]{:S(2)}) collective-permute-start(f32[8,128]{1,0:T(8,128)S(1)} %add.3.refs_7_), channel_id=1, source_target_pairs={{0,2},{1,9},{2,4},{3,11},{4,6},{5,13},{6,0},{7,15},{8,10},{9,17},{... | collective-permute-start | bytes 12296 | tf_op jit(solution)/shard_map/ppermute | solution.py:30
  56.8 5.8 %collective-permute-start.17 = (f32[8,128]{1,0:T(8,128)S(1)}, f32[8,128]{1,0:T(8,128)S(1)}, u32[]{:S(2)}, u32[]{:S(2)}) collective-permute-start(f32[8,128]{1,0:T(8,128)S(1)} %add.3.refs_7_), channel_id=1, source_target_pairs={{0,4},{1,17},{2,6},{3,19},{4,0},{5,21},{6,2},{7,23},{8,12},{9,25},... | collective-permute-start | bytes 12296 | tf_op jit(solution)/shard_map/ppermute | solution.py:30
  56.8 6.8 %collective-permute-start.18 = (f32[8,128]{1,0:T(8,128)S(1)}, f32[8,128]{1,0:T(8,128)S(1)}, u32[]{:S(2)}, u32[]{:S(2)}) collective-permute-start(f32[8,128]{1,0:T(8,128)S(1)} %add.3.refs_7_), channel_id=1, source_target_pairs={{0,6},{1,25},{2,0},{3,27},{4,2},{5,29},{6,4},{7,31},{8,14},{9,1},{... | collective-permute-start | bytes 12296 | tf_op jit(solution)/shard_map/ppermute | solution.py:30
  65.1 8.1 %collective-permute-start.19 = (bf16[32,4736]{1,0:T(8,128)(2,1)S(1)}, bf16[32,4736]{1,0:T(8,128)(2,1)S(1)}, u32[]{:S(2)}, u32[]{:S(2)}) collective-permute-start(bf16[32,4736]{1,0:T(8,128)(2,1)S(1)} %get-tuple-element.49), channel_id=1, source_target_pairs={{0,8},{1,3},{2,10},{3,5},{4,12},{5,7},{6,14},{7,1},{8,16},{9,11},{... | collective-permute-start | bytes 909320 | tf_op jit(solution)/shard_map/ppermute | solution.py:30
  65.6 11.7 %collective-permute-start.20 = (bf16[32,4736]{1,0:T(8,128)(2,1)S(1)}, bf16[32,4736]{1,0:T(8,128)(2,1)S(1)}, u32[]{:S(2)}, u32[]{:S(2)}) collective-permute-start(bf16[32,4736]{1,0:T(8,128)(2,1)S(1)} %get-tuple-element.50), channel_id=1, source_target_pairs={{0,16},{1,5},{2,18},{3,7},{4,20},{5,1},{6,22},{7,3},{8,24},{9,13},... | collective-permute-start | bytes 909320 | tf_op jit(solution)/shard_map/ppermute | solution.py:30
  69.2 8.1 %collective-permute-start.21 = (bf16[32,4736]{1,0:T(8,128)(2,1)S(1)}, bf16[32,4736]{1,0:T(8,128)(2,1)S(1)}, u32[]{:S(2)}, u32[]{:S(2)}) collective-permute-start(bf16[32,4736]{1,0:T(8,128)(2,1)S(1)} %get-tuple-element.51), channel_id=1, source_target_pairs={{0,24},{1,7},{2,26},{3,1},{4,28},{5,3},{6,30},{7,5},{8,0},{9,15},{... | collective-permute-start | bytes 909320 | tf_op jit(solution)/shard_map/ppermute | solution.py:30
  (1 other events, 0.7 us)

commit v3 on v2

--- a/solution.py
+++ b/solution.py
@@ -43,6 +43,10 @@
         return ((y + by) % SIDE, x, core)
 
     return permuted(array, target)
+
+
+def direct(arrays, stage):
+    return [ahead(arrays[j], stage, j) for j in (2, 1, 3)]
 
 
 def from_behind(array, axis, by):
@@ -171,8 +175,12 @@
     return jnp.where(n < 4, forward(n)[0], backward(n - 4)[0]), lax.rem(n, SIDE)
 
 
+def passing(n):
+    return jnp.where(n < 2, 1, 3), lax.rem(n + 2, SIDE)
+
+
 def later(n):
-    return jnp.where(n < 2, 1, jnp.where(n < 4, 3, 0)), lax.rem(jnp.where(n < 4, n + 2, n), SIDE)
+    return jnp.where(n < 4, passing(n)[0], 0), lax.rem(jnp.where(n < 4, n + 2, n), SIDE)
 
 
 def every(n):
@@ -215,39 +223,67 @@
         shape = ((count, BAND, self.total), jnp.bfloat16)
         return self.run(body, [shape], [], after, True)[0]
 
-    def loaded(self, frame, parts):
-        def kernel(moves, frame, out, bands, held, sems):
+    def loaded(self, frame, low, high, middle):
+        rows, cols = frame.shape
+        first, last = middle[0][0], middle[-1][1]
+        ends = [min(end + LANES, high) for _, end in middle]
+        parts = [(0, low), (high, cols), *zip([low, *ends[:-1]], ends)]
+        halves = [slice(i * rows // SIDE, (i + 1) * rows // SIDE) for i in range(SIDE)]
+
+        def kernel(moves_far, frame, out, bands, both, held, held_middle, moves, sems, moves_sem):
             copies = [
-                pltpu.make_async_copy(
-                    frame.at[:, begin:end], out.at[:, begin:end], sems.at[p]
-                )
+                [
+                    pltpu.make_async_copy(
+                        frame.at[half, begin:end], out.at[half, begin:end], sems.at[p, h]
+                    )
+                    for h, half in enumerate(halves)
+                ]
                 for p, (begin, end) in enumerate(parts)
             ]
-            for copy in copies:
-                copy.start()
+            moves_copy = pltpu.make_async_copy(moves_far, moves, moves_sem)
+            moves_copy.start()
+            for pair in copies:
+                for copy in pair:
+                    copy.start()
+            moves_copy.wait()
+            for copy in (*copies[0], *copies[1]):
+                copy.wait()
             mover = self.mover(moves, [out] * len(self.places), held, True)
-            for copy in copies[:-1]:
-                copy.wait()
 
             def write(n, begin, value):
                 bands[n, :, begin : begin + LANES] = value.astype(jnp.bfloat16)
 
             each_band(mover, SIDE * SIDE, every, write)
-            copies[-1].wait()
+            for pair, (begin, end) in zip(copies[2:], middle):
+                for copy in pair:
+                    copy.wait()
+                mover = Mover(moves, [(out, 0, begin, end - begin)], rows, cols, held_middle, True)
+
+                def write_middle(n, at, value, begin=begin):
+                    at = at + begin - first
+                    both[n, :, at : at + LANES] = value.astype(jnp.bfloat16)
+
+                each_band(mover, 2 * SIDE, both_ways, write_middle)
 
         vmem = pl.BlockSpec(memory_space=pltpu.VMEM)
+        far = pl.BlockSpec(memory_space=pltpu.HBM)
+        widest = max(end - begin for begin, end in middle)
         return pl.pallas_call(
             kernel,
-            in_specs=[
-                pl.BlockSpec(memory_space=pltpu.SMEM),
-                pl.BlockSpec(memory_space=pltpu.HBM),
-            ],
-            out_specs=[vmem, vmem],
+            in_specs=[far, far],
+            out_specs=[vmem, vmem, vmem],
             out_shape=[
                 jax.ShapeDtypeStruct(frame.shape, frame.dtype),
                 jax.ShapeDtypeStruct((SIDE * SIDE, BAND, self.total), jnp.bfloat16),
+                jax.ShapeDtypeStruct((2 * SIDE, BAND, last - first), jnp.bfloat16),
             ],
-            scratch_shapes=[*self.scratch, pltpu.SemaphoreType.DMA((len(parts),))],
+            scratch_shapes=[
+                *self.scratch,
+                held_for([widest]),
+                pltpu.SMEM(self.moves.shape, jnp.int32),
+                pltpu.SemaphoreType.DMA((len(parts), len(halves))),
+                pltpu.SemaphoreType.DMA,
+            ],
             compiler_params=pltpu.CompilerParams(vmem_limit_bytes=LOADING),
             cost_estimate=pl.CostEstimate(flops=1024, bytes_accessed=1024, transcendentals=0),
         )(self.moves, frame)
@@ -281,53 +317,54 @@
         shapes = [(quarter, jnp.float32)] + [(quarter, jnp.bfloat16)] * (SIDE - 1)
         return self.run(body, shapes, [other], after)
 
-    def passed(self, forth, other, got, after=()):
-        first, j, d0 = (0, 1, 2) if forth else (2, 3, 0)
-
-        def body(mover, other, got, out):
-            def write(n, begin, value):
-                at = slice(begin, begin + LANES)
-                value = (value + wide(other[first + n, :, at])) + wide(got[d0 + n, :, at])
-                out[n, :, at] = value.astype(jnp.bfloat16)
-
-            each_band(mover, 2, lambda n: (j, d0 + n), write)
-
-        shape = ((2, BAND, self.total), jnp.bfloat16)
-        return self.run(body, [shape], [other, got], after)[0]
-
-    def rows_of_chip(self, other, forth, back, forth_far, back_far, scores, after=()):
-        total = self.total
-
-        def body(mover, other, forth, back, forth_far, back_far, *refs):
-            score_refs, outs = refs[:SIDE], refs[SIDE:]
-            for n in range(SIDE):
-                near = forth if n < 2 else back
-                far = back_far if n < 2 else forth_far
-
-                def write(begin, value, n=n, near=near, far=far):
+    def later_pairs(self, other, after=()):
+        def body(mover, other, *outs):
+            for part, out in enumerate(outs):
+
+                def write(n, begin, value, part=part, out=out):
                     at = slice(begin, begin + LANES)
-                    value = value + wide(other[SIDE + n, :, at])
-                    value = value + (wide(near[n, :, at]) + wide(far[n % 2, :, at]))
-                    outs[n][:, at] = value.astype(outs[n].dtype)
-
-                mover.band(n % 2, 0, n, write)
-            score = (score_refs[0][...] + score_refs[1][...]) + (
-                score_refs[2][...] + score_refs[3][...]
-            )
-            high = wide(score.astype(jnp.bfloat16))
-            middle = wide((score - high).astype(jnp.bfloat16))
-            low = (score - high) - middle
-            line = lax.broadcasted_iota(jnp.int32, score.shape, 0)
-            three = jnp.where(line == 0, high, jnp.where(line == 1, middle, low))
-            three = jnp.where(line < 3, three, 0.0)
-            three = jnp.concatenate([three, jnp.zeros((BAND - PAD, LANES), jnp.float32)], 0)
-            for out in outs:
-                out[:, total:] = three.astype(out.dtype)
-
-        wider = (BAND, total + LANES)
-        shapes = [(wider, jnp.float32)] + [(wider, jnp.bfloat16)] * (SIDE - 1)
-        operands = [other, forth, back, forth_far, back_far, *scores]
-        return self.run(body, shapes, operands, after)
+                    out[n, :, at] = value + wide(other[part * SIDE + n, :, at])
+
+                where = (passing, own)[part]
+                each_band(mover, SIDE, where, write)
+
+        shape = ((SIDE, BAND, self.total), jnp.float32)
+        return self.run(body, [shape, shape], [other], after)
+
+
+def pass_kernel(first, d0, pair, got, out):
+    for n in range(SIDE // 2):
+        out[n] = (pair[first + n] + wide(got[d0 + n])).astype(out.dtype)
+
+
+def passed(forth, pair, got, after=()):
+    _, band, total = pair.shape
+    return call(
+        functools.partial(pass_kernel, *((0, 2) if forth else (2, 0))),
+        [((SIDE // 2, band, total), jnp.bfloat16)],
+        [pair, got],
+        after=after,
+    )[0]
+
+
+def chip_kernel(pair, forth, back, forth_far, back_far, *refs):
+    score_refs, outs = refs[:SIDE], refs[SIDE:]
+    total = pair.shape[2]
+    for n in range(SIDE):
+        near = forth if n < 2 else back
+        far = back_far if n < 2 else forth_far
+        value = pair[n] + (wide(near[n]) + wide(far[n % 2]))
+        outs[n][:, :total] = value.astype(outs[n].dtype)
+    score = (score_refs[0][...] + score_refs[1][...]) + (score_refs[2][...] + score_refs[3][...])
+    high = wide(score.astype(jnp.bfloat16))
+    middle = wide((score - high).astype(jnp.bfloat16))
+    low = (score - high) - middle
+    line = lax.broadcasted_iota(jnp.int32, score.shape, 0)
+    three = jnp.where(line == 0, high, jnp.where(line == 1, middle, low))
+    three = jnp.where(line < 3, three, 0.0)
+    three = jnp.concatenate([three, jnp.zeros((BAND - PAD, LANES), jnp.float32)], 0)
+    for out in outs:
+        out[:, total:] = three.astype(out.dtype)
 
 
 def row_kernel(mine, a, b, c, *outs):
@@ -344,57 +381,54 @@
     right_sent[...] = value[:, EDGE:].astype(jnp.bfloat16)
 
 
-def image_kernel(scale, left, right, mine, a, b, c, out, score):
+def rounded(ref):
+    return wide(ref[...].astype(jnp.bfloat16))
+
+
+def right_blend(width, shift, own_right, next_left):
+    mine, after = rounded(own_right), rounded(next_left)
+    column = lax.broadcasted_iota(jnp.int32, mine.shape, 1)
+    aligned = pltpu.roll(after, lax.rem(STRIP - width - shift + EDGE, EDGE), 1)[:, :STRIP]
+    feather = (wide(STRIP - column) - 0.5) / wide(jnp.maximum(width, 1))
+    blend = feather * mine + (1.0 - feather) * aligned
+    return jnp.where(column >= STRIP - width, blend, mine)
+
+
+def left_blend(width, shift, own_left, prev_right):
+    mine = rounded(own_left)
+    rows = mine.shape[0]
+    before = jnp.concatenate([rounded(prev_right), jnp.zeros((rows, LAGS), jnp.float32)], 1)
+    before = pltpu.roll(before, lax.rem(shift + width - STRIP + EDGE, EDGE), 1)
+    column = lax.broadcasted_iota(jnp.int32, mine.shape, 1)
+    feather = (wide(width - column + shift) - 0.5) / wide(jnp.maximum(width, 1))
+    blend = feather * before + (1.0 - feather) * mine
+    return jnp.where((column >= shift) & (column < shift + width), blend, mine)
+
+
+def image_kernel(
+    scale, widths, shifts, own_left, own_right, next_left, prev_right, mine, a, b, c, out, score
+):
+    tile = lax.axis_index("tile")
+    earlier = jnp.maximum(tile - 1, 0)
     total = mine.shape[1] - LANES
-    out[:, :EDGE] = left[...]
     for begin in range(0, total, LANES):
         at = slice(begin, begin + LANES)
         value = mine[:, at] + ((wide(a[:, at]) + wide(b[:, at])) + wide(c[:, at]))
         out[:, EDGE + begin : EDGE + begin + LANES] = (value * scale).astype(jnp.bfloat16)
-    out[:, EDGE + total :] = right[...]
+    value = right_blend(widths[tile], shifts[tile], own_right, next_left)
+    out[:, EDGE + total :] = value.astype(jnp.bfloat16)
+    width, shift = jnp.where(tile > 0, widths[earlier], 0), jnp.where(tile > 0, shifts[earlier], 0)
+    out[:, :EDGE] = left_blend(width, shift, own_left, prev_right).astype(jnp.bfloat16)
     at = slice(total, total + LANES)
     value = mine[:PAD, at] + ((wide(a[:, at]) + wide(b[:, at])) + wide(c[:, at]))[:PAD]
     score[...] = jnp.sum(value, axis=0, keepdims=True)
 
 
-def seam_kernel(
-    widths, shifts, all_rows, own_left, own_right, next_left, prev_right, left_out, right_out, score_out
-):
-    tile = lax.axis_index("tile")
-    earlier = jnp.maximum(tile - 1, 0)
-    width_now, shift_now = widths[tile], shifts[tile]
-    width_left = jnp.where(tile > 0, widths[earlier], 0)
-    shift_left = jnp.where(tile > 0, shifts[earlier], 0)
-    rows = own_left.shape[0]
-
-    def rounded(ref):
-        return wide(ref[...].astype(jnp.bfloat16))
-
-    mine, after = rounded(own_right), rounded(next_left)
-    column = lax.broadcasted_iota(jnp.int32, (rows, STRIP), 1)
-    inside = column >= STRIP - width_now
-    aligned = pltpu.roll(after, lax.rem(STRIP - width_now - shift_now + EDGE, EDGE), 1)[:, :STRIP]
-    feather = ((STRIP - column).astype(jnp.float32) - 0.5) / jnp.maximum(width_now, 1).astype(
-        jnp.float32
-    )
-    right_out[...] = jnp.where(inside, feather * mine + (1.0 - feather) * aligned, mine).astype(
-        right_out.dtype
-    )
-    mine = rounded(own_left)
-    before = jnp.concatenate(
-        [prev_right[...].astype(jnp.float32), jnp.zeros((rows, LAGS), jnp.float32)], 1
-    )
-    before = pltpu.roll(before, lax.rem(shift_left + width_left - STRIP + EDGE, EDGE), 1)
-    place = lax.broadcasted_iota(jnp.int32, (rows, EDGE), 1)
-    within = (place >= shift_left) & (place < shift_left + width_left)
-    weight = ((width_left - place + shift_left).astype(jnp.float32) - 0.5) / jnp.maximum(
-        width_left, 1
-    ).astype(jnp.float32)
-    left_out[...] = jnp.where(within, weight * before + (1.0 - weight) * mine, mine).astype(
-        left_out.dtype
-    )
-    masked = jnp.where(inside, own_right[...], 0.0)
-    masked = pltpu.roll(masked, lax.rem(width_now, STRIP), 1)
+def score_kernel(all_rows, widths, own_right, next_left, score_out):
+    width = widths[lax.axis_index("tile")]
+    column = lax.broadcasted_iota(jnp.int32, own_right.shape, 1)
+    masked = jnp.where(column >= STRIP - width, own_right[...], 0.0)
+    masked = pltpu.roll(masked, lax.rem(width, STRIP), 1)
     after = next_left[...]
     mine_high, after_high = masked.astype(jnp.bfloat16), after.astype(jnp.bfloat16)
     mine_low = (masked - wide(mine_high)).astype(jnp.bfloat16)
@@ -414,7 +448,7 @@
         gram = jnp.where((line & step) != 0, pltpu.roll(gram, 2 * LANES - step, 1), gram)
         step *= 2
     total = jnp.sum(gram[:, :LANES], axis=0, keepdims=True)
-    terms = jnp.full((PAD, LANES), all_rows * jnp.maximum(width_now, 1), jnp.int32)
+    terms = jnp.full((PAD, LANES), all_rows * jnp.maximum(width, 1), jnp.int32)
     score_out[...] = jnp.broadcast_to(total, (PAD, LANES)) / jnp.sqrt(terms.astype(jnp.float32))
 
 
@@ -426,20 +460,21 @@
 
     low, high = EDGE + LANES, cols - STRIP - LANES
     places = [(0, 0, EDGE), (0, cols - STRIP, STRIP)]
-    frame, theirs_s = Columns(moves, rows, cols, [], places).loaded(
-        frame, [(0, low), (high, cols), (low, high)]
+    third = (cols - STRIP - EDGE) // 3 // LANES * LANES
+    cuts = [EDGE, EDGE + third, EDGE + 2 * third, cols - STRIP]
+    frame, theirs_s, theirs_m = Columns(moves, rows, cols, [], places).loaded(
+        frame, low, high, list(zip(cuts[:-1], cuts[1:]))
     )
     strips = Columns(moves, rows, cols, [frame], places)
     middle = Columns(moves, rows, cols, [frame], [(0, EDGE, cols - STRIP - EDGE)])
 
     other_s = to_other_core(theirs_s)
-    theirs_m = middle.theirs(2 * SIDE, both_ways, [theirs_s])
-    other_m = to_other_core(*gated([theirs_m], [other_s]))
-    pair_s = strips.every_pair(other_s, [theirs_m])
-    got_s = [ahead(pair_s[j], 1, j) for j in (1, 2, 3)]
-    theirs_l = middle.theirs(2 * SIDE, later, [pair_s[0]])
+    theirs_l = middle.theirs(2 * SIDE, later, [theirs_s])
+    other_m = to_other_core(*gated([theirs_m], [other_s, theirs_l]))
     other_l = to_other_core(theirs_l)
-    pair_m = middle.pairs(other_m, [theirs_l])
+    pair_s = strips.every_pair(other_s, [theirs_l])
+    got_s = direct(pair_s, 1)
+    pair_m = middle.pairs(other_m, [pair_s[0]])
     pair_f, pair_b = gated(pair_m, got_s)
     got_f, got_b = ahead(pair_f, 1, 1), ahead(pair_b, 1, -1)
 
@@ -453,25 +488,33 @@
     own_left, own_right, sent_right = call(
         functools.partial(edge_kernel, scale),
         [((BAND, EDGE), jnp.float32), ((BAND, STRIP), jnp.float32), ((BAND, STRIP), jnp.bfloat16)],
-        [row_s[0], *[ahead(row_s[j], 2, j) for j in (1, 2, 3)]],
+        [row_s[0], *direct(row_s, 2)],
     )
     next_left = from_behind(own_left, "tile", -1)
     prev_right = from_behind(sent_right, "tile", 1)
-    left_part, right_part, score = call(
-        lambda widths, shifts, *refs: seam_kernel(widths, shifts, rows, *refs),
-        [((BAND, EDGE), jnp.bfloat16), ((BAND, STRIP), jnp.bfloat16), ((PAD, LANES), jnp.float32)],
-        [own_left, own_right, next_left, prev_right],
-        [intersection, seam_shift],
-    )
-    far_f = ahead(middle.passed(True, other_l, got_f, [score]), 1, 1)
-    far_b = ahead(middle.passed(False, other_l, got_b, [score]), 1, -1)
+    passing_m, own_m = middle.later_pairs(other_l, [own_left])
+    (score,) = call(
+        functools.partial(score_kernel, rows),
+        [((PAD, LANES), jnp.float32)],
+        [own_right, next_left],
+        [intersection],
+        after=[passing_m],
+    )
+
+    far_f = ahead(passed(True, passing_m, got_f, [score]), 1, 1)
+    far_b = ahead(passed(False, passing_m, got_b, [score]), 1, -1)
     score = score + to_other_core(score)
-    scores = [score, *[ahead(score, 1, j) for j in (1, 2, 3)]]
-    row_m = middle.rows_of_chip(other_l, got_f, got_b, far_f, far_b, scores)
+    wider = (BAND, middle.total + LANES)
+    row_m = call(
+        chip_kernel,
+        [(wider, jnp.float32)] + [(wider, jnp.bfloat16)] * (SIDE - 1),
+        [own_m, got_f, got_b, far_f, far_b, *[score], *direct([score] * SIDE, 1)],
+    )
     image, score = call(
         functools.partial(image_kernel, scale),
         [((BAND, cols), jnp.bfloat16), ((1, LAGS), jnp.float32)],
-        [left_part, right_part, row_m[0], *[ahead(row_m[j], 2, j) for j in (1, 2, 3)]],
+        [own_left, own_right, next_left, prev_right, row_m[0], *direct(row_m, 2)],
+        [intersection, seam_shift],
     )
     return (image[None], score)
 

time: 79 us -> 72.7 us (0.920)
  waiting for transfers between devices: 27 us -> 23.2 us
  Pallas kernels: 19.8 us -> 18.5 us
    ppermute x20, waiting for transfers between devices: 25.4 us -> 18.3 us  [permuted(): lax.ppermute(array, 'frame', [(device_at(*place), device_at(*target(*plac...]
    ppermute x2, waiting for transfers between devices: 1.58 us -> 4.94 us  [from_behind(): return lax.ppermute(array, axis, pairs)]
    pallas_call x11, Pallas kernels: 14.8 us -> 13.1 us  [call(): pl.pallas_call(run, in_specs=[pl.BlockSpec(memory_space=pltpu.SMEM)] * le...]
    ppermute x2, starting transfers between devices: 7.05 us -> 5.82 us  [from_behind(): return lax.ppermute(array, axis, pairs)]
  transfers between devices with their start and end apart: 22 -> 22, of which waited for: 15 -> 13; matrix products, arithmetic and copies ran while one was open for 0% -> 0% of each run, Pallas kernels for 13% -> 15%
where the time goes in v3:
time: 72.7 us; the launch traced here: 72.6 us
  starting transfers between devices  29.5 us (41%)
  waiting for transfers between devices  23.2 us (32%)
  Pallas kernels  18.5 us (25%)
  between operations  0.75 us (1%)
    ppermute x20, starting transfers between devices, permuted(): lax.ppermute(array, 'frame', [(device_at(*place), device_at(*target(*plac...  23.7 us
    ppermute x20, waiting for transfers between devices, permuted(): lax.ppermute(array, 'frame', [(device_at(*place), device_at(*target(*plac...  18.3 us
    pallas_call x11, Pallas kernels, call(): pl.pallas_call(run, in_specs=[pl.BlockSpec(memory_space=pltpu.SMEM)] * le...  13.1 us
    ppermute x2, starting transfers between devices, from_behind(): return lax.ppermute(array, axis, pairs)  5.82 us
    pallas_call x1, Pallas kernels, loaded(): pl.pallas_call(kernel, in_specs=[far, far], out_specs=[vmem, vmem, vmem],...  5.4 us
    ppermute x2, waiting for transfers between devices, from_behind(): return lax.ppermute(array, axis, pairs)  4.94 us
  transfers between devices with their start and end apart: 22, of which 13 were waited for; matrix products, arithmetic and copies ran while one was open for 0% of the time, Pallas kernels for 15%

profile of v3, /device:TPU:102, one launch (start us, length us, event | category | flops | bytes accessed | tf_op | source)
XLA Modules:
  0.0 72.6 jit_solution(15428436273774408858)
XLA Ops:
  1.3 5.4 %shard_map.59 = (bf16[1024,5760]{1,0:T(8,128)(2,1)S(1)}, bf16[16,32,1152]{2,1,0:T(8,128)(2,1)S(1)}, bf16[8,32,4608]{2,1,0:T(8,128)(2,1)S(1)}) custom-call(s32[2]{0:T(128)S(1)} %bitcast.3, bf16[1024,5760]{1,0:T(8,128)(2,1)} %bitcast.8), custom_call_target="tpu_custom_call" | custom-call | flops 1024 | bytes 1024 | tf_op jit(solution)/shard_map/pallas_call | solution.py:271
  6.8 1.9 %shard_map.60.refs_3_.refs_2_ = bf16[8,32,4608]{2,1,0:T(8,128)(2,1)S(1)} custom-call(s32[2]{0:T(128)S(1)} %bitcast.4, bf16[1024,5760]{1,0:T(8,128)(2,1)S(1)} %get-tuple-element.28.refs_1_, bf16[16,32,1152]{2,1,0:T(8,128)(2,1)S(1)} %get-tuple-element.29.refs_2_), custom_call_target="tpu_custom_call" | custom-call | flops 1024 | bytes 1024 | tf_op jit(solution)/shard_map/pallas_call | solution.py:70
  10.1 2.1 %shard_map.61 = (f32[4,32,1152]{2,1,0:T(8,128)S(1)}, bf16[4,32,1152]{2,1,0:T(8,128)(2,1)S(1)}, bf16[4,32,1152]{2,1,0:T(8,128)(2,1)S(1)}, bf16[4,32,1152]{2,1,0:T(8,128)(2,1)S(1)}) custom-call(s32[2]{0:T(128)S(1)} %bitcast.5, bf16[1024,5760]{1,0:T(8,128)(2,1)S(1)} %get-tuple-element.28.refs_1_, ...), custom_call_target="tpu_custom_call" | custom-call | flops 1024 | bytes 1024 | tf_op jit(solution)/shard_map/pallas_call | solution.py:70
  12.2 1.5 %collective-permute-start.1 = (bf16[4,32,1152]{2,1,0:T(8,128)(2,1)S(1)}, bf16[4,32,1152]{2,1,0:T(8,128)(2,1)S(1)}, u32[]{:S(2)}, u32[]{:S(2)}) collective-permute-start(bf16[4,32,1152]{2,1,0:T(8,128)(2,1)S(1)} %get-tuple-element.31), channel_id=1, source_target_pairs={{0,4},{1,17},{2,6},{3,19},{4,0},{5,21},{6,2},{7,23},{8,12},{9,25},... | collective-permute-start | bytes 884744 | tf_op jit(solution)/shard_map/ppermute | solution.py:30
  13.7 2.1 %collective-permute-start.2 = (bf16[4,32,1152]{2,1,0:T(8,128)(2,1)S(1)}, bf16[4,32,1152]{2,1,0:T(8,128)(2,1)S(1)}, u32[]{:S(2)}, u32[]{:S(2)}) collective-permute-start(bf16[4,32,1152]{2,1,0:T(8,128)(2,1)S(1)} %get-tuple-element.32), channel_id=1, source_target_pairs={{0,2},{1,9},{2,4},{3,11},{4,6},{5,13},{6,0},{7,15},{8,10},{9,17},{... | collective-permute-start | bytes 884744 | tf_op jit(solution)/shard_map/ppermute | solution.py:30
  15.8 2.6 %shard_map.63 = (bf16[4,32,4608]{2,1,0:T(8,128)(2,1)S(1)}, bf16[4,32,4608]{2,1,0:T(8,128)(2,1)S(1)}) custom-call(s32[2]{0:T(128)S(1)} %bitcast.6, bf16[1024,5760]{1,0:T(8,128)(2,1)S(1)} %get-tuple-element.28.refs_1_, bf16[8,32,4608]{2,1,0:T(8,128)(2,1)S(1)} %collective-permute-done.4.refs_2_, f32[4,32,1152]{2,1,0:T(8,128)S(1)} %get-tuple-element.30.refs_3_.refs_0_), custom_call_target="tpu_custom_call" | custom-call | flops 1024 | bytes 1024 | tf_op jit(solution)/shard_map/pallas_call | solution.py:70
  18.4 2.2 %collective-permute-done.1.refs_2_.refs_1_ = bf16[4,32,1152]{2,1,0:T(8,128)(2,1)S(1)} collective-permute-done((bf16[4,32,1152]{2,1,0:T(8,128)(2,1)S(1)}, bf16[4,32,1152]{2,1,0:T(8,128)(2,1)S(1)}, u32[]{:S(2)}, u32[]{:S(2)}) %collective-permute-start.1) | collective-permute-done | bytes 294944 | tf_op jit(solution)/shard_map/ppermute | solution.py:30
  21.5 2.3 %collective-permute-done.3.refs_4_.refs_3_ = bf16[4,32,1152]{2,1,0:T(8,128)(2,1)S(1)} collective-permute-done((bf16[4,32,1152]{2,1,0:T(8,128)(2,1)S(1)}, bf16[4,32,1152]{2,1,0:T(8,128)(2,1)S(1)}, u32[]{:S(2)}, u32[]{:S(2)}) %collective-permute-start.3) | collective-permute-done | bytes 294944 | tf_op jit(solution)/shard_map/ppermute | solution.py:30
  24.3 1.5 %collective-permute-start.12 = (bf16[4,32,4608]{2,1,0:T(8,128)(2,1)S(1)}, bf16[4,32,4608]{2,1,0:T(8,128)(2,1)S(1)}, u32[]{:S(2)}, u32[]{:S(2)}) collective-permute-start(bf16[4,32,4608]{2,1,0:T(8,128)(2,1)S(1)} %get-tuple-element.46), channel_id=1, source_target_pairs={{0,6},{1,25},{2,0},{3,27},{4,2},{5,29},{6,4},{7,31},{8,14},{9,1},{... | collective-permute-start | bytes 3538952 | tf_op jit(solution)/shard_map/ppermute | solution.py:30
  25.9 3.3 %collective-permute-start.6 = (bf16[32,1152]{1,0:T(8,128)(2,1)S(1)}, bf16[32,1152]{1,0:T(8,128)(2,1)S(1)}, u32[]{:S(2)}, u32[]{:S(2)}) collective-permute-start(bf16[32,1152]{1,0:T(8,128)(2,1)S(1)} %get-tuple-element.39), channel_id=1, source_target_pairs={{0,16},{1,5},{2,18},{3,7},{4,20},{5,1},{6,22},{7,3},{8,24},{9,13},... | collective-permute-start | bytes 221192 | tf_op jit(solution)/shard_map/ppermute | solution.py:30
  29.9 2.5 %collective-permute-start.8 = (bf16[32,1152]{1,0:T(8,128)(2,1)S(1)}, bf16[32,1152]{1,0:T(8,128)(2,1)S(1)}, u32[]{:S(2)}, u32[]{:S(2)}) collective-permute-start(bf16[32,1152]{1,0:T(8,128)(2,1)S(1)} %get-tuple-element.41), channel_id=1, source_target_pairs={{0,24},{1,7},{2,26},{3,1},{4,28},{5,3},{6,30},{7,5},{8,0},{9,15},{... | collective-permute-start | bytes 221192 | tf_op jit(solution)/shard_map/ppermute | solution.py:30
  32.7 2.9 %collective-permute-done.7.refs_2_ = bf16[32,1152]{1,0:T(8,128)(2,1)S(1)} collective-permute-done((bf16[32,1152]{1,0:T(8,128)(2,1)S(1)}, bf16[32,1152]{1,0:T(8,128)(2,1)S(1)}, u32[]{:S(2)}, u32[]{:S(2)}) %collective-permute-start.7) | collective-permute-done | bytes 73760 | tf_op jit(solution)/shard_map/ppermute | solution.py:30
  35.7 2.0 %collective-permute-start.9 = (f32[32,640]{1,0:T(8,128)S(1)}, f32[32,640]{1,0:T(8,128)S(1)}, u32[]{:S(2)}, u32[]{:S(2)}) collective-permute-start(f32[32,640]{1,0:T(8,128)S(1)} %get-tuple-element.42.refs_3_.refs_2_), channel_id=1, source_target_pairs={{32,0},{64,32},{96,64},{128,96},{160,128},{192,160},{224,192},{33,... | collective-permute-start | bytes 245768 | tf_op jit(solution)/shard_map/ppermute | solution.py:55
  37.7 2.6 %shard_map.67 = (f32[4,32,4608]{2,1,0:T(8,128)S(1)}, f32[4,32,4608]{2,1,0:T(8,128)S(1)}) custom-call(s32[2]{0:T(128)S(1)} %bitcast.7, bf16[1024,5760]{1,0:T(8,128)(2,1)S(1)} %get-tuple-element.28.refs_1_, bf16[8,32,4608]{2,1,0:T(8,128)(2,1)S(1)} %collective-permute-done.5.refs_5_.refs_2_, f32[32,640]{1,0:T(8,128)S(1)} %get-tuple-element.42.refs_3_.refs_2_), custom_call_target="tpu_custom_call" | custom-call | flops 1024 | bytes 1024 | tf_op jit(solution)/shard_map/pallas_call | solution.py:70
  40.3 3.0 %collective-permute-done.9.refs_2_.refs_4_ = f32[32,640]{1,0:T(8,128)S(1)} collective-permute-done((f32[32,640]{1,0:T(8,128)S(1)}, f32[32,640]{1,0:T(8,128)S(1)}, u32[]{:S(2)}, u32[]{:S(2)}) %collective-permute-start.9) | collective-permute-done | bytes 81952 | tf_op jit(solution)/shard_map/ppermute | solution.py:55
  43.2 1.5 %shard_map.68.refs_2_ = f32[8,128]{1,0:T(8,128)S(1)} custom-call(s32[8]{0:T(128)S(1)} %copy-done.1, f32[32,512]{1,0:T(8,128)S(1)} %get-tuple-element.43.refs_1_.refs_3_, f32[32,640]{1,0:T(8,128)S(1)} %collective-permute-done.9.refs_2_.refs_4_, f32[4,32,4608]{2,1,0:T(8,128)S(1)} %get-tuple-element.47.refs_3_.refs_0_), custom_call_target="tpu_custom_call" | custom-call | flops 1024 | bytes 1024 | tf_op jit(solution)/shard_map/pallas_call | solution.py:70
  44.9 2.0 %collective-permute-start.13 = (bf16[2,32,4608]{2,1,0:T(8,128)(2,1)S(1)}, bf16[2,32,4608]{2,1,0:T(8,128)(2,1)S(1)}, u32[]{:S(2)}, u32[]{:S(2)}) collective-permute-start(bf16[2,32,4608]{2,1,0:T(8,128)(2,1)S(1)} %shard_map.69), channel_id=1, source_target_pairs={{0,2},{1,9},{2,4},{3,11},{4,6},{5,13},{6,0},{7,15},{8,10},{9,17},{... | collective-permute-start | bytes 1769480 | tf_op jit(solution)/shard_map/ppermute | solution.py:30
  50.1 1.5 %collective-permute-start.17 = (f32[8,128]{1,0:T(8,128)S(1)}, f32[8,128]{1,0:T(8,128)S(1)}, u32[]{:S(2)}, u32[]{:S(2)}) collective-permute-start(f32[8,128]{1,0:T(8,128)S(1)} %add.3.refs_5_), channel_id=1, source_target_pairs={{0,2},{1,9},{2,4},{3,11},{4,6},{5,13},{6,0},{7,15},{8,10},{9,17},{... | collective-permute-start | bytes 12296 | tf_op jit(solution)/shard_map/ppermute | solution.py:30
  52.4 4.5 %collective-permute-done.16.refs_6_ = f32[8,128]{1,0:T(8,128)S(1)} collective-permute-done((f32[8,128]{1,0:T(8,128)S(1)}, f32[8,128]{1,0:T(8,128)S(1)}, u32[]{:S(2)}, u32[]{:S(2)}) %collective-permute-start.16) | collective-permute-done | bytes 4128 | tf_op jit(solution)/shard_map/ppermute | solution.py:30
  58.8 1.5 %collective-permute-start.19 = (bf16[32,4736]{1,0:T(8,128)(2,1)S(1)}, bf16[32,4736]{1,0:T(8,128)(2,1)S(1)}, u32[]{:S(2)}, u32[]{:S(2)}) collective-permute-start(bf16[32,4736]{1,0:T(8,128)(2,1)S(1)} %get-tuple-element.49), channel_id=1, source_target_pairs={{0,16},{1,5},{2,18},{3,7},{4,20},{5,1},{6,22},{7,3},{8,24},{9,13},... | collective-permute-start | bytes 909320 | tf_op jit(solution)/shard_map/ppermute | solution.py:30
  60.3 2.6 %collective-permute-start.20 = (bf16[32,4736]{1,0:T(8,128)(2,1)S(1)}, bf16[32,4736]{1,0:T(8,128)(2,1)S(1)}, u32[]{:S(2)}, u32[]{:S(2)}) collective-permute-start(bf16[32,4736]{1,0:T(8,128)(2,1)S(1)} %get-tuple-element.50), channel_id=1, source_target_pairs={{0,8},{1,3},{2,10},{3,5},{4,12},{5,7},{6,14},{7,1},{8,16},{9,11},{... | collective-permute-start | bytes 909320 | tf_op jit(solution)/shard_map/ppermute | solution.py:30
  63.5 3.8 %collective-permute-start.10 = (bf16[32,512]{1,0:T(8,128)(2,1)S(1)}, bf16[32,512]{1,0:T(8,128)(2,1)S(1)}, u32[]{:S(2)}, u32[]{:S(2)}) collective-permute-start(bf16[32,512]{1,0:T(8,128)(2,1)S(1)} %get-tuple-element.44), channel_id=1, source_target_pairs={{0,32},{32,64},{64,96},{96,128},{128,160},{160,192},{192,224},{1,3... | collective-permute-start | bytes 98312 | tf_op jit(solution)/shard_map/ppermute | solution.py:55
  67.4 2.0 %collective-permute-done.10.refs_5_ = bf16[32,512]{1,0:T(8,128)(2,1)S(1)} collective-permute-done((bf16[32,512]{1,0:T(8,128)(2,1)S(1)}, bf16[32,512]{1,0:T(8,128)(2,1)S(1)}, u32[]{:S(2)}, u32[]{:S(2)}) %collective-permute-start.10) | collective-permute-done | bytes 32800 | tf_op jit(solution)/shard_map/ppermute | solution.py:55
  71.0 1.6 %shard_map.72 = (bf16[32,5760]{1,0:T(8,128)(2,1)}, f32[1,128]{1,0:T(1,128)}) custom-call(s32[8]{0:T(128)S(1)} %copy-done.1, s32[8]{0:T(128)S(1)} %copy-done.2, f32[32,640]{1,0:T(8,128)S(1)} %get-tuple-element.42.refs_3_.refs_2_, f32[32,512]{1,0:T(8,128)S(1)} %get-tuple-element.43.refs_1_.refs_3_, f32[32,640]{1,0:T(8,128)S(1)} %collective-permute-done.9.refs_2_.refs_4_, ...), custom_call_target="tpu_custom_call" | custom-call | flops 1024 | bytes 1024 | tf_op jit(solution)/shard_map/pallas_call | solution.py:70
  (41 shorter events, 13.2 us)
Async XLA Ops:
  6.7 2.9 %collective-permute-start = (bf16[16,32,1152]{2,1,0:T(8,128)(2,1)S(1)}, bf16[16,32,1152]{2,1,0:T(8,128)(2,1)S(1)}, u32[]{:S(2)}, u32[]{:S(2)}) collective-permute-start(bf16[16,32,1152]{2,1,0:T(8,128)(2,1)S(1)} %get-tuple-element.29.refs_2_), channel_id=1, source_target_pairs={{0,1},{1,0},{2,3},{3,2},{4,5},{5,4},{6,7},{7,6},{8,9},{9,8},{10,11... | collective-permute-start | bytes 3538952 | tf_op jit(solution)/shard_map/ppermute | solution.py:30
  9.6 6.2 %collective-permute-start.4 = (bf16[8,32,4608]{2,1,0:T(8,128)(2,1)S(1)}, bf16[8,32,4608]{2,1,0:T(8,128)(2,1)S(1)}, u32[]{:S(2)}, u32[]{:S(2)}) collective-permute-start(bf16[8,32,4608]{2,1,0:T(8,128)(2,1)S(1)} %shard_map.62), channel_id=1, source_target_pairs={{0,1},{1,0},{2,3},{3,2},{4,5},{5,4},{6,7},{7,6},{8,9},{9,8},{10,11... | collective-permute-start | bytes 7077896 | tf_op jit(solution)/shard_map/ppermute | solution.py:30
  9.8 16.0 %collective-permute-start.5 = (bf16[8,32,4608]{2,1,0:T(8,128)(2,1)S(1)}, bf16[8,32,4608]{2,1,0:T(8,128)(2,1)S(1)}, u32[]{:S(2)}, u32[]{:S(2)}) collective-permute-start(bf16[8,32,4608]{2,1,0:T(8,128)(2,1)S(1)} %shard_map.60.refs_3_.refs_2_), channel_id=1, source_target_pairs={{0,1},{1,0},{2,3},{3,2},{4,5},{5,4},{6,7},{7,6},{8,9},{9,8},{10,11... | collective-permute-start | bytes 7077896 | tf_op jit(solution)/shard_map/ppermute | solution.py:30
  12.2 8.3 %collective-permute-start.1 = (bf16[4,32,1152]{2,1,0:T(8,128)(2,1)S(1)}, bf16[4,32,1152]{2,1,0:T(8,128)(2,1)S(1)}, u32[]{:S(2)}, u32[]{:S(2)}) collective-permute-start(bf16[4,32,1152]{2,1,0:T(8,128)(2,1)S(1)} %get-tuple-element.31), channel_id=1, source_target_pairs={{0,4},{1,17},{2,6},{3,19},{4,0},{5,21},{6,2},{7,23},{8,12},{9,25},... | collective-permute-start | bytes 884744 | tf_op jit(solution)/shard_map/ppermute | solution.py:30
  13.7 7.8 %collective-permute-start.2 = (bf16[4,32,1152]{2,1,0:T(8,128)(2,1)S(1)}, bf16[4,32,1152]{2,1,0:T(8,128)(2,1)S(1)}, u32[]{:S(2)}, u32[]{:S(2)}) collective-permute-start(bf16[4,32,1152]{2,1,0:T(8,128)(2,1)S(1)} %get-tuple-element.32), channel_id=1, source_target_pairs={{0,2},{1,9},{2,4},{3,11},{4,6},{5,13},{6,0},{7,15},{8,10},{9,17},{... | collective-permute-start | bytes 884744 | tf_op jit(solution)/shard_map/ppermute | solution.py:30
  15.8 7.9 %collective-permute-start.3 = (bf16[4,32,1152]{2,1,0:T(8,128)(2,1)S(1)}, bf16[4,32,1152]{2,1,0:T(8,128)(2,1)S(1)}, u32[]{:S(2)}, u32[]{:S(2)}) collective-permute-start(bf16[4,32,1152]{2,1,0:T(8,128)(2,1)S(1)} %get-tuple-element.33), channel_id=1, source_target_pairs={{0,6},{1,25},{2,0},{3,27},{4,2},{5,29},{6,4},{7,31},{8,14},{9,1},{... | collective-permute-start | bytes 884744 | tf_op jit(solution)/shard_map/ppermute | solution.py:30
  23.8 21.0 %collective-permute-start.11 = (bf16[4,32,4608]{2,1,0:T(8,128)(2,1)S(1)}, bf16[4,32,4608]{2,1,0:T(8,128)(2,1)S(1)}, u32[]{:S(2)}, u32[]{:S(2)}) collective-permute-start(bf16[4,32,4608]{2,1,0:T(8,128)(2,1)S(1)} %get-tuple-element.37.refs_4_), channel_id=1, source_target_pairs={{0,2},{1,9},{2,4},{3,11},{4,6},{5,13},{6,0},{7,15},{8,10},{9,17},{... | collective-permute-start | bytes 3538952 | tf_op jit(solution)/shard_map/ppermute | solution.py:30
  24.3 22.6 %collective-permute-start.12 = (bf16[4,32,4608]{2,1,0:T(8,128)(2,1)S(1)}, bf16[4,32,4608]{2,1,0:T(8,128)(2,1)S(1)}, u32[]{:S(2)}, u32[]{:S(2)}) collective-permute-start(bf16[4,32,4608]{2,1,0:T(8,128)(2,1)S(1)} %get-tuple-element.46), channel_id=1, source_target_pairs={{0,6},{1,25},{2,0},{3,27},{4,2},{5,29},{6,4},{7,31},{8,14},{9,1},{... | collective-permute-start | bytes 3538952 | tf_op jit(solution)/shard_map/ppermute | solution.py:30
  25.9 6.8 %collective-permute-start.6 = (bf16[32,1152]{1,0:T(8,128)(2,1)S(1)}, bf16[32,1152]{1,0:T(8,128)(2,1)S(1)}, u32[]{:S(2)}, u32[]{:S(2)}) collective-permute-start(bf16[32,1152]{1,0:T(8,128)(2,1)S(1)} %get-tuple-element.39), channel_id=1, source_target_pairs={{0,16},{1,5},{2,18},{3,7},{4,20},{5,1},{6,22},{7,3},{8,24},{9,13},... | collective-permute-start | bytes 221192 | tf_op jit(solution)/shard_map/ppermute | solution.py:30
  29.2 6.4 %collective-permute-start.7 = (bf16[32,1152]{1,0:T(8,128)(2,1)S(1)}, bf16[32,1152]{1,0:T(8,128)(2,1)S(1)}, u32[]{:S(2)}, u32[]{:S(2)}) collective-permute-start(bf16[32,1152]{1,0:T(8,128)(2,1)S(1)} %get-tuple-element.40), channel_id=1, source_target_pairs={{0,8},{1,3},{2,10},{3,5},{4,12},{5,7},{6,14},{7,1},{8,16},{9,11},{... | collective-permute-start | bytes 221192 | tf_op jit(solution)/shard_map/ppermute | solution.py:30
  29.9 5.7 %collective-permute-start.8 = (bf16[32,1152]{1,0:T(8,128)(2,1)S(1)}, bf16[32,1152]{1,0:T(8,128)(2,1)S(1)}, u32[]{:S(2)}, u32[]{:S(2)}) collective-permute-start(bf16[32,1152]{1,0:T(8,128)(2,1)S(1)} %get-tuple-element.41), channel_id=1, source_target_pairs={{0,24},{1,7},{2,26},{3,1},{4,28},{5,3},{6,30},{7,5},{8,0},{9,15},{... | collective-permute-start | bytes 221192 | tf_op jit(solution)/shard_map/ppermute | solution.py:30
  35.7 7.6 %copy-start.1 = (s32[8]{0:T(128)S(1)}, s32[8]{0:T(128)}, u32[]{:S(2)}) copy-start(s32[8]{0:T(128)} %refs_0_.3) | copy-start | bytes 100
  35.7 7.5 %collective-permute-start.9 = (f32[32,640]{1,0:T(8,128)S(1)}, f32[32,640]{1,0:T(8,128)S(1)}, u32[]{:S(2)}, u32[]{:S(2)}) collective-permute-start(f32[32,640]{1,0:T(8,128)S(1)} %get-tuple-element.42.refs_3_.refs_2_), channel_id=1, source_target_pairs={{32,0},{64,32},{96,64},{128,96},{160,128},{192,160},{224,192},{33,... | collective-permute-start | bytes 245768 | tf_op jit(solution)/shard_map/ppermute | solution.py:55
  44.9 13.4 %collective-permute-start.13 = (bf16[2,32,4608]{2,1,0:T(8,128)(2,1)S(1)}, bf16[2,32,4608]{2,1,0:T(8,128)(2,1)S(1)}, u32[]{:S(2)}, u32[]{:S(2)}) collective-permute-start(bf16[2,32,4608]{2,1,0:T(8,128)(2,1)S(1)} %shard_map.69), channel_id=1, source_target_pairs={{0,2},{1,9},{2,4},{3,11},{4,6},{5,13},{6,0},{7,15},{8,10},{9,17},{... | collective-permute-start | bytes 1769480 | tf_op jit(solution)/shard_map/ppermute | solution.py:30
  47.1 11.3 %collective-permute-start.14 = (bf16[2,32,4608]{2,1,0:T(8,128)(2,1)S(1)}, bf16[2,32,4608]{2,1,0:T(8,128)(2,1)S(1)}, u32[]{:S(2)}, u32[]{:S(2)}) collective-permute-start(bf16[2,32,4608]{2,1,0:T(8,128)(2,1)S(1)} %shard_map.70), channel_id=1, source_target_pairs={{0,6},{1,25},{2,0},{3,27},{4,2},{5,29},{6,4},{7,31},{8,14},{9,1},{... | collective-permute-start | bytes 1769480 | tf_op jit(solution)/shard_map/ppermute | solution.py:30
  47.5 1.2 %collective-permute-start.15 = (f32[8,128]{1,0:T(8,128)S(1)}, f32[8,128]{1,0:T(8,128)S(1)}, u32[]{:S(2)}, u32[]{:S(2)}) collective-permute-start(f32[8,128]{1,0:T(8,128)S(1)} %shard_map.68.refs_2_), channel_id=1, source_target_pairs={{0,1},{1,0},{2,3},{3,2},{4,5},{5,4},{6,7},{7,6},{8,9},{9,8},{10,11... | collective-permute-start | bytes 12296 | tf_op jit(solution)/shard_map/ppermute | solution.py:30
  48.6 8.3 %collective-permute-start.16 = (f32[8,128]{1,0:T(8,128)S(1)}, f32[8,128]{1,0:T(8,128)S(1)}, u32[]{:S(2)}, u32[]{:S(2)}) collective-permute-start(f32[8,128]{1,0:T(8,128)S(1)} %add.3.refs_5_), channel_id=1, source_target_pairs={{0,4},{1,17},{2,6},{3,19},{4,0},{5,21},{6,2},{7,23},{8,12},{9,25},... | collective-permute-start | bytes 12296 | tf_op jit(solution)/shard_map/ppermute | solution.py:30
  50.1 6.8 %collective-permute-start.17 = (f32[8,128]{1,0:T(8,128)S(1)}, f32[8,128]{1,0:T(8,128)S(1)}, u32[]{:S(2)}, u32[]{:S(2)}) collective-permute-start(f32[8,128]{1,0:T(8,128)S(1)} %add.3.refs_5_), channel_id=1, source_target_pairs={{0,2},{1,9},{2,4},{3,11},{4,6},{5,13},{6,0},{7,15},{8,10},{9,17},{... | collective-permute-start | bytes 12296 | tf_op jit(solution)/shard_map/ppermute | solution.py:30
  51.6 6.8 %collective-permute-start.18 = (f32[8,128]{1,0:T(8,128)S(1)}, f32[8,128]{1,0:T(8,128)S(1)}, u32[]{:S(2)}, u32[]{:S(2)}) collective-permute-start(f32[8,128]{1,0:T(8,128)S(1)} %add.3.refs_5_), channel_id=1, source_target_pairs={{0,6},{1,25},{2,0},{3,27},{4,2},{5,29},{6,4},{7,31},{8,14},{9,1},{... | collective-permute-start | bytes 12296 | tf_op jit(solution)/shard_map/ppermute | solution.py:30
  58.3 12.7 %copy-start.2 = (s32[8]{0:T(128)S(1)}, s32[8]{0:T(128)}, u32[]{:S(2)}) copy-start(s32[8]{0:T(128)} %refs_1_.1) | copy-start | bytes 100
  58.8 10.6 %collective-permute-start.19 = (bf16[32,4736]{1,0:T(8,128)(2,1)S(1)}, bf16[32,4736]{1,0:T(8,128)(2,1)S(1)}, u32[]{:S(2)}, u32[]{:S(2)}) collective-permute-start(bf16[32,4736]{1,0:T(8,128)(2,1)S(1)} %get-tuple-element.49), channel_id=1, source_target_pairs={{0,16},{1,5},{2,18},{3,7},{4,20},{5,1},{6,22},{7,3},{8,24},{9,13},... | collective-permute-start | bytes 909320 | tf_op jit(solution)/shard_map/ppermute | solution.py:30
  60.3 10.1 %collective-permute-start.20 = (bf16[32,4736]{1,0:T(8,128)(2,1)S(1)}, bf16[32,4736]{1,0:T(8,128)(2,1)S(1)}, u32[]{:S(2)}, u32[]{:S(2)}) collective-permute-start(bf16[32,4736]{1,0:T(8,128)(2,1)S(1)} %get-tuple-element.50), channel_id=1, source_target_pairs={{0,8},{1,3},{2,10},{3,5},{4,12},{5,7},{6,14},{7,1},{8,16},{9,11},{... | collective-permute-start | bytes 909320 | tf_op jit(solution)/shard_map/ppermute | solution.py:30
  62.9 8.1 %collective-permute-start.21 = (bf16[32,4736]{1,0:T(8,128)(2,1)S(1)}, bf16[32,4736]{1,0:T(8,128)(2,1)S(1)}, u32[]{:S(2)}, u32[]{:S(2)}) collective-permute-start(bf16[32,4736]{1,0:T(8,128)(2,1)S(1)} %get-tuple-element.51), channel_id=1, source_target_pairs={{0,24},{1,7},{2,26},{3,1},{4,28},{5,3},{6,30},{7,5},{8,0},{9,15},{... | collective-permute-start | bytes 909320 | tf_op jit(solution)/shard_map/ppermute | solution.py:30
  63.5 5.8 %collective-permute-start.10 = (bf16[32,512]{1,0:T(8,128)(2,1)S(1)}, bf16[32,512]{1,0:T(8,128)(2,1)S(1)}, u32[]{:S(2)}, u32[]{:S(2)}) collective-permute-start(bf16[32,512]{1,0:T(8,128)(2,1)S(1)} %get-tuple-element.44), channel_id=1, source_target_pairs={{0,32},{32,64},{64,96},{96,128},{128,160},{160,192},{192,224},{1,3... | collective-permute-start | bytes 98312 | tf_op jit(solution)/shard_map/ppermute | solution.py:55
  (1 other events, 0.7 us)

commit v4 on v3

--- a/solution.py
+++ b/solution.py
@@ -107,7 +107,7 @@
         for source, origin, first, width in pieces:
             begin, end = max(first - LANES, 0), min(first + width + LANES, cols)
             blank = jnp.zeros(held.shape[2:], held.dtype)
-            for slot in range(2):
+            for slot in range(held.shape[0]):
                 if begin == first:
                     held[slot, base] = blank
                 if end == first + width:
@@ -147,14 +147,16 @@
 
 def held_for(widths):
     tiles = sum(width // LANES + 2 for width in widths)
-    return pltpu.VMEM((2, tiles, BAND + 2 * PAD, LANES), jnp.float32)
+    return pltpu.VMEM((2 if tiles > 16 else SIDE, tiles, BAND + 2 * PAD, LANES), jnp.float32)
 
 
 def each_band(mover, count, where, write):
-    @pl.loop(0, count // 2)
-    def _(pair):
-        for slot in range(2):
-            n = 2 * pair + slot
+    slots = mover.held.shape[0]
+
+    @pl.loop(0, count // slots)
+    def _(turn):
+        for slot in range(slots):
+            n = slots * turn + slot
             j, d = where(n)
             mover.band(slot, j, d, functools.partial(write, n))
 
@@ -332,19 +334,11 @@
         return self.run(body, [shape, shape], [other], after)
 
 
-def pass_kernel(first, d0, pair, got, out):
-    for n in range(SIDE // 2):
-        out[n] = (pair[first + n] + wide(got[d0 + n])).astype(out.dtype)
-
-
-def passed(forth, pair, got, after=()):
-    _, band, total = pair.shape
-    return call(
-        functools.partial(pass_kernel, *((0, 2) if forth else (2, 0))),
-        [((SIDE // 2, band, total), jnp.bfloat16)],
-        [pair, got],
-        after=after,
-    )[0]
+def pass_kernel(pair, forth, back, out_forth, out_back):
+    half = SIDE // 2
+    for n in range(half):
+        out_forth[n] = (pair[n] + wide(forth[half + n])).astype(out_forth.dtype)
+        out_back[n] = (pair[half + n] + wide(back[n])).astype(out_back.dtype)
 
 
 def chip_kernel(pair, forth, back, forth_far, back_far, *refs):
@@ -405,20 +399,23 @@
     return jnp.where((column >= shift) & (column < shift + width), blend, mine)
 
 
-def image_kernel(
-    scale, widths, shifts, own_left, own_right, next_left, prev_right, mine, a, b, c, out, score
-):
+def blend_kernel(widths, shifts, own_left, own_right, next_left, prev_right, left, right):
     tile = lax.axis_index("tile")
     earlier = jnp.maximum(tile - 1, 0)
+    value = right_blend(widths[tile], shifts[tile], own_right, next_left)
+    right[...] = value.astype(jnp.bfloat16)
+    width, shift = jnp.where(tile > 0, widths[earlier], 0), jnp.where(tile > 0, shifts[earlier], 0)
+    left[...] = left_blend(width, shift, own_left, prev_right).astype(jnp.bfloat16)
+
+
+def image_kernel(scale, left, right, mine, a, b, c, out, score):
     total = mine.shape[1] - LANES
     for begin in range(0, total, LANES):
         at = slice(begin, begin + LANES)
         value = mine[:, at] + ((wide(a[:, at]) + wide(b[:, at])) + wide(c[:, at]))
         out[:, EDGE + begin : EDGE + begin + LANES] = (value * scale).astype(jnp.bfloat16)
-    value = right_blend(widths[tile], shifts[tile], own_right, next_left)
-    out[:, EDGE + total :] = value.astype(jnp.bfloat16)
-    width, shift = jnp.where(tile > 0, widths[earlier], 0), jnp.where(tile > 0, shifts[earlier], 0)
-    out[:, :EDGE] = left_blend(width, shift, own_left, prev_right).astype(jnp.bfloat16)
+    out[:, :EDGE] = left[...]
+    out[:, EDGE + total :] = right[...]
     at = slice(total, total + LANES)
     value = mine[:PAD, at] + ((wide(a[:, at]) + wide(b[:, at])) + wide(c[:, at]))[:PAD]
     score[...] = jnp.sum(value, axis=0, keepdims=True)
@@ -433,15 +430,14 @@
     mine_high, after_high = masked.astype(jnp.bfloat16), after.astype(jnp.bfloat16)
     mine_low = (masked - wide(mine_high)).astype(jnp.bfloat16)
     after_low = (after - wide(after_high)).astype(jnp.bfloat16)
-    gram = jnp.zeros((LANES, 2 * LANES), jnp.float32)
-    for t in range(STRIP // LANES):
-        for one, two in ((mine_high, after_high), (mine_high, after_low), (mine_low, after_high)):
-            gram += lax.dot_general(
-                one[:, t * LANES : (t + 1) * LANES],
-                two[:, t * LANES : (t + 2) * LANES],
-                (((0,), (0,)), ((), ())),
-                preferred_element_type=jnp.float32,
-            )
+    pairs = ((mine_high, after_high), (mine_high, after_low), (mine_low, after_high))
+    starts = range(0, STRIP, LANES)
+    gram = lax.dot_general(
+        jnp.concatenate([one[:, t : t + LANES] for one, _ in pairs for t in starts], 0),
+        jnp.concatenate([two[:, t : t + 2 * LANES] for _, two in pairs for t in starts], 0),
+        (((0,), (0,)), ((), ())),
+        preferred_element_type=jnp.float32,
+    )
     line = lax.broadcasted_iota(jnp.int32, gram.shape, 0)
     step = 1
     while step < LANES:
@@ -460,8 +456,8 @@
 
     low, high = EDGE + LANES, cols - STRIP - LANES
     places = [(0, 0, EDGE), (0, cols - STRIP, STRIP)]
-    third = (cols - STRIP - EDGE) // 3 // LANES * LANES
-    cuts = [EDGE, EDGE + third, EDGE + 2 * third, cols - STRIP]
+    ninth = (cols - STRIP - EDGE) // 9 // LANES * LANES
+    cuts = [EDGE, EDGE + 4 * ninth, EDGE + 7 * ninth, cols - STRIP]
     frame, theirs_s, theirs_m = Columns(moves, rows, cols, [], places).loaded(
         frame, low, high, list(zip(cuts[:-1], cuts[1:]))
     )
@@ -501,8 +497,14 @@
         after=[passing_m],
     )
 
-    far_f = ahead(passed(True, passing_m, got_f, [score]), 1, 1)
-    far_b = ahead(passed(False, passing_m, got_b, [score]), 1, -1)
+    half = (SIDE // 2, BAND, middle.total)
+    far_f, far_b = call(
+        pass_kernel,
+        [(half, jnp.bfloat16)] * 2,
+        [passing_m, got_f, got_b],
+        after=[score],
+    )
+    far_f, far_b = ahead(far_f, 1, 1), ahead(far_b, 1, -1)
     score = score + to_other_core(score)
     wider = (BAND, middle.total + LANES)
     row_m = call(
@@ -510,11 +512,16 @@
         [(wider, jnp.float32)] + [(wider, jnp.bfloat16)] * (SIDE - 1),
         [own_m, got_f, got_b, far_f, far_b, *[score], *direct([score] * SIDE, 1)],
     )
+    left_part, right_part = call(
+        blend_kernel,
+        [((BAND, EDGE), jnp.bfloat16), ((BAND, STRIP), jnp.bfloat16)],
+        [own_left, own_right, next_left, prev_right],
+        [intersection, seam_shift],
+    )
     image, score = call(
         functools.partial(image_kernel, scale),
         [((BAND, cols), jnp.bfloat16), ((1, LAGS), jnp.float32)],
-        [own_left, own_right, next_left, prev_right, row_m[0], *direct(row_m, 2)],
-        [intersection, seam_shift],
+        [left_part, right_part, row_m[0], *direct(row_m, 2)],
     )
     return (image[None], score)
 

time: 72.7 us -> 71.1 us (0.978)
  waiting for transfers between devices: 23.2 us -> 22.3 us
where the time goes in v4:
time: 71.1 us; the launch traced here: 71 us
  starting transfers between devices  29.5 us (41%)
  waiting for transfers between devices  22.3 us (31%)
  Pallas kernels  17.9 us (25%)
  between operations  0.76 us (1%)
    ppermute x20, starting transfers between devices, permuted(): lax.ppermute(array, 'frame', [(device_at(*place), device_at(*target(*plac...  23.4 us
    ppermute x20, waiting for transfers between devices, permuted(): lax.ppermute(array, 'frame', [(device_at(*place), device_at(*target(*plac...  17.5 us
    pallas_call x11, Pallas kernels, call(): pl.pallas_call(run, in_specs=[pl.BlockSpec(memory_space=pltpu.SMEM)] * le...  12.4 us
    ppermute x2, starting transfers between devices, from_behind(): return lax.ppermute(array, axis, pairs)  6.04 us
    pallas_call x1, Pallas kernels, loaded(): pl.pallas_call(kernel, in_specs=[far, far], out_specs=[vmem, vmem, vmem],...  5.48 us
    ppermute x2, waiting for transfers between devices, from_behind(): return lax.ppermute(array, axis, pairs)  4.73 us
  transfers between devices with their start and end apart: 22, of which 13 were waited for; matrix products, arithmetic and copies ran while one was open for 0% of the time, Pallas kernels for 15%

profile of v4, /device:TPU:102, one launch (start us, length us, event | category | flops | bytes accessed | tf_op | source)
XLA Modules:
  0.0 71.0 jit_solution(534626253793536860)
XLA Ops:
  1.3 5.5 %shard_map.59 = (bf16[1024,5760]{1,0:T(8,128)(2,1)S(1)}, bf16[16,32,1152]{2,1,0:T(8,128)(2,1)S(1)}, bf16[8,32,4608]{2,1,0:T(8,128)(2,1)S(1)}) custom-call(s32[2]{0:T(128)S(1)} %bitcast.3, bf16[1024,5760]{1,0:T(8,128)(2,1)} %bitcast.8), custom_call_target="tpu_custom_call" | custom-call | flops 1024 | bytes 1024 | tf_op jit(solution)/shard_map/pallas_call | solution.py:273
  6.9 1.9 %shard_map.60.refs_3_.refs_2_ = bf16[8,32,4608]{2,1,0:T(8,128)(2,1)S(1)} custom-call(s32[2]{0:T(128)S(1)} %bitcast.4, bf16[1024,5760]{1,0:T(8,128)(2,1)S(1)} %get-tuple-element.32.refs_1_, bf16[16,32,1152]{2,1,0:T(8,128)(2,1)S(1)} %get-tuple-element.33.refs_2_), custom_call_target="tpu_custom_call" | custom-call | flops 1024 | bytes 1024 | tf_op jit(solution)/shard_map/pallas_call | solution.py:70
  10.2 1.5 %shard_map.61 = (f32[4,32,1152]{2,1,0:T(8,128)S(1)}, bf16[4,32,1152]{2,1,0:T(8,128)(2,1)S(1)}, bf16[4,32,1152]{2,1,0:T(8,128)(2,1)S(1)}, bf16[4,32,1152]{2,1,0:T(8,128)(2,1)S(1)}) custom-call(s32[2]{0:T(128)S(1)} %bitcast.5, bf16[1024,5760]{1,0:T(8,128)(2,1)S(1)} %get-tuple-element.32.refs_1_, ...), custom_call_target="tpu_custom_call" | custom-call | flops 1024 | bytes 1024 | tf_op jit(solution)/shard_map/pallas_call | solution.py:70
  11.7 1.5 %collective-permute-start.1 = (bf16[4,32,1152]{2,1,0:T(8,128)(2,1)S(1)}, bf16[4,32,1152]{2,1,0:T(8,128)(2,1)S(1)}, u32[]{:S(2)}, u32[]{:S(2)}) collective-permute-start(bf16[4,32,1152]{2,1,0:T(8,128)(2,1)S(1)} %get-tuple-element.35), channel_id=1, source_target_pairs={{0,4},{1,17},{2,6},{3,19},{4,0},{5,21},{6,2},{7,23},{8,12},{9,25},... | collective-permute-start | bytes 884744 | tf_op jit(solution)/shard_map/ppermute | solution.py:30
  13.2 2.1 %collective-permute-start.2 = (bf16[4,32,1152]{2,1,0:T(8,128)(2,1)S(1)}, bf16[4,32,1152]{2,1,0:T(8,128)(2,1)S(1)}, u32[]{:S(2)}, u32[]{:S(2)}) collective-permute-start(bf16[4,32,1152]{2,1,0:T(8,128)(2,1)S(1)} %get-tuple-element.36), channel_id=1, source_target_pairs={{0,2},{1,9},{2,4},{3,11},{4,6},{5,13},{6,0},{7,15},{8,10},{9,17},{... | collective-permute-start | bytes 884744 | tf_op jit(solution)/shard_map/ppermute | solution.py:30
  15.3 2.6 %shard_map.63 = (bf16[4,32,4608]{2,1,0:T(8,128)(2,1)S(1)}, bf16[4,32,4608]{2,1,0:T(8,128)(2,1)S(1)}) custom-call(s32[2]{0:T(128)S(1)} %bitcast.6, bf16[1024,5760]{1,0:T(8,128)(2,1)S(1)} %get-tuple-element.32.refs_1_, bf16[8,32,4608]{2,1,0:T(8,128)(2,1)S(1)} %collective-permute-done.4.refs_2_, f32[4,32,1152]{2,1,0:T(8,128)S(1)} %get-tuple-element.34.refs_3_.refs_0_), custom_call_target="tpu_custom_call" | custom-call | flops 1024 | bytes 1024 | tf_op jit(solution)/shard_map/pallas_call | solution.py:70
  17.9 2.2 %collective-permute-done.1.refs_2_.refs_1_ = bf16[4,32,1152]{2,1,0:T(8,128)(2,1)S(1)} collective-permute-done((bf16[4,32,1152]{2,1,0:T(8,128)(2,1)S(1)}, bf16[4,32,1152]{2,1,0:T(8,128)(2,1)S(1)}, u32[]{:S(2)}, u32[]{:S(2)}) %collective-permute-start.1) | collective-permute-done | bytes 294944 | tf_op jit(solution)/shard_map/ppermute | solution.py:30
  21.0 2.2 %collective-permute-done.3.refs_4_.refs_3_ = bf16[4,32,1152]{2,1,0:T(8,128)(2,1)S(1)} collective-permute-done((bf16[4,32,1152]{2,1,0:T(8,128)(2,1)S(1)}, bf16[4,32,1152]{2,1,0:T(8,128)(2,1)S(1)}, u32[]{:S(2)}, u32[]{:S(2)}) %collective-permute-start.3) | collective-permute-done | bytes 294944 | tf_op jit(solution)/shard_map/ppermute | solution.py:30
  23.8 1.5 %collective-permute-start.12 = (bf16[4,32,4608]{2,1,0:T(8,128)(2,1)S(1)}, bf16[4,32,4608]{2,1,0:T(8,128)(2,1)S(1)}, u32[]{:S(2)}, u32[]{:S(2)}) collective-permute-start(bf16[4,32,4608]{2,1,0:T(8,128)(2,1)S(1)} %get-tuple-element.52), channel_id=1, source_target_pairs={{0,6},{1,25},{2,0},{3,27},{4,2},{5,29},{6,4},{7,31},{8,14},{9,1},{... | collective-permute-start | bytes 3538952 | tf_op jit(solution)/shard_map/ppermute | solution.py:30
  25.4 3.3 %collective-permute-start.6 = (bf16[32,1152]{1,0:T(8,128)(2,1)S(1)}, bf16[32,1152]{1,0:T(8,128)(2,1)S(1)}, u32[]{:S(2)}, u32[]{:S(2)}) collective-permute-start(bf16[32,1152]{1,0:T(8,128)(2,1)S(1)} %get-tuple-element.43), channel_id=1, source_target_pairs={{0,16},{1,5},{2,18},{3,7},{4,20},{5,1},{6,22},{7,3},{8,24},{9,13},... | collective-permute-start | bytes 221192 | tf_op jit(solution)/shard_map/ppermute | solution.py:30
  29.4 2.5 %collective-permute-start.8 = (bf16[32,1152]{1,0:T(8,128)(2,1)S(1)}, bf16[32,1152]{1,0:T(8,128)(2,1)S(1)}, u32[]{:S(2)}, u32[]{:S(2)}) collective-permute-start(bf16[32,1152]{1,0:T(8,128)(2,1)S(1)} %get-tuple-element.45), channel_id=1, source_target_pairs={{0,24},{1,7},{2,26},{3,1},{4,28},{5,3},{6,30},{7,5},{8,0},{9,15},{... | collective-permute-start | bytes 221192 | tf_op jit(solution)/shard_map/ppermute | solution.py:30
  32.2 2.9 %collective-permute-done.7.refs_2_ = bf16[32,1152]{1,0:T(8,128)(2,1)S(1)} collective-permute-done((bf16[32,1152]{1,0:T(8,128)(2,1)S(1)}, bf16[32,1152]{1,0:T(8,128)(2,1)S(1)}, u32[]{:S(2)}, u32[]{:S(2)}) %collective-permute-start.7) | collective-permute-done | bytes 73760 | tf_op jit(solution)/shard_map/ppermute | solution.py:30
  35.2 2.2 %collective-permute-start.9 = (f32[32,640]{1,0:T(8,128)S(1)}, f32[32,640]{1,0:T(8,128)S(1)}, u32[]{:S(2)}, u32[]{:S(2)}) collective-permute-start(f32[32,640]{1,0:T(8,128)S(1)} %get-tuple-element.46.refs_2_.refs_3_), channel_id=1, source_target_pairs={{32,0},{64,32},{96,64},{128,96},{160,128},{192,160},{224,192},{33,... | collective-permute-start | bytes 245768 | tf_op jit(solution)/shard_map/ppermute | solution.py:55
  37.4 2.6 %shard_map.68 = (f32[4,32,4608]{2,1,0:T(8,128)S(1)}, f32[4,32,4608]{2,1,0:T(8,128)S(1)}) custom-call(s32[2]{0:T(128)S(1)} %bitcast.7, bf16[1024,5760]{1,0:T(8,128)(2,1)S(1)} %get-tuple-element.32.refs_1_, bf16[8,32,4608]{2,1,0:T(8,128)(2,1)S(1)} %collective-permute-done.5.refs_5_.refs_2_, f32[32,640]{1,0:T(8,128)S(1)} %get-tuple-element.46.refs_2_.refs_3_), custom_call_target="tpu_custom_call" | custom-call | flops 1024 | bytes 1024 | tf_op jit(solution)/shard_map/pallas_call | solution.py:70
  40.0 2.7 %collective-permute-done.9.refs_4_.refs_2_ = f32[32,640]{1,0:T(8,128)S(1)} collective-permute-done((f32[32,640]{1,0:T(8,128)S(1)}, f32[32,640]{1,0:T(8,128)S(1)}, u32[]{:S(2)}, u32[]{:S(2)}) %collective-permute-start.9) | collective-permute-done | bytes 81952 | tf_op jit(solution)/shard_map/ppermute | solution.py:55
  44.4 1.8 %collective-permute-start.13 = (bf16[2,32,4608]{2,1,0:T(8,128)(2,1)S(1)}, bf16[2,32,4608]{2,1,0:T(8,128)(2,1)S(1)}, u32[]{:S(2)}, u32[]{:S(2)}) collective-permute-start(bf16[2,32,4608]{2,1,0:T(8,128)(2,1)S(1)} %get-tuple-element.54), channel_id=1, source_target_pairs={{0,2},{1,9},{2,4},{3,11},{4,6},{5,13},{6,0},{7,15},{8,10},{9,17},{... | collective-permute-start | bytes 1769480 | tf_op jit(solution)/shard_map/ppermute | solution.py:30
  47.7 1.4 %collective-permute-start.16 = (f32[8,128]{1,0:T(8,128)S(1)}, f32[8,128]{1,0:T(8,128)S(1)}, u32[]{:S(2)}, u32[]{:S(2)}) collective-permute-start(f32[8,128]{1,0:T(8,128)S(1)} %add.3.refs_5_), channel_id=1, source_target_pairs={{0,4},{1,17},{2,6},{3,19},{4,0},{5,21},{6,2},{7,23},{8,12},{9,25},... | collective-permute-start | bytes 12296 | tf_op jit(solution)/shard_map/ppermute | solution.py:30
  49.1 1.5 %collective-permute-start.17 = (f32[8,128]{1,0:T(8,128)S(1)}, f32[8,128]{1,0:T(8,128)S(1)}, u32[]{:S(2)}, u32[]{:S(2)}) collective-permute-start(f32[8,128]{1,0:T(8,128)S(1)} %add.3.refs_5_), channel_id=1, source_target_pairs={{0,2},{1,9},{2,4},{3,11},{4,6},{5,13},{6,0},{7,15},{8,10},{9,17},{... | collective-permute-start | bytes 12296 | tf_op jit(solution)/shard_map/ppermute | solution.py:30
  51.5 4.4 %collective-permute-done.16.refs_6_ = f32[8,128]{1,0:T(8,128)S(1)} collective-permute-done((f32[8,128]{1,0:T(8,128)S(1)}, f32[8,128]{1,0:T(8,128)S(1)}, u32[]{:S(2)}, u32[]{:S(2)}) %collective-permute-start.16) | collective-permute-done | bytes 4128 | tf_op jit(solution)/shard_map/ppermute | solution.py:30
  55.9 1.5 %collective-permute-done.18.refs_8_ = f32[8,128]{1,0:T(8,128)S(1)} collective-permute-done((f32[8,128]{1,0:T(8,128)S(1)}, f32[8,128]{1,0:T(8,128)S(1)}, u32[]{:S(2)}, u32[]{:S(2)}) %collective-permute-start.18) | collective-permute-done | bytes 4128 | tf_op jit(solution)/shard_map/ppermute | solution.py:30
  57.8 1.5 %collective-permute-start.19 = (bf16[32,4736]{1,0:T(8,128)(2,1)S(1)}, bf16[32,4736]{1,0:T(8,128)(2,1)S(1)}, u32[]{:S(2)}, u32[]{:S(2)}) collective-permute-start(bf16[32,4736]{1,0:T(8,128)(2,1)S(1)} %get-tuple-element.57), channel_id=1, source_target_pairs={{0,16},{1,5},{2,18},{3,7},{4,20},{5,1},{6,22},{7,3},{8,24},{9,13},... | collective-permute-start | bytes 909320 | tf_op jit(solution)/shard_map/ppermute | solution.py:30
  59.4 2.6 %collective-permute-start.20 = (bf16[32,4736]{1,0:T(8,128)(2,1)S(1)}, bf16[32,4736]{1,0:T(8,128)(2,1)S(1)}, u32[]{:S(2)}, u32[]{:S(2)}) collective-permute-start(bf16[32,4736]{1,0:T(8,128)(2,1)S(1)} %get-tuple-element.58), channel_id=1, source_target_pairs={{0,8},{1,3},{2,10},{3,5},{4,12},{5,7},{6,14},{7,1},{8,16},{9,11},{... | collective-permute-start | bytes 909320 | tf_op jit(solution)/shard_map/ppermute | solution.py:30
  62.6 3.8 %collective-permute-start.10 = (bf16[32,512]{1,0:T(8,128)(2,1)S(1)}, bf16[32,512]{1,0:T(8,128)(2,1)S(1)}, u32[]{:S(2)}, u32[]{:S(2)}) collective-permute-start(bf16[32,512]{1,0:T(8,128)(2,1)S(1)} %get-tuple-element.48), channel_id=1, source_target_pairs={{0,32},{32,64},{64,96},{96,128},{128,160},{160,192},{192,224},{1,3... | collective-permute-start | bytes 98312 | tf_op jit(solution)/shard_map/ppermute | solution.py:55
  66.4 2.0 %collective-permute-done.10.refs_5_ = bf16[32,512]{1,0:T(8,128)(2,1)S(1)} collective-permute-done((bf16[32,512]{1,0:T(8,128)(2,1)S(1)}, bf16[32,512]{1,0:T(8,128)(2,1)S(1)}, u32[]{:S(2)}, u32[]{:S(2)}) %collective-permute-start.10) | collective-permute-done | bytes 32800 | tf_op jit(solution)/shard_map/ppermute | solution.py:55
  (41 shorter events, 12.5 us)
Async XLA Ops:
  6.8 2.9 %collective-permute-start = (bf16[16,32,1152]{2,1,0:T(8,128)(2,1)S(1)}, bf16[16,32,1152]{2,1,0:T(8,128)(2,1)S(1)}, u32[]{:S(2)}, u32[]{:S(2)}) collective-permute-start(bf16[16,32,1152]{2,1,0:T(8,128)(2,1)S(1)} %get-tuple-element.33.refs_2_), channel_id=1, source_target_pairs={{0,1},{1,0},{2,3},{3,2},{4,5},{5,4},{6,7},{7,6},{8,9},{9,8},{10,11... | collective-permute-start | bytes 3538952 | tf_op jit(solution)/shard_map/ppermute | solution.py:30
  9.7 5.6 %collective-permute-start.4 = (bf16[8,32,4608]{2,1,0:T(8,128)(2,1)S(1)}, bf16[8,32,4608]{2,1,0:T(8,128)(2,1)S(1)}, u32[]{:S(2)}, u32[]{:S(2)}) collective-permute-start(bf16[8,32,4608]{2,1,0:T(8,128)(2,1)S(1)} %shard_map.62), channel_id=1, source_target_pairs={{0,1},{1,0},{2,3},{3,2},{4,5},{5,4},{6,7},{7,6},{8,9},{9,8},{10,11... | collective-permute-start | bytes 7077896 | tf_op jit(solution)/shard_map/ppermute | solution.py:30
  9.8 15.4 %collective-permute-start.5 = (bf16[8,32,4608]{2,1,0:T(8,128)(2,1)S(1)}, bf16[8,32,4608]{2,1,0:T(8,128)(2,1)S(1)}, u32[]{:S(2)}, u32[]{:S(2)}) collective-permute-start(bf16[8,32,4608]{2,1,0:T(8,128)(2,1)S(1)} %shard_map.60.refs_3_.refs_2_), channel_id=1, source_target_pairs={{0,1},{1,0},{2,3},{3,2},{4,5},{5,4},{6,7},{7,6},{8,9},{9,8},{10,11... | collective-permute-start | bytes 7077896 | tf_op jit(solution)/shard_map/ppermute | solution.py:30
  11.7 8.3 %collective-permute-start.1 = (bf16[4,32,1152]{2,1,0:T(8,128)(2,1)S(1)}, bf16[4,32,1152]{2,1,0:T(8,128)(2,1)S(1)}, u32[]{:S(2)}, u32[]{:S(2)}) collective-permute-start(bf16[4,32,1152]{2,1,0:T(8,128)(2,1)S(1)} %get-tuple-element.35), channel_id=1, source_target_pairs={{0,4},{1,17},{2,6},{3,19},{4,0},{5,21},{6,2},{7,23},{8,12},{9,25},... | collective-permute-start | bytes 884744 | tf_op jit(solution)/shard_map/ppermute | solution.py:30
  13.2 7.8 %collective-permute-start.2 = (bf16[4,32,1152]{2,1,0:T(8,128)(2,1)S(1)}, bf16[4,32,1152]{2,1,0:T(8,128)(2,1)S(1)}, u32[]{:S(2)}, u32[]{:S(2)}) collective-permute-start(bf16[4,32,1152]{2,1,0:T(8,128)(2,1)S(1)} %get-tuple-element.36), channel_id=1, source_target_pairs={{0,2},{1,9},{2,4},{3,11},{4,6},{5,13},{6,0},{7,15},{8,10},{9,17},{... | collective-permute-start | bytes 884744 | tf_op jit(solution)/shard_map/ppermute | solution.py:30
  15.3 7.9 %collective-permute-start.3 = (bf16[4,32,1152]{2,1,0:T(8,128)(2,1)S(1)}, bf16[4,32,1152]{2,1,0:T(8,128)(2,1)S(1)}, u32[]{:S(2)}, u32[]{:S(2)}) collective-permute-start(bf16[4,32,1152]{2,1,0:T(8,128)(2,1)S(1)} %get-tuple-element.37), channel_id=1, source_target_pairs={{0,6},{1,25},{2,0},{3,27},{4,2},{5,29},{6,4},{7,31},{8,14},{9,1},{... | collective-permute-start | bytes 884744 | tf_op jit(solution)/shard_map/ppermute | solution.py:30
  23.2 20.8 %collective-permute-start.11 = (bf16[4,32,4608]{2,1,0:T(8,128)(2,1)S(1)}, bf16[4,32,4608]{2,1,0:T(8,128)(2,1)S(1)}, u32[]{:S(2)}, u32[]{:S(2)}) collective-permute-start(bf16[4,32,4608]{2,1,0:T(8,128)(2,1)S(1)} %get-tuple-element.41.refs_4_), channel_id=1, source_target_pairs={{0,2},{1,9},{2,4},{3,11},{4,6},{5,13},{6,0},{7,15},{8,10},{9,17},{... | collective-permute-start | bytes 3538952 | tf_op jit(solution)/shard_map/ppermute | solution.py:30
  23.8 20.3 %collective-permute-start.12 = (bf16[4,32,4608]{2,1,0:T(8,128)(2,1)S(1)}, bf16[4,32,4608]{2,1,0:T(8,128)(2,1)S(1)}, u32[]{:S(2)}, u32[]{:S(2)}) collective-permute-start(bf16[4,32,4608]{2,1,0:T(8,128)(2,1)S(1)} %get-tuple-element.52), channel_id=1, source_target_pairs={{0,6},{1,25},{2,0},{3,27},{4,2},{5,29},{6,4},{7,31},{8,14},{9,1},{... | collective-permute-start | bytes 3538952 | tf_op jit(solution)/shard_map/ppermute | solution.py:30
  25.4 6.8 %collective-permute-start.6 = (bf16[32,1152]{1,0:T(8,128)(2,1)S(1)}, bf16[32,1152]{1,0:T(8,128)(2,1)S(1)}, u32[]{:S(2)}, u32[]{:S(2)}) collective-permute-start(bf16[32,1152]{1,0:T(8,128)(2,1)S(1)} %get-tuple-element.43), channel_id=1, source_target_pairs={{0,16},{1,5},{2,18},{3,7},{4,20},{5,1},{6,22},{7,3},{8,24},{9,13},... | collective-permute-start | bytes 221192 | tf_op jit(solution)/shard_map/ppermute | solution.py:30
  28.7 6.4 %collective-permute-start.7 = (bf16[32,1152]{1,0:T(8,128)(2,1)S(1)}, bf16[32,1152]{1,0:T(8,128)(2,1)S(1)}, u32[]{:S(2)}, u32[]{:S(2)}) collective-permute-start(bf16[32,1152]{1,0:T(8,128)(2,1)S(1)} %get-tuple-element.44), channel_id=1, source_target_pairs={{0,8},{1,3},{2,10},{3,5},{4,12},{5,7},{6,14},{7,1},{8,16},{9,11},{... | collective-permute-start | bytes 221192 | tf_op jit(solution)/shard_map/ppermute | solution.py:30
  29.4 5.7 %collective-permute-start.8 = (bf16[32,1152]{1,0:T(8,128)(2,1)S(1)}, bf16[32,1152]{1,0:T(8,128)(2,1)S(1)}, u32[]{:S(2)}, u32[]{:S(2)}) collective-permute-start(bf16[32,1152]{1,0:T(8,128)(2,1)S(1)} %get-tuple-element.45), channel_id=1, source_target_pairs={{0,24},{1,7},{2,26},{3,1},{4,28},{5,3},{6,30},{7,5},{8,0},{9,15},{... | collective-permute-start | bytes 221192 | tf_op jit(solution)/shard_map/ppermute | solution.py:30
  35.2 7.6 %copy-start.1 = (s32[8]{0:T(128)S(1)}, s32[8]{0:T(128)}, u32[]{:S(2)}) copy-start(s32[8]{0:T(128)} %refs_0_.3) | copy-start | bytes 100
  35.2 7.5 %collective-permute-start.9 = (f32[32,640]{1,0:T(8,128)S(1)}, f32[32,640]{1,0:T(8,128)S(1)}, u32[]{:S(2)}, u32[]{:S(2)}) collective-permute-start(f32[32,640]{1,0:T(8,128)S(1)} %get-tuple-element.46.refs_2_.refs_3_), channel_id=1, source_target_pairs={{32,0},{64,32},{96,64},{128,96},{160,128},{192,160},{224,192},{33,... | collective-permute-start | bytes 245768 | tf_op jit(solution)/shard_map/ppermute | solution.py:55
  44.4 13.0 %collective-permute-start.13 = (bf16[2,32,4608]{2,1,0:T(8,128)(2,1)S(1)}, bf16[2,32,4608]{2,1,0:T(8,128)(2,1)S(1)}, u32[]{:S(2)}, u32[]{:S(2)}) collective-permute-start(bf16[2,32,4608]{2,1,0:T(8,128)(2,1)S(1)} %get-tuple-element.54), channel_id=1, source_target_pairs={{0,2},{1,9},{2,4},{3,11},{4,6},{5,13},{6,0},{7,15},{8,10},{9,17},{... | collective-permute-start | bytes 1769480 | tf_op jit(solution)/shard_map/ppermute | solution.py:30
  46.2 11.2 %collective-permute-start.14 = (bf16[2,32,4608]{2,1,0:T(8,128)(2,1)S(1)}, bf16[2,32,4608]{2,1,0:T(8,128)(2,1)S(1)}, u32[]{:S(2)}, u32[]{:S(2)}) collective-permute-start(bf16[2,32,4608]{2,1,0:T(8,128)(2,1)S(1)} %get-tuple-element.55), channel_id=1, source_target_pairs={{0,6},{1,25},{2,0},{3,27},{4,2},{5,29},{6,4},{7,31},{8,14},{9,1},{... | collective-permute-start | bytes 1769480 | tf_op jit(solution)/shard_map/ppermute | solution.py:30
  46.5 1.2 %collective-permute-start.15 = (f32[8,128]{1,0:T(8,128)S(1)}, f32[8,128]{1,0:T(8,128)S(1)}, u32[]{:S(2)}, u32[]{:S(2)}) collective-permute-start(f32[8,128]{1,0:T(8,128)S(1)} %shard_map.69.refs_3_), channel_id=1, source_target_pairs={{0,1},{1,0},{2,3},{3,2},{4,5},{5,4},{6,7},{7,6},{8,9},{9,8},{10,11... | collective-permute-start | bytes 12296 | tf_op jit(solution)/shard_map/ppermute | solution.py:30
  47.7 8.3 %collective-permute-start.16 = (f32[8,128]{1,0:T(8,128)S(1)}, f32[8,128]{1,0:T(8,128)S(1)}, u32[]{:S(2)}, u32[]{:S(2)}) collective-permute-start(f32[8,128]{1,0:T(8,128)S(1)} %add.3.refs_5_), channel_id=1, source_target_pairs={{0,4},{1,17},{2,6},{3,19},{4,0},{5,21},{6,2},{7,23},{8,12},{9,25},... | collective-permute-start | bytes 12296 | tf_op jit(solution)/shard_map/ppermute | solution.py:30
  49.1 6.8 %collective-permute-start.17 = (f32[8,128]{1,0:T(8,128)S(1)}, f32[8,128]{1,0:T(8,128)S(1)}, u32[]{:S(2)}, u32[]{:S(2)}) collective-permute-start(f32[8,128]{1,0:T(8,128)S(1)} %add.3.refs_5_), channel_id=1, source_target_pairs={{0,2},{1,9},{2,4},{3,11},{4,6},{5,13},{6,0},{7,15},{8,10},{9,17},{... | collective-permute-start | bytes 12296 | tf_op jit(solution)/shard_map/ppermute | solution.py:30
  50.6 6.8 %collective-permute-start.18 = (f32[8,128]{1,0:T(8,128)S(1)}, f32[8,128]{1,0:T(8,128)S(1)}, u32[]{:S(2)}, u32[]{:S(2)}) collective-permute-start(f32[8,128]{1,0:T(8,128)S(1)} %add.3.refs_5_), channel_id=1, source_target_pairs={{0,6},{1,25},{2,0},{3,27},{4,2},{5,29},{6,4},{7,31},{8,14},{9,1},{... | collective-permute-start | bytes 12296 | tf_op jit(solution)/shard_map/ppermute | solution.py:30
  57.4 11.0 %copy-start.2 = (s32[8]{0:T(128)S(1)}, s32[8]{0:T(128)}, u32[]{:S(2)}) copy-start(s32[8]{0:T(128)} %refs_1_.1) | copy-start | bytes 100
  57.8 11.3 %collective-permute-start.19 = (bf16[32,4736]{1,0:T(8,128)(2,1)S(1)}, bf16[32,4736]{1,0:T(8,128)(2,1)S(1)}, u32[]{:S(2)}, u32[]{:S(2)}) collective-permute-start(bf16[32,4736]{1,0:T(8,128)(2,1)S(1)} %get-tuple-element.57), channel_id=1, source_target_pairs={{0,16},{1,5},{2,18},{3,7},{4,20},{5,1},{6,22},{7,3},{8,24},{9,13},... | collective-permute-start | bytes 909320 | tf_op jit(solution)/shard_map/ppermute | solution.py:30
  59.4 10.1 %collective-permute-start.20 = (bf16[32,4736]{1,0:T(8,128)(2,1)S(1)}, bf16[32,4736]{1,0:T(8,128)(2,1)S(1)}, u32[]{:S(2)}, u32[]{:S(2)}) collective-permute-start(bf16[32,4736]{1,0:T(8,128)(2,1)S(1)} %get-tuple-element.58), channel_id=1, source_target_pairs={{0,8},{1,3},{2,10},{3,5},{4,12},{5,7},{6,14},{7,1},{8,16},{9,11},{... | collective-permute-start | bytes 909320 | tf_op jit(solution)/shard_map/ppermute | solution.py:30
  62.0 8.1 %collective-permute-start.21 = (bf16[32,4736]{1,0:T(8,128)(2,1)S(1)}, bf16[32,4736]{1,0:T(8,128)(2,1)S(1)}, u32[]{:S(2)}, u32[]{:S(2)}) collective-permute-start(bf16[32,4736]{1,0:T(8,128)(2,1)S(1)} %get-tuple-element.59), channel_id=1, source_target_pairs={{0,24},{1,7},{2,26},{3,1},{4,28},{5,3},{6,30},{7,5},{8,0},{9,15},{... | collective-permute-start | bytes 909320 | tf_op jit(solution)/shard_map/ppermute | solution.py:30
  62.6 5.8 %collective-permute-start.10 = (bf16[32,512]{1,0:T(8,128)(2,1)S(1)}, bf16[32,512]{1,0:T(8,128)(2,1)S(1)}, u32[]{:S(2)}, u32[]{:S(2)}) collective-permute-start(bf16[32,512]{1,0:T(8,128)(2,1)S(1)} %get-tuple-element.48), channel_id=1, source_target_pairs={{0,32},{32,64},{64,96},{96,128},{128,160},{160,192},{192,224},{1,3... | collective-permute-start | bytes 98312 | tf_op jit(solution)/shard_map/ppermute | solution.py:55
  (1 other events, 0.7 us)

commit v5 on v4

--- a/solution.py
+++ b/solution.py
@@ -59,7 +59,7 @@
     return array.astype(jnp.float32)
 
 
-def call(kernel, out_shape, operands, scalars=(), after=(), scratch=()):
+def call(kernel, out_shape, operands, scalars=(), after=(), scratch=(), aliases=None):
     vmem = pl.BlockSpec(memory_space=pltpu.VMEM)
     anywhere = pl.BlockSpec(memory_space=pl.ANY)
     first, last = len(scalars) + len(operands), len(scalars) + len(operands) + len(after)
@@ -74,6 +74,7 @@
         + [anywhere] * len(after),
         out_specs=[vmem] * len(out_shape),
         out_shape=[jax.ShapeDtypeStruct(shape, dtype) for shape, dtype in out_shape],
+        input_output_aliases=aliases or {},
         scratch_shapes=list(scratch),
         compiler_params=pltpu.CompilerParams(vmem_limit_bytes=VMEM),
         cost_estimate=pl.CostEstimate(flops=1024, bytes_accessed=1024, transcendentals=0),
@@ -256,9 +257,11 @@
                 bands[n, :, begin : begin + LANES] = value.astype(jnp.bfloat16)
 
             each_band(mover, SIDE * SIDE, every, write)
-            for pair, (begin, end) in zip(copies[2:], middle):
+            for p, (pair, (begin, end)) in enumerate(zip(copies[2:], middle)):
                 for copy in pair:
                     copy.wait()
+                if p == len(middle) - 1:
+                    break
                 mover = Mover(moves, [(out, 0, begin, end - begin)], rows, cols, held_middle, True)
 
                 def write_middle(n, at, value, begin=begin):
@@ -269,7 +272,7 @@
 
         vmem = pl.BlockSpec(memory_space=pltpu.VMEM)
         far = pl.BlockSpec(memory_space=pltpu.HBM)
-        widest = max(end - begin for begin, end in middle)
+        widest = max(end - begin for begin, end in middle[:-1])
         return pl.pallas_call(
             kernel,
             in_specs=[far, far],
@@ -290,6 +293,35 @@
             cost_estimate=pl.CostEstimate(flops=1024, bytes_accessed=1024, transcendentals=0),
         )(self.moves, frame)
 
+    def theirs_rest(self, both, last, after=()):
+        first = both.shape[2] - last.total
+
+        def kernel(moves, frame, both, bands, out, held, held_last):
+            mover = last.mover(moves, [frame], held_last, True)
+
+            def write_last(n, begin, value):
+                at = slice(first + begin, first + begin + LANES)
+                out[n, :, at] = value.astype(jnp.bfloat16)
+
+            each_band(mover, 2 * SIDE, both_ways, write_last)
+            mover = self.mover(moves, [frame], held, True)
+
+            def write(n, begin, value):
+                bands[n, :, begin : begin + LANES] = value.astype(jnp.bfloat16)
+
+            each_band(mover, 2 * SIDE, later, write)
+
+        shape = ((2 * SIDE, BAND, self.total), jnp.bfloat16)
+        return call(
+            kernel,
+            [shape, shape],
+            [*self.arrays, both],
+            [self.moves],
+            after,
+            [*self.scratch, *last.scratch],
+            {2: 1},
+        )
+
     def pairs(self, other, after=()):
         def body(mover, other, *outs):
             for way, where in enumerate((forward, backward)):
@@ -465,8 +497,9 @@
     middle = Columns(moves, rows, cols, [frame], [(0, EDGE, cols - STRIP - EDGE)])
 
     other_s = to_other_core(theirs_s)
-    theirs_l = middle.theirs(2 * SIDE, later, [theirs_s])
-    other_m = to_other_core(*gated([theirs_m], [other_s, theirs_l]))
+    ending = Columns(moves, rows, cols, [frame], [(0, cuts[-2], cuts[-1] - cuts[-2])])
+    theirs_l, theirs_m = middle.theirs_rest(theirs_m, ending, [theirs_s])
+    other_m = to_other_core(*gated([theirs_m], [other_s]))
     other_l = to_other_core(theirs_l)
     pair_s = strips.every_pair(other_s, [theirs_l])
     got_s = direct(pair_s, 1)

time: 71.1 us -> 70.5 us (level)
  transfers between devices with their start and end apart: 22 -> 22, of which waited for: 13 -> 13; matrix products, arithmetic and copies ran while one was open for 0% -> 0% of each run, Pallas kernels for 15% -> 16%
where the time goes in v5:
time: 70.5 us; the launch traced here: 70.4 us
  starting transfers between devices  29.4 us (42%)
  waiting for transfers between devices  21.9 us (31%)
  Pallas kernels  17.6 us (25%)
  between operations  0.76 us (1%)
    ppermute x20, starting transfers between devices, permuted(): lax.ppermute(array, 'frame', [(device_at(*place), device_at(*target(*plac...  23.4 us
    ppermute x20, waiting for transfers between devices, permuted(): lax.ppermute(array, 'frame', [(device_at(*place), device_at(*target(*plac...  17.1 us
    pallas_call x11, Pallas kernels, call(): pl.pallas_call(run, in_specs=[pl.BlockSpec(memory_space=pltpu.SMEM)] * le...  12.8 us
    ppermute x2, starting transfers between devices, from_behind(): return lax.ppermute(array, axis, pairs)  5.98 us
    pallas_call x1, Pallas kernels, loaded(): pl.pallas_call(kernel, in_specs=[far, far], out_specs=[vmem, vmem, vmem],...  4.84 us
    ppermute x2, waiting for transfers between devices, from_behind(): return lax.ppermute(array, axis, pairs)  4.78 us
  transfers between devices with their start and end apart: 22, of which 13 were waited for; matrix products, arithmetic and copies ran while one was open for 0% of the time, Pallas kernels for 16%

profile of v5, /device:TPU:102, one launch (start us, length us, event | category | flops | bytes accessed | tf_op | source)
XLA Modules:
  0.0 70.4 jit_solution(12270856731121268088)
XLA Ops:
  1.3 4.8 %shard_map.59 = (bf16[1024,5760]{1,0:T(8,128)(2,1)S(1)}, bf16[16,32,1152]{2,1,0:T(8,128)(2,1)S(1)}, bf16[8,32,4608]{2,1,0:T(8,128)(2,1)S(1)}) custom-call(s32[2]{0:T(128)S(1)} %bitcast.3, bf16[1024,5760]{1,0:T(8,128)(2,1)} %bitcast.8), custom_call_target="tpu_custom_call" | custom-call | flops 1024 | bytes 1024 | tf_op jit(solution)/shard_map/pallas_call | solution.py:276
  6.2 2.3 %shard_map.60 = (bf16[8,32,4608]{2,1,0:T(8,128)(2,1)S(1)}, bf16[8,32,4608]{2,1,0:T(8,128)(2,1)S(1)}) custom-call(s32[2]{0:T(128)S(1)} %bitcast.4, bf16[1024,5760]{1,0:T(8,128)(2,1)S(1)} %get-tuple-element.34.refs_1_, bf16[8,32,4608]{2,1,0:T(8,128)(2,1)S(1)} %get-tuple-element.36.refs_2_, ...), custom_call_target="tpu_custom_call", output_to_operand_aliasing={{1}: (2, {})} | custom-call | flops 1024 | bytes 1024 | tf_op jit(solution)/shard_map/pallas_call | solution.py:70
  9.6 1.5 %shard_map.61 = (f32[4,32,1152]{2,1,0:T(8,128)S(1)}, bf16[4,32,1152]{2,1,0:T(8,128)(2,1)S(1)}, bf16[4,32,1152]{2,1,0:T(8,128)(2,1)S(1)}, bf16[4,32,1152]{2,1,0:T(8,128)(2,1)S(1)}) custom-call(s32[2]{0:T(128)S(1)} %bitcast.5, bf16[1024,5760]{1,0:T(8,128)(2,1)S(1)} %get-tuple-element.34.refs_1_, ...), custom_call_target="tpu_custom_call" | custom-call | flops 1024 | bytes 1024 | tf_op jit(solution)/shard_map/pallas_call | solution.py:70
  11.1 1.5 %collective-permute-start.1 = (bf16[4,32,1152]{2,1,0:T(8,128)(2,1)S(1)}, bf16[4,32,1152]{2,1,0:T(8,128)(2,1)S(1)}, u32[]{:S(2)}, u32[]{:S(2)}) collective-permute-start(bf16[4,32,1152]{2,1,0:T(8,128)(2,1)S(1)} %get-tuple-element.39), channel_id=1, source_target_pairs={{0,4},{1,17},{2,6},{3,19},{4,0},{5,21},{6,2},{7,23},{8,12},{9,25},... | collective-permute-start | bytes 884744 | tf_op jit(solution)/shard_map/ppermute | solution.py:30
  12.6 2.1 %collective-permute-start.2 = (bf16[4,32,1152]{2,1,0:T(8,128)(2,1)S(1)}, bf16[4,32,1152]{2,1,0:T(8,128)(2,1)S(1)}, u32[]{:S(2)}, u32[]{:S(2)}) collective-permute-start(bf16[4,32,1152]{2,1,0:T(8,128)(2,1)S(1)} %get-tuple-element.40), channel_id=1, source_target_pairs={{0,2},{1,9},{2,4},{3,11},{4,6},{5,13},{6,0},{7,15},{8,10},{9,17},{... | collective-permute-start | bytes 884744 | tf_op jit(solution)/shard_map/ppermute | solution.py:30
  14.7 2.6 %shard_map.63 = (bf16[4,32,4608]{2,1,0:T(8,128)(2,1)S(1)}, bf16[4,32,4608]{2,1,0:T(8,128)(2,1)S(1)}) custom-call(s32[2]{0:T(128)S(1)} %bitcast.6, bf16[1024,5760]{1,0:T(8,128)(2,1)S(1)} %get-tuple-element.34.refs_1_, bf16[8,32,4608]{2,1,0:T(8,128)(2,1)S(1)} %collective-permute-done.4.refs_2_, f32[4,32,1152]{2,1,0:T(8,128)S(1)} %get-tuple-element.38.refs_3_.refs_0_), custom_call_target="tpu_custom_call" | custom-call | flops 1024 | bytes 1024 | tf_op jit(solution)/shard_map/pallas_call | solution.py:70
  17.3 2.1 %collective-permute-done.1.refs_2_.refs_1_ = bf16[4,32,1152]{2,1,0:T(8,128)(2,1)S(1)} collective-permute-done((bf16[4,32,1152]{2,1,0:T(8,128)(2,1)S(1)}, bf16[4,32,1152]{2,1,0:T(8,128)(2,1)S(1)}, u32[]{:S(2)}, u32[]{:S(2)}) %collective-permute-start.1) | collective-permute-done | bytes 294944 | tf_op jit(solution)/shard_map/ppermute | solution.py:30
  20.4 2.3 %collective-permute-done.3.refs_4_.refs_3_ = bf16[4,32,1152]{2,1,0:T(8,128)(2,1)S(1)} collective-permute-done((bf16[4,32,1152]{2,1,0:T(8,128)(2,1)S(1)}, bf16[4,32,1152]{2,1,0:T(8,128)(2,1)S(1)}, u32[]{:S(2)}, u32[]{:S(2)}) %collective-permute-start.3) | collective-permute-done | bytes 294944 | tf_op jit(solution)/shard_map/ppermute | solution.py:30
  23.1 1.5 %collective-permute-start.12 = (bf16[4,32,4608]{2,1,0:T(8,128)(2,1)S(1)}, bf16[4,32,4608]{2,1,0:T(8,128)(2,1)S(1)}, u32[]{:S(2)}, u32[]{:S(2)}) collective-permute-start(bf16[4,32,4608]{2,1,0:T(8,128)(2,1)S(1)} %get-tuple-element.56), channel_id=1, source_target_pairs={{0,6},{1,25},{2,0},{3,27},{4,2},{5,29},{6,4},{7,31},{8,14},{9,1},{... | collective-permute-start | bytes 3538952 | tf_op jit(solution)/shard_map/ppermute | solution.py:30
  24.8 3.3 %collective-permute-start.6 = (bf16[32,1152]{1,0:T(8,128)(2,1)S(1)}, bf16[32,1152]{1,0:T(8,128)(2,1)S(1)}, u32[]{:S(2)}, u32[]{:S(2)}) collective-permute-start(bf16[32,1152]{1,0:T(8,128)(2,1)S(1)} %get-tuple-element.47), channel_id=1, source_target_pairs={{0,16},{1,5},{2,18},{3,7},{4,20},{5,1},{6,22},{7,3},{8,24},{9,13},... | collective-permute-start | bytes 221192 | tf_op jit(solution)/shard_map/ppermute | solution.py:30
  28.8 2.6 %collective-permute-start.8 = (bf16[32,1152]{1,0:T(8,128)(2,1)S(1)}, bf16[32,1152]{1,0:T(8,128)(2,1)S(1)}, u32[]{:S(2)}, u32[]{:S(2)}) collective-permute-start(bf16[32,1152]{1,0:T(8,128)(2,1)S(1)} %get-tuple-element.49), channel_id=1, source_target_pairs={{0,24},{1,7},{2,26},{3,1},{4,28},{5,3},{6,30},{7,5},{8,0},{9,15},{... | collective-permute-start | bytes 221192 | tf_op jit(solution)/shard_map/ppermute | solution.py:30
  31.6 2.9 %collective-permute-done.7.refs_2_ = bf16[32,1152]{1,0:T(8,128)(2,1)S(1)} collective-permute-done((bf16[32,1152]{1,0:T(8,128)(2,1)S(1)}, bf16[32,1152]{1,0:T(8,128)(2,1)S(1)}, u32[]{:S(2)}, u32[]{:S(2)}) %collective-permute-start.7) | collective-permute-done | bytes 73760 | tf_op jit(solution)/shard_map/ppermute | solution.py:30
  34.5 2.2 %collective-permute-start.9 = (f32[32,640]{1,0:T(8,128)S(1)}, f32[32,640]{1,0:T(8,128)S(1)}, u32[]{:S(2)}, u32[]{:S(2)}) collective-permute-start(f32[32,640]{1,0:T(8,128)S(1)} %get-tuple-element.50.refs_2_.refs_3_), channel_id=1, source_target_pairs={{32,0},{64,32},{96,64},{128,96},{160,128},{192,160},{224,192},{33,... | collective-permute-start | bytes 245768 | tf_op jit(solution)/shard_map/ppermute | solution.py:55
  36.7 2.6 %shard_map.68 = (f32[4,32,4608]{2,1,0:T(8,128)S(1)}, f32[4,32,4608]{2,1,0:T(8,128)S(1)}) custom-call(s32[2]{0:T(128)S(1)} %bitcast.7, bf16[1024,5760]{1,0:T(8,128)(2,1)S(1)} %get-tuple-element.34.refs_1_, bf16[8,32,4608]{2,1,0:T(8,128)(2,1)S(1)} %collective-permute-done.5.refs_5_.refs_2_, f32[32,640]{1,0:T(8,128)S(1)} %get-tuple-element.50.refs_2_.refs_3_), custom_call_target="tpu_custom_call" | custom-call | flops 1024 | bytes 1024 | tf_op jit(solution)/shard_map/pallas_call | solution.py:70
  39.3 2.8 %collective-permute-done.9.refs_4_.refs_2_ = f32[32,640]{1,0:T(8,128)S(1)} collective-permute-done((f32[32,640]{1,0:T(8,128)S(1)}, f32[32,640]{1,0:T(8,128)S(1)}, u32[]{:S(2)}, u32[]{:S(2)}) %collective-permute-start.9) | collective-permute-done | bytes 81952 | tf_op jit(solution)/shard_map/ppermute | solution.py:55
  43.8 1.8 %collective-permute-start.13 = (bf16[2,32,4608]{2,1,0:T(8,128)(2,1)S(1)}, bf16[2,32,4608]{2,1,0:T(8,128)(2,1)S(1)}, u32[]{:S(2)}, u32[]{:S(2)}) collective-permute-start(bf16[2,32,4608]{2,1,0:T(8,128)(2,1)S(1)} %get-tuple-element.58), channel_id=1, source_target_pairs={{0,2},{1,9},{2,4},{3,11},{4,6},{5,13},{6,0},{7,15},{8,10},{9,17},{... | collective-permute-start | bytes 1769480 | tf_op jit(solution)/shard_map/ppermute | solution.py:30
  47.1 1.4 %collective-permute-start.16 = (f32[8,128]{1,0:T(8,128)S(1)}, f32[8,128]{1,0:T(8,128)S(1)}, u32[]{:S(2)}, u32[]{:S(2)}) collective-permute-start(f32[8,128]{1,0:T(8,128)S(1)} %add.3.refs_5_), channel_id=1, source_target_pairs={{0,4},{1,17},{2,6},{3,19},{4,0},{5,21},{6,2},{7,23},{8,12},{9,25},... | collective-permute-start | bytes 12296 | tf_op jit(solution)/shard_map/ppermute | solution.py:30
  48.5 1.5 %collective-permute-start.17 = (f32[8,128]{1,0:T(8,128)S(1)}, f32[8,128]{1,0:T(8,128)S(1)}, u32[]{:S(2)}, u32[]{:S(2)}) collective-permute-start(f32[8,128]{1,0:T(8,128)S(1)} %add.3.refs_5_), channel_id=1, source_target_pairs={{0,2},{1,9},{2,4},{3,11},{4,6},{5,13},{6,0},{7,15},{8,10},{9,17},{... | collective-permute-start | bytes 12296 | tf_op jit(solution)/shard_map/ppermute | solution.py:30
  50.9 4.5 %collective-permute-done.16.refs_6_ = f32[8,128]{1,0:T(8,128)S(1)} collective-permute-done((f32[8,128]{1,0:T(8,128)S(1)}, f32[8,128]{1,0:T(8,128)S(1)}, u32[]{:S(2)}, u32[]{:S(2)}) %collective-permute-start.16) | collective-permute-done | bytes 4128 | tf_op jit(solution)/shard_map/ppermute | solution.py:30
  55.3 1.4 %collective-permute-done.18.refs_8_ = f32[8,128]{1,0:T(8,128)S(1)} collective-permute-done((f32[8,128]{1,0:T(8,128)S(1)}, f32[8,128]{1,0:T(8,128)S(1)}, u32[]{:S(2)}, u32[]{:S(2)}) %collective-permute-start.18) | collective-permute-done | bytes 4128 | tf_op jit(solution)/shard_map/ppermute | solution.py:30
  57.2 1.5 %collective-permute-start.19 = (bf16[32,4736]{1,0:T(8,128)(2,1)S(1)}, bf16[32,4736]{1,0:T(8,128)(2,1)S(1)}, u32[]{:S(2)}, u32[]{:S(2)}) collective-permute-start(bf16[32,4736]{1,0:T(8,128)(2,1)S(1)} %get-tuple-element.61), channel_id=1, source_target_pairs={{0,16},{1,5},{2,18},{3,7},{4,20},{5,1},{6,22},{7,3},{8,24},{9,13},... | collective-permute-start | bytes 909320 | tf_op jit(solution)/shard_map/ppermute | solution.py:30
  58.8 2.6 %collective-permute-start.20 = (bf16[32,4736]{1,0:T(8,128)(2,1)S(1)}, bf16[32,4736]{1,0:T(8,128)(2,1)S(1)}, u32[]{:S(2)}, u32[]{:S(2)}) collective-permute-start(bf16[32,4736]{1,0:T(8,128)(2,1)S(1)} %get-tuple-element.62), channel_id=1, source_target_pairs={{0,8},{1,3},{2,10},{3,5},{4,12},{5,7},{6,14},{7,1},{8,16},{9,11},{... | collective-permute-start | bytes 909320 | tf_op jit(solution)/shard_map/ppermute | solution.py:30
  62.0 3.8 %collective-permute-start.10 = (bf16[32,512]{1,0:T(8,128)(2,1)S(1)}, bf16[32,512]{1,0:T(8,128)(2,1)S(1)}, u32[]{:S(2)}, u32[]{:S(2)}) collective-permute-start(bf16[32,512]{1,0:T(8,128)(2,1)S(1)} %get-tuple-element.52), channel_id=1, source_target_pairs={{0,32},{32,64},{64,96},{96,128},{128,160},{160,192},{192,224},{1,3... | collective-permute-start | bytes 98312 | tf_op jit(solution)/shard_map/ppermute | solution.py:55
  65.8 2.0 %collective-permute-done.10.refs_5_ = bf16[32,512]{1,0:T(8,128)(2,1)S(1)} collective-permute-done((bf16[32,512]{1,0:T(8,128)(2,1)S(1)}, bf16[32,512]{1,0:T(8,128)(2,1)S(1)}, u32[]{:S(2)}, u32[]{:S(2)}) %collective-permute-start.10) | collective-permute-done | bytes 32800 | tf_op jit(solution)/shard_map/ppermute | solution.py:55
  (41 shorter events, 12.0 us)
Async XLA Ops:
  6.1 2.9 %collective-permute-start = (bf16[16,32,1152]{2,1,0:T(8,128)(2,1)S(1)}, bf16[16,32,1152]{2,1,0:T(8,128)(2,1)S(1)}, u32[]{:S(2)}, u32[]{:S(2)}) collective-permute-start(bf16[16,32,1152]{2,1,0:T(8,128)(2,1)S(1)} %get-tuple-element.35.refs_3_), channel_id=1, source_target_pairs={{0,1},{1,0},{2,3},{3,2},{4,5},{5,4},{6,7},{7,6},{8,9},{9,8},{10,11... | collective-permute-start | bytes 3538952 | tf_op jit(solution)/shard_map/ppermute | solution.py:30
  9.1 5.6 %collective-permute-start.4 = (bf16[8,32,4608]{2,1,0:T(8,128)(2,1)S(1)}, bf16[8,32,4608]{2,1,0:T(8,128)(2,1)S(1)}, u32[]{:S(2)}, u32[]{:S(2)}) collective-permute-start(bf16[8,32,4608]{2,1,0:T(8,128)(2,1)S(1)} %shard_map.62), channel_id=1, source_target_pairs={{0,1},{1,0},{2,3},{3,2},{4,5},{5,4},{6,7},{7,6},{8,9},{9,8},{10,11... | collective-permute-start | bytes 7077896 | tf_op jit(solution)/shard_map/ppermute | solution.py:30
  9.2 15.5 %collective-permute-start.5 = (bf16[8,32,4608]{2,1,0:T(8,128)(2,1)S(1)}, bf16[8,32,4608]{2,1,0:T(8,128)(2,1)S(1)}, u32[]{:S(2)}, u32[]{:S(2)}) collective-permute-start(bf16[8,32,4608]{2,1,0:T(8,128)(2,1)S(1)} %get-tuple-element.37.refs_3_), channel_id=1, source_target_pairs={{0,1},{1,0},{2,3},{3,2},{4,5},{5,4},{6,7},{7,6},{8,9},{9,8},{10,11... | collective-permute-start | bytes 7077896 | tf_op jit(solution)/shard_map/ppermute | solution.py:30
  11.1 8.3 %collective-permute-start.1 = (bf16[4,32,1152]{2,1,0:T(8,128)(2,1)S(1)}, bf16[4,32,1152]{2,1,0:T(8,128)(2,1)S(1)}, u32[]{:S(2)}, u32[]{:S(2)}) collective-permute-start(bf16[4,32,1152]{2,1,0:T(8,128)(2,1)S(1)} %get-tuple-element.39), channel_id=1, source_target_pairs={{0,4},{1,17},{2,6},{3,19},{4,0},{5,21},{6,2},{7,23},{8,12},{9,25},... | collective-permute-start | bytes 884744 | tf_op jit(solution)/shard_map/ppermute | solution.py:30
  12.6 7.8 %collective-permute-start.2 = (bf16[4,32,1152]{2,1,0:T(8,128)(2,1)S(1)}, bf16[4,32,1152]{2,1,0:T(8,128)(2,1)S(1)}, u32[]{:S(2)}, u32[]{:S(2)}) collective-permute-start(bf16[4,32,1152]{2,1,0:T(8,128)(2,1)S(1)} %get-tuple-element.40), channel_id=1, source_target_pairs={{0,2},{1,9},{2,4},{3,11},{4,6},{5,13},{6,0},{7,15},{8,10},{9,17},{... | collective-permute-start | bytes 884744 | tf_op jit(solution)/shard_map/ppermute | solution.py:30
  14.7 7.9 %collective-permute-start.3 = (bf16[4,32,1152]{2,1,0:T(8,128)(2,1)S(1)}, bf16[4,32,1152]{2,1,0:T(8,128)(2,1)S(1)}, u32[]{:S(2)}, u32[]{:S(2)}) collective-permute-start(bf16[4,32,1152]{2,1,0:T(8,128)(2,1)S(1)} %get-tuple-element.41), channel_id=1, source_target_pairs={{0,6},{1,25},{2,0},{3,27},{4,2},{5,29},{6,4},{7,31},{8,14},{9,1},{... | collective-permute-start | bytes 884744 | tf_op jit(solution)/shard_map/ppermute | solution.py:30
  22.6 20.8 %collective-permute-start.11 = (bf16[4,32,4608]{2,1,0:T(8,128)(2,1)S(1)}, bf16[4,32,4608]{2,1,0:T(8,128)(2,1)S(1)}, u32[]{:S(2)}, u32[]{:S(2)}) collective-permute-start(bf16[4,32,4608]{2,1,0:T(8,128)(2,1)S(1)} %get-tuple-element.45.refs_4_), channel_id=1, source_target_pairs={{0,2},{1,9},{2,4},{3,11},{4,6},{5,13},{6,0},{7,15},{8,10},{9,17},{... | collective-permute-start | bytes 3538952 | tf_op jit(solution)/shard_map/ppermute | solution.py:30
  23.1 20.3 %collective-permute-start.12 = (bf16[4,32,4608]{2,1,0:T(8,128)(2,1)S(1)}, bf16[4,32,4608]{2,1,0:T(8,128)(2,1)S(1)}, u32[]{:S(2)}, u32[]{:S(2)}) collective-permute-start(bf16[4,32,4608]{2,1,0:T(8,128)(2,1)S(1)} %get-tuple-element.56), channel_id=1, source_target_pairs={{0,6},{1,25},{2,0},{3,27},{4,2},{5,29},{6,4},{7,31},{8,14},{9,1},{... | collective-permute-start | bytes 3538952 | tf_op jit(solution)/shard_map/ppermute | solution.py:30
  24.8 6.8 %collective-permute-start.6 = (bf16[32,1152]{1,0:T(8,128)(2,1)S(1)}, bf16[32,1152]{1,0:T(8,128)(2,1)S(1)}, u32[]{:S(2)}, u32[]{:S(2)}) collective-permute-start(bf16[32,1152]{1,0:T(8,128)(2,1)S(1)} %get-tuple-element.47), channel_id=1, source_target_pairs={{0,16},{1,5},{2,18},{3,7},{4,20},{5,1},{6,22},{7,3},{8,24},{9,13},... | collective-permute-start | bytes 221192 | tf_op jit(solution)/shard_map/ppermute | solution.py:30
  28.1 6.4 %collective-permute-start.7 = (bf16[32,1152]{1,0:T(8,128)(2,1)S(1)}, bf16[32,1152]{1,0:T(8,128)(2,1)S(1)}, u32[]{:S(2)}, u32[]{:S(2)}) collective-permute-start(bf16[32,1152]{1,0:T(8,128)(2,1)S(1)} %get-tuple-element.48), channel_id=1, source_target_pairs={{0,8},{1,3},{2,10},{3,5},{4,12},{5,7},{6,14},{7,1},{8,16},{9,11},{... | collective-permute-start | bytes 221192 | tf_op jit(solution)/shard_map/ppermute | solution.py:30
  28.8 5.7 %collective-permute-start.8 = (bf16[32,1152]{1,0:T(8,128)(2,1)S(1)}, bf16[32,1152]{1,0:T(8,128)(2,1)S(1)}, u32[]{:S(2)}, u32[]{:S(2)}) collective-permute-start(bf16[32,1152]{1,0:T(8,128)(2,1)S(1)} %get-tuple-element.49), channel_id=1, source_target_pairs={{0,24},{1,7},{2,26},{3,1},{4,28},{5,3},{6,30},{7,5},{8,0},{9,15},{... | collective-permute-start | bytes 221192 | tf_op jit(solution)/shard_map/ppermute | solution.py:30
  34.5 7.6 %copy-start.1 = (s32[8]{0:T(128)S(1)}, s32[8]{0:T(128)}, u32[]{:S(2)}) copy-start(s32[8]{0:T(128)} %refs_0_.3) | copy-start | bytes 100
  34.5 7.5 %collective-permute-start.9 = (f32[32,640]{1,0:T(8,128)S(1)}, f32[32,640]{1,0:T(8,128)S(1)}, u32[]{:S(2)}, u32[]{:S(2)}) collective-permute-start(f32[32,640]{1,0:T(8,128)S(1)} %get-tuple-element.50.refs_2_.refs_3_), channel_id=1, source_target_pairs={{32,0},{64,32},{96,64},{128,96},{160,128},{192,160},{224,192},{33,... | collective-permute-start | bytes 245768 | tf_op jit(solution)/shard_map/ppermute | solution.py:55
  43.8 13.0 %collective-permute-start.13 = (bf16[2,32,4608]{2,1,0:T(8,128)(2,1)S(1)}, bf16[2,32,4608]{2,1,0:T(8,128)(2,1)S(1)}, u32[]{:S(2)}, u32[]{:S(2)}) collective-permute-start(bf16[2,32,4608]{2,1,0:T(8,128)(2,1)S(1)} %get-tuple-element.58), channel_id=1, source_target_pairs={{0,2},{1,9},{2,4},{3,11},{4,6},{5,13},{6,0},{7,15},{8,10},{9,17},{... | collective-permute-start | bytes 1769480 | tf_op jit(solution)/shard_map/ppermute | solution.py:30
  45.6 11.2 %collective-permute-start.14 = (bf16[2,32,4608]{2,1,0:T(8,128)(2,1)S(1)}, bf16[2,32,4608]{2,1,0:T(8,128)(2,1)S(1)}, u32[]{:S(2)}, u32[]{:S(2)}) collective-permute-start(bf16[2,32,4608]{2,1,0:T(8,128)(2,1)S(1)} %get-tuple-element.59), channel_id=1, source_target_pairs={{0,6},{1,25},{2,0},{3,27},{4,2},{5,29},{6,4},{7,31},{8,14},{9,1},{... | collective-permute-start | bytes 1769480 | tf_op jit(solution)/shard_map/ppermute | solution.py:30
  45.9 1.2 %collective-permute-start.15 = (f32[8,128]{1,0:T(8,128)S(1)}, f32[8,128]{1,0:T(8,128)S(1)}, u32[]{:S(2)}, u32[]{:S(2)}) collective-permute-start(f32[8,128]{1,0:T(8,128)S(1)} %shard_map.69.refs_3_), channel_id=1, source_target_pairs={{0,1},{1,0},{2,3},{3,2},{4,5},{5,4},{6,7},{7,6},{8,9},{9,8},{10,11... | collective-permute-start | bytes 12296 | tf_op jit(solution)/shard_map/ppermute | solution.py:30
  47.1 8.3 %collective-permute-start.16 = (f32[8,128]{1,0:T(8,128)S(1)}, f32[8,128]{1,0:T(8,128)S(1)}, u32[]{:S(2)}, u32[]{:S(2)}) collective-permute-start(f32[8,128]{1,0:T(8,128)S(1)} %add.3.refs_5_), channel_id=1, source_target_pairs={{0,4},{1,17},{2,6},{3,19},{4,0},{5,21},{6,2},{7,23},{8,12},{9,25},... | collective-permute-start | bytes 12296 | tf_op jit(solution)/shard_map/ppermute | solution.py:30
  48.5 6.8 %collective-permute-start.17 = (f32[8,128]{1,0:T(8,128)S(1)}, f32[8,128]{1,0:T(8,128)S(1)}, u32[]{:S(2)}, u32[]{:S(2)}) collective-permute-start(f32[8,128]{1,0:T(8,128)S(1)} %add.3.refs_5_), channel_id=1, source_target_pairs={{0,2},{1,9},{2,4},{3,11},{4,6},{5,13},{6,0},{7,15},{8,10},{9,17},{... | collective-permute-start | bytes 12296 | tf_op jit(solution)/shard_map/ppermute | solution.py:30
  50.0 6.8 %collective-permute-start.18 = (f32[8,128]{1,0:T(8,128)S(1)}, f32[8,128]{1,0:T(8,128)S(1)}, u32[]{:S(2)}, u32[]{:S(2)}) collective-permute-start(f32[8,128]{1,0:T(8,128)S(1)} %add.3.refs_5_), channel_id=1, source_target_pairs={{0,6},{1,25},{2,0},{3,27},{4,2},{5,29},{6,4},{7,31},{8,14},{9,1},{... | collective-permute-start | bytes 12296 | tf_op jit(solution)/shard_map/ppermute | solution.py:30
  56.8 11.0 %copy-start.2 = (s32[8]{0:T(128)S(1)}, s32[8]{0:T(128)}, u32[]{:S(2)}) copy-start(s32[8]{0:T(128)} %refs_1_.1) | copy-start | bytes 100
  57.2 11.3 %collective-permute-start.19 = (bf16[32,4736]{1,0:T(8,128)(2,1)S(1)}, bf16[32,4736]{1,0:T(8,128)(2,1)S(1)}, u32[]{:S(2)}, u32[]{:S(2)}) collective-permute-start(bf16[32,4736]{1,0:T(8,128)(2,1)S(1)} %get-tuple-element.61), channel_id=1, source_target_pairs={{0,16},{1,5},{2,18},{3,7},{4,20},{5,1},{6,22},{7,3},{8,24},{9,13},... | collective-permute-start | bytes 909320 | tf_op jit(solution)/shard_map/ppermute | solution.py:30
  58.8 10.1 %collective-permute-start.20 = (bf16[32,4736]{1,0:T(8,128)(2,1)S(1)}, bf16[32,4736]{1,0:T(8,128)(2,1)S(1)}, u32[]{:S(2)}, u32[]{:S(2)}) collective-permute-start(bf16[32,4736]{1,0:T(8,128)(2,1)S(1)} %get-tuple-element.62), channel_id=1, source_target_pairs={{0,8},{1,3},{2,10},{3,5},{4,12},{5,7},{6,14},{7,1},{8,16},{9,11},{... | collective-permute-start | bytes 909320 | tf_op jit(solution)/shard_map/ppermute | solution.py:30
  61.4 8.1 %collective-permute-start.21 = (bf16[32,4736]{1,0:T(8,128)(2,1)S(1)}, bf16[32,4736]{1,0:T(8,128)(2,1)S(1)}, u32[]{:S(2)}, u32[]{:S(2)}) collective-permute-start(bf16[32,4736]{1,0:T(8,128)(2,1)S(1)} %get-tuple-element.63), channel_id=1, source_target_pairs={{0,24},{1,7},{2,26},{3,1},{4,28},{5,3},{6,30},{7,5},{8,0},{9,15},{... | collective-permute-start | bytes 909320 | tf_op jit(solution)/shard_map/ppermute | solution.py:30
  62.0 5.8 %collective-permute-start.10 = (bf16[32,512]{1,0:T(8,128)(2,1)S(1)}, bf16[32,512]{1,0:T(8,128)(2,1)S(1)}, u32[]{:S(2)}, u32[]{:S(2)}) collective-permute-start(bf16[32,512]{1,0:T(8,128)(2,1)S(1)} %get-tuple-element.52), channel_id=1, source_target_pairs={{0,32},{32,64},{64,96},{96,128},{128,160},{160,192},{192,224},{1,3... | collective-permute-start | bytes 98312 | tf_op jit(solution)/shard_map/ppermute | solution.py:55
  (1 other events, 0.7 us)

commit v6 on v5

--- a/solution.py
+++ b/solution.py
@@ -489,7 +489,7 @@
     low, high = EDGE + LANES, cols - STRIP - LANES
     places = [(0, 0, EDGE), (0, cols - STRIP, STRIP)]
     ninth = (cols - STRIP - EDGE) // 9 // LANES * LANES
-    cuts = [EDGE, EDGE + 4 * ninth, EDGE + 7 * ninth, cols - STRIP]
+    cuts = [EDGE, EDGE + 4 * ninth, EDGE + 6 * ninth, cols - STRIP]
     frame, theirs_s, theirs_m = Columns(moves, rows, cols, [], places).loaded(
         frame, low, high, list(zip(cuts[:-1], cuts[1:]))
     )

time: 70.5 us -> 70.4 us (level)
  no operation moved by 1% of the time
where the time goes in v6:
time: 70.4 us; the launch traced here: 70.2 us
  starting transfers between devices  29.4 us (42%)
  waiting for transfers between devices  21.8 us (31%)
  Pallas kernels  17.6 us (25%)
  between operations  0.76 us (1%)
    ppermute x20, starting transfers between devices, permuted(): lax.ppermute(array, 'frame', [(device_at(*place), device_at(*target(*plac...  23.4 us
    ppermute x20, waiting for transfers between devices, permuted(): lax.ppermute(array, 'frame', [(device_at(*place), device_at(*target(*plac...  17 us
    pallas_call x11, Pallas kernels, call(): pl.pallas_call(run, in_specs=[pl.BlockSpec(memory_space=pltpu.SMEM)] * le...  12.9 us
    ppermute x2, starting transfers between devices, from_behind(): return lax.ppermute(array, axis, pairs)  6 us
    ppermute x2, waiting for transfers between devices, from_behind(): return lax.ppermute(array, axis, pairs)  4.76 us
    pallas_call x1, Pallas kernels, loaded(): pl.pallas_call(kernel, in_specs=[far, far], out_specs=[vmem, vmem, vmem],...  4.7 us
  transfers between devices with their start and end apart: 22, of which 13 were waited for; matrix products, arithmetic and copies ran while one was open for 0% of the time, Pallas kernels for 16%

profile of v6, /device:TPU:102, one launch (start us, length us, event | category | flops | bytes accessed | tf_op | source)
XLA Modules:
  0.0 70.2 jit_solution(14617617021506143824)
XLA Ops:
  1.3 4.7 %shard_map.59 = (bf16[1024,5760]{1,0:T(8,128)(2,1)S(1)}, bf16[16,32,1152]{2,1,0:T(8,128)(2,1)S(1)}, bf16[8,32,4608]{2,1,0:T(8,128)(2,1)S(1)}) custom-call(s32[2]{0:T(128)S(1)} %bitcast.3, bf16[1024,5760]{1,0:T(8,128)(2,1)} %bitcast.8), custom_call_target="tpu_custom_call" | custom-call | flops 1024 | bytes 1024 | tf_op jit(solution)/shard_map/pallas_call | solution.py:276
  6.1 2.4 %shard_map.60 = (bf16[8,32,4608]{2,1,0:T(8,128)(2,1)S(1)}, bf16[8,32,4608]{2,1,0:T(8,128)(2,1)S(1)}) custom-call(s32[2]{0:T(128)S(1)} %bitcast.4, bf16[1024,5760]{1,0:T(8,128)(2,1)S(1)} %get-tuple-element.34.refs_1_, bf16[8,32,4608]{2,1,0:T(8,128)(2,1)S(1)} %get-tuple-element.36.refs_2_, ...), custom_call_target="tpu_custom_call", output_to_operand_aliasing={{1}: (2, {})} | custom-call | flops 1024 | bytes 1024 | tf_op jit(solution)/shard_map/pallas_call | solution.py:70
  9.4 1.5 %shard_map.61 = (f32[4,32,1152]{2,1,0:T(8,128)S(1)}, bf16[4,32,1152]{2,1,0:T(8,128)(2,1)S(1)}, bf16[4,32,1152]{2,1,0:T(8,128)(2,1)S(1)}, bf16[4,32,1152]{2,1,0:T(8,128)(2,1)S(1)}) custom-call(s32[2]{0:T(128)S(1)} %bitcast.5, bf16[1024,5760]{1,0:T(8,128)(2,1)S(1)} %get-tuple-element.34.refs_1_, ...), custom_call_target="tpu_custom_call" | custom-call | flops 1024 | bytes 1024 | tf_op jit(solution)/shard_map/pallas_call | solution.py:70
  11.0 1.5 %collective-permute-start.1 = (bf16[4,32,1152]{2,1,0:T(8,128)(2,1)S(1)}, bf16[4,32,1152]{2,1,0:T(8,128)(2,1)S(1)}, u32[]{:S(2)}, u32[]{:S(2)}) collective-permute-start(bf16[4,32,1152]{2,1,0:T(8,128)(2,1)S(1)} %get-tuple-element.39), channel_id=1, source_target_pairs={{0,4},{1,17},{2,6},{3,19},{4,0},{5,21},{6,2},{7,23},{8,12},{9,25},... | collective-permute-start | bytes 884744 | tf_op jit(solution)/shard_map/ppermute | solution.py:30
  12.4 2.1 %collective-permute-start.2 = (bf16[4,32,1152]{2,1,0:T(8,128)(2,1)S(1)}, bf16[4,32,1152]{2,1,0:T(8,128)(2,1)S(1)}, u32[]{:S(2)}, u32[]{:S(2)}) collective-permute-start(bf16[4,32,1152]{2,1,0:T(8,128)(2,1)S(1)} %get-tuple-element.40), channel_id=1, source_target_pairs={{0,2},{1,9},{2,4},{3,11},{4,6},{5,13},{6,0},{7,15},{8,10},{9,17},{... | collective-permute-start | bytes 884744 | tf_op jit(solution)/shard_map/ppermute | solution.py:30
  14.5 2.6 %shard_map.63 = (bf16[4,32,4608]{2,1,0:T(8,128)(2,1)S(1)}, bf16[4,32,4608]{2,1,0:T(8,128)(2,1)S(1)}) custom-call(s32[2]{0:T(128)S(1)} %bitcast.6, bf16[1024,5760]{1,0:T(8,128)(2,1)S(1)} %get-tuple-element.34.refs_1_, bf16[8,32,4608]{2,1,0:T(8,128)(2,1)S(1)} %collective-permute-done.4.refs_2_, f32[4,32,1152]{2,1,0:T(8,128)S(1)} %get-tuple-element.38.refs_3_.refs_0_), custom_call_target="tpu_custom_call" | custom-call | flops 1024 | bytes 1024 | tf_op jit(solution)/shard_map/pallas_call | solution.py:70
  17.1 2.2 %collective-permute-done.1.refs_2_.refs_1_ = bf16[4,32,1152]{2,1,0:T(8,128)(2,1)S(1)} collective-permute-done((bf16[4,32,1152]{2,1,0:T(8,128)(2,1)S(1)}, bf16[4,32,1152]{2,1,0:T(8,128)(2,1)S(1)}, u32[]{:S(2)}, u32[]{:S(2)}) %collective-permute-start.1) | collective-permute-done | bytes 294944 | tf_op jit(solution)/shard_map/ppermute | solution.py:30
  20.2 2.2 %collective-permute-done.3.refs_4_.refs_3_ = bf16[4,32,1152]{2,1,0:T(8,128)(2,1)S(1)} collective-permute-done((bf16[4,32,1152]{2,1,0:T(8,128)(2,1)S(1)}, bf16[4,32,1152]{2,1,0:T(8,128)(2,1)S(1)}, u32[]{:S(2)}, u32[]{:S(2)}) %collective-permute-start.3) | collective-permute-done | bytes 294944 | tf_op jit(solution)/shard_map/ppermute | solution.py:30
  23.0 1.5 %collective-permute-start.12 = (bf16[4,32,4608]{2,1,0:T(8,128)(2,1)S(1)}, bf16[4,32,4608]{2,1,0:T(8,128)(2,1)S(1)}, u32[]{:S(2)}, u32[]{:S(2)}) collective-permute-start(bf16[4,32,4608]{2,1,0:T(8,128)(2,1)S(1)} %get-tuple-element.56), channel_id=1, source_target_pairs={{0,6},{1,25},{2,0},{3,27},{4,2},{5,29},{6,4},{7,31},{8,14},{9,1},{... | collective-permute-start | bytes 3538952 | tf_op jit(solution)/shard_map/ppermute | solution.py:30
  24.6 3.3 %collective-permute-start.6 = (bf16[32,1152]{1,0:T(8,128)(2,1)S(1)}, bf16[32,1152]{1,0:T(8,128)(2,1)S(1)}, u32[]{:S(2)}, u32[]{:S(2)}) collective-permute-start(bf16[32,1152]{1,0:T(8,128)(2,1)S(1)} %get-tuple-element.47), channel_id=1, source_target_pairs={{0,16},{1,5},{2,18},{3,7},{4,20},{5,1},{6,22},{7,3},{8,24},{9,13},... | collective-permute-start | bytes 221192 | tf_op jit(solution)/shard_map/ppermute | solution.py:30
  28.6 2.5 %collective-permute-start.8 = (bf16[32,1152]{1,0:T(8,128)(2,1)S(1)}, bf16[32,1152]{1,0:T(8,128)(2,1)S(1)}, u32[]{:S(2)}, u32[]{:S(2)}) collective-permute-start(bf16[32,1152]{1,0:T(8,128)(2,1)S(1)} %get-tuple-element.49), channel_id=1, source_target_pairs={{0,24},{1,7},{2,26},{3,1},{4,28},{5,3},{6,30},{7,5},{8,0},{9,15},{... | collective-permute-start | bytes 221192 | tf_op jit(solution)/shard_map/ppermute | solution.py:30
  31.4 2.9 %collective-permute-done.7.refs_2_ = bf16[32,1152]{1,0:T(8,128)(2,1)S(1)} collective-permute-done((bf16[32,1152]{1,0:T(8,128)(2,1)S(1)}, bf16[32,1152]{1,0:T(8,128)(2,1)S(1)}, u32[]{:S(2)}, u32[]{:S(2)}) %collective-permute-start.7) | collective-permute-done | bytes 73760 | tf_op jit(solution)/shard_map/ppermute | solution.py:30
  34.4 2.2 %collective-permute-start.9 = (f32[32,640]{1,0:T(8,128)S(1)}, f32[32,640]{1,0:T(8,128)S(1)}, u32[]{:S(2)}, u32[]{:S(2)}) collective-permute-start(f32[32,640]{1,0:T(8,128)S(1)} %get-tuple-element.50.refs_2_.refs_3_), channel_id=1, source_target_pairs={{32,0},{64,32},{96,64},{128,96},{160,128},{192,160},{224,192},{33,... | collective-permute-start | bytes 245768 | tf_op jit(solution)/shard_map/ppermute | solution.py:55
  36.6 2.6 %shard_map.68 = (f32[4,32,4608]{2,1,0:T(8,128)S(1)}, f32[4,32,4608]{2,1,0:T(8,128)S(1)}) custom-call(s32[2]{0:T(128)S(1)} %bitcast.7, bf16[1024,5760]{1,0:T(8,128)(2,1)S(1)} %get-tuple-element.34.refs_1_, bf16[8,32,4608]{2,1,0:T(8,128)(2,1)S(1)} %collective-permute-done.5.refs_5_.refs_2_, f32[32,640]{1,0:T(8,128)S(1)} %get-tuple-element.50.refs_2_.refs_3_), custom_call_target="tpu_custom_call" | custom-call | flops 1024 | bytes 1024 | tf_op jit(solution)/shard_map/pallas_call | solution.py:70
  39.2 2.8 %collective-permute-done.9.refs_4_.refs_2_ = f32[32,640]{1,0:T(8,128)S(1)} collective-permute-done((f32[32,640]{1,0:T(8,128)S(1)}, f32[32,640]{1,0:T(8,128)S(1)}, u32[]{:S(2)}, u32[]{:S(2)}) %collective-permute-start.9) | collective-permute-done | bytes 81952 | tf_op jit(solution)/shard_map/ppermute | solution.py:55
  43.6 1.8 %collective-permute-start.13 = (bf16[2,32,4608]{2,1,0:T(8,128)(2,1)S(1)}, bf16[2,32,4608]{2,1,0:T(8,128)(2,1)S(1)}, u32[]{:S(2)}, u32[]{:S(2)}) collective-permute-start(bf16[2,32,4608]{2,1,0:T(8,128)(2,1)S(1)} %get-tuple-element.58), channel_id=1, source_target_pairs={{0,2},{1,9},{2,4},{3,11},{4,6},{5,13},{6,0},{7,15},{8,10},{9,17},{... | collective-permute-start | bytes 1769480 | tf_op jit(solution)/shard_map/ppermute | solution.py:30
  46.9 1.4 %collective-permute-start.16 = (f32[8,128]{1,0:T(8,128)S(1)}, f32[8,128]{1,0:T(8,128)S(1)}, u32[]{:S(2)}, u32[]{:S(2)}) collective-permute-start(f32[8,128]{1,0:T(8,128)S(1)} %add.3.refs_5_), channel_id=1, source_target_pairs={{0,4},{1,17},{2,6},{3,19},{4,0},{5,21},{6,2},{7,23},{8,12},{9,25},... | collective-permute-start | bytes 12296 | tf_op jit(solution)/shard_map/ppermute | solution.py:30
  48.3 1.5 %collective-permute-start.17 = (f32[8,128]{1,0:T(8,128)S(1)}, f32[8,128]{1,0:T(8,128)S(1)}, u32[]{:S(2)}, u32[]{:S(2)}) collective-permute-start(f32[8,128]{1,0:T(8,128)S(1)} %add.3.refs_5_), channel_id=1, source_target_pairs={{0,2},{1,9},{2,4},{3,11},{4,6},{5,13},{6,0},{7,15},{8,10},{9,17},{... | collective-permute-start | bytes 12296 | tf_op jit(solution)/shard_map/ppermute | solution.py:30
  50.7 4.4 %collective-permute-done.16.refs_6_ = f32[8,128]{1,0:T(8,128)S(1)} collective-permute-done((f32[8,128]{1,0:T(8,128)S(1)}, f32[8,128]{1,0:T(8,128)S(1)}, u32[]{:S(2)}, u32[]{:S(2)}) %collective-permute-start.16) | collective-permute-done | bytes 4128 | tf_op jit(solution)/shard_map/ppermute | solution.py:30
  55.1 1.5 %collective-permute-done.18.refs_8_ = f32[8,128]{1,0:T(8,128)S(1)} collective-permute-done((f32[8,128]{1,0:T(8,128)S(1)}, f32[8,128]{1,0:T(8,128)S(1)}, u32[]{:S(2)}, u32[]{:S(2)}) %collective-permute-start.18) | collective-permute-done | bytes 4128 | tf_op jit(solution)/shard_map/ppermute | solution.py:30
  57.1 1.5 %collective-permute-start.19 = (bf16[32,4736]{1,0:T(8,128)(2,1)S(1)}, bf16[32,4736]{1,0:T(8,128)(2,1)S(1)}, u32[]{:S(2)}, u32[]{:S(2)}) collective-permute-start(bf16[32,4736]{1,0:T(8,128)(2,1)S(1)} %get-tuple-element.61), channel_id=1, source_target_pairs={{0,16},{1,5},{2,18},{3,7},{4,20},{5,1},{6,22},{7,3},{8,24},{9,13},... | collective-permute-start | bytes 909320 | tf_op jit(solution)/shard_map/ppermute | solution.py:30
  58.6 2.6 %collective-permute-start.20 = (bf16[32,4736]{1,0:T(8,128)(2,1)S(1)}, bf16[32,4736]{1,0:T(8,128)(2,1)S(1)}, u32[]{:S(2)}, u32[]{:S(2)}) collective-permute-start(bf16[32,4736]{1,0:T(8,128)(2,1)S(1)} %get-tuple-element.62), channel_id=1, source_target_pairs={{0,8},{1,3},{2,10},{3,5},{4,12},{5,7},{6,14},{7,1},{8,16},{9,11},{... | collective-permute-start | bytes 909320 | tf_op jit(solution)/shard_map/ppermute | solution.py:30
  61.8 3.8 %collective-permute-start.10 = (bf16[32,512]{1,0:T(8,128)(2,1)S(1)}, bf16[32,512]{1,0:T(8,128)(2,1)S(1)}, u32[]{:S(2)}, u32[]{:S(2)}) collective-permute-start(bf16[32,512]{1,0:T(8,128)(2,1)S(1)} %get-tuple-element.52), channel_id=1, source_target_pairs={{0,32},{32,64},{64,96},{96,128},{128,160},{160,192},{192,224},{1,3... | collective-permute-start | bytes 98312 | tf_op jit(solution)/shard_map/ppermute | solution.py:55
  65.6 2.0 %collective-permute-done.10.refs_5_ = bf16[32,512]{1,0:T(8,128)(2,1)S(1)} collective-permute-done((bf16[32,512]{1,0:T(8,128)(2,1)S(1)}, bf16[32,512]{1,0:T(8,128)(2,1)S(1)}, u32[]{:S(2)}, u32[]{:S(2)}) %collective-permute-start.10) | collective-permute-done | bytes 32800 | tf_op jit(solution)/shard_map/ppermute | solution.py:55
  (41 shorter events, 11.9 us)
Async XLA Ops:
  6.0 2.9 %collective-permute-start = (bf16[16,32,1152]{2,1,0:T(8,128)(2,1)S(1)}, bf16[16,32,1152]{2,1,0:T(8,128)(2,1)S(1)}, u32[]{:S(2)}, u32[]{:S(2)}) collective-permute-start(bf16[16,32,1152]{2,1,0:T(8,128)(2,1)S(1)} %get-tuple-element.35.refs_3_), channel_id=1, source_target_pairs={{0,1},{1,0},{2,3},{3,2},{4,5},{5,4},{6,7},{7,6},{8,9},{9,8},{10,11... | collective-permute-start | bytes 3538952 | tf_op jit(solution)/shard_map/ppermute | solution.py:30
  8.9 5.6 %collective-permute-start.4 = (bf16[8,32,4608]{2,1,0:T(8,128)(2,1)S(1)}, bf16[8,32,4608]{2,1,0:T(8,128)(2,1)S(1)}, u32[]{:S(2)}, u32[]{:S(2)}) collective-permute-start(bf16[8,32,4608]{2,1,0:T(8,128)(2,1)S(1)} %shard_map.62), channel_id=1, source_target_pairs={{0,1},{1,0},{2,3},{3,2},{4,5},{5,4},{6,7},{7,6},{8,9},{9,8},{10,11... | collective-permute-start | bytes 7077896 | tf_op jit(solution)/shard_map/ppermute | solution.py:30
  9.1 15.4 %collective-permute-start.5 = (bf16[8,32,4608]{2,1,0:T(8,128)(2,1)S(1)}, bf16[8,32,4608]{2,1,0:T(8,128)(2,1)S(1)}, u32[]{:S(2)}, u32[]{:S(2)}) collective-permute-start(bf16[8,32,4608]{2,1,0:T(8,128)(2,1)S(1)} %get-tuple-element.37.refs_3_), channel_id=1, source_target_pairs={{0,1},{1,0},{2,3},{3,2},{4,5},{5,4},{6,7},{7,6},{8,9},{9,8},{10,11... | collective-permute-start | bytes 7077896 | tf_op jit(solution)/shard_map/ppermute | solution.py:30
  11.0 8.3 %collective-permute-start.1 = (bf16[4,32,1152]{2,1,0:T(8,128)(2,1)S(1)}, bf16[4,32,1152]{2,1,0:T(8,128)(2,1)S(1)}, u32[]{:S(2)}, u32[]{:S(2)}) collective-permute-start(bf16[4,32,1152]{2,1,0:T(8,128)(2,1)S(1)} %get-tuple-element.39), channel_id=1, source_target_pairs={{0,4},{1,17},{2,6},{3,19},{4,0},{5,21},{6,2},{7,23},{8,12},{9,25},... | collective-permute-start | bytes 884744 | tf_op jit(solution)/shard_map/ppermute | solution.py:30
  12.4 7.8 %collective-permute-start.2 = (bf16[4,32,1152]{2,1,0:T(8,128)(2,1)S(1)}, bf16[4,32,1152]{2,1,0:T(8,128)(2,1)S(1)}, u32[]{:S(2)}, u32[]{:S(2)}) collective-permute-start(bf16[4,32,1152]{2,1,0:T(8,128)(2,1)S(1)} %get-tuple-element.40), channel_id=1, source_target_pairs={{0,2},{1,9},{2,4},{3,11},{4,6},{5,13},{6,0},{7,15},{8,10},{9,17},{... | collective-permute-start | bytes 884744 | tf_op jit(solution)/shard_map/ppermute | solution.py:30
  14.5 7.9 %collective-permute-start.3 = (bf16[4,32,1152]{2,1,0:T(8,128)(2,1)S(1)}, bf16[4,32,1152]{2,1,0:T(8,128)(2,1)S(1)}, u32[]{:S(2)}, u32[]{:S(2)}) collective-permute-start(bf16[4,32,1152]{2,1,0:T(8,128)(2,1)S(1)} %get-tuple-element.41), channel_id=1, source_target_pairs={{0,6},{1,25},{2,0},{3,27},{4,2},{5,29},{6,4},{7,31},{8,14},{9,1},{... | collective-permute-start | bytes 884744 | tf_op jit(solution)/shard_map/ppermute | solution.py:30
  22.5 20.8 %collective-permute-start.11 = (bf16[4,32,4608]{2,1,0:T(8,128)(2,1)S(1)}, bf16[4,32,4608]{2,1,0:T(8,128)(2,1)S(1)}, u32[]{:S(2)}, u32[]{:S(2)}) collective-permute-start(bf16[4,32,4608]{2,1,0:T(8,128)(2,1)S(1)} %get-tuple-element.45.refs_4_), channel_id=1, source_target_pairs={{0,2},{1,9},{2,4},{3,11},{4,6},{5,13},{6,0},{7,15},{8,10},{9,17},{... | collective-permute-start | bytes 3538952 | tf_op jit(solution)/shard_map/ppermute | solution.py:30
  23.0 20.2 %collective-permute-start.12 = (bf16[4,32,4608]{2,1,0:T(8,128)(2,1)S(1)}, bf16[4,32,4608]{2,1,0:T(8,128)(2,1)S(1)}, u32[]{:S(2)}, u32[]{:S(2)}) collective-permute-start(bf16[4,32,4608]{2,1,0:T(8,128)(2,1)S(1)} %get-tuple-element.56), channel_id=1, source_target_pairs={{0,6},{1,25},{2,0},{3,27},{4,2},{5,29},{6,4},{7,31},{8,14},{9,1},{... | collective-permute-start | bytes 3538952 | tf_op jit(solution)/shard_map/ppermute | solution.py:30
  24.6 6.8 %collective-permute-start.6 = (bf16[32,1152]{1,0:T(8,128)(2,1)S(1)}, bf16[32,1152]{1,0:T(8,128)(2,1)S(1)}, u32[]{:S(2)}, u32[]{:S(2)}) collective-permute-start(bf16[32,1152]{1,0:T(8,128)(2,1)S(1)} %get-tuple-element.47), channel_id=1, source_target_pairs={{0,16},{1,5},{2,18},{3,7},{4,20},{5,1},{6,22},{7,3},{8,24},{9,13},... | collective-permute-start | bytes 221192 | tf_op jit(solution)/shard_map/ppermute | solution.py:30
  27.9 6.4 %collective-permute-start.7 = (bf16[32,1152]{1,0:T(8,128)(2,1)S(1)}, bf16[32,1152]{1,0:T(8,128)(2,1)S(1)}, u32[]{:S(2)}, u32[]{:S(2)}) collective-permute-start(bf16[32,1152]{1,0:T(8,128)(2,1)S(1)} %get-tuple-element.48), channel_id=1, source_target_pairs={{0,8},{1,3},{2,10},{3,5},{4,12},{5,7},{6,14},{7,1},{8,16},{9,11},{... | collective-permute-start | bytes 221192 | tf_op jit(solution)/shard_map/ppermute | solution.py:30
  28.6 5.7 %collective-permute-start.8 = (bf16[32,1152]{1,0:T(8,128)(2,1)S(1)}, bf16[32,1152]{1,0:T(8,128)(2,1)S(1)}, u32[]{:S(2)}, u32[]{:S(2)}) collective-permute-start(bf16[32,1152]{1,0:T(8,128)(2,1)S(1)} %get-tuple-element.49), channel_id=1, source_target_pairs={{0,24},{1,7},{2,26},{3,1},{4,28},{5,3},{6,30},{7,5},{8,0},{9,15},{... | collective-permute-start | bytes 221192 | tf_op jit(solution)/shard_map/ppermute | solution.py:30
  34.4 7.6 %copy-start.1 = (s32[8]{0:T(128)S(1)}, s32[8]{0:T(128)}, u32[]{:S(2)}) copy-start(s32[8]{0:T(128)} %refs_0_.3) | copy-start | bytes 100
  34.4 7.5 %collective-permute-start.9 = (f32[32,640]{1,0:T(8,128)S(1)}, f32[32,640]{1,0:T(8,128)S(1)}, u32[]{:S(2)}, u32[]{:S(2)}) collective-permute-start(f32[32,640]{1,0:T(8,128)S(1)} %get-tuple-element.50.refs_2_.refs_3_), channel_id=1, source_target_pairs={{32,0},{64,32},{96,64},{128,96},{160,128},{192,160},{224,192},{33,... | collective-permute-start | bytes 245768 | tf_op jit(solution)/shard_map/ppermute | solution.py:55
  43.6 13.0 %collective-permute-start.13 = (bf16[2,32,4608]{2,1,0:T(8,128)(2,1)S(1)}, bf16[2,32,4608]{2,1,0:T(8,128)(2,1)S(1)}, u32[]{:S(2)}, u32[]{:S(2)}) collective-permute-start(bf16[2,32,4608]{2,1,0:T(8,128)(2,1)S(1)} %get-tuple-element.58), channel_id=1, source_target_pairs={{0,2},{1,9},{2,4},{3,11},{4,6},{5,13},{6,0},{7,15},{8,10},{9,17},{... | collective-permute-start | bytes 1769480 | tf_op jit(solution)/shard_map/ppermute | solution.py:30
  45.4 11.2 %collective-permute-start.14 = (bf16[2,32,4608]{2,1,0:T(8,128)(2,1)S(1)}, bf16[2,32,4608]{2,1,0:T(8,128)(2,1)S(1)}, u32[]{:S(2)}, u32[]{:S(2)}) collective-permute-start(bf16[2,32,4608]{2,1,0:T(8,128)(2,1)S(1)} %get-tuple-element.59), channel_id=1, source_target_pairs={{0,6},{1,25},{2,0},{3,27},{4,2},{5,29},{6,4},{7,31},{8,14},{9,1},{... | collective-permute-start | bytes 1769480 | tf_op jit(solution)/shard_map/ppermute | solution.py:30
  45.7 1.2 %collective-permute-start.15 = (f32[8,128]{1,0:T(8,128)S(1)}, f32[8,128]{1,0:T(8,128)S(1)}, u32[]{:S(2)}, u32[]{:S(2)}) collective-permute-start(f32[8,128]{1,0:T(8,128)S(1)} %shard_map.69.refs_3_), channel_id=1, source_target_pairs={{0,1},{1,0},{2,3},{3,2},{4,5},{5,4},{6,7},{7,6},{8,9},{9,8},{10,11... | collective-permute-start | bytes 12296 | tf_op jit(solution)/shard_map/ppermute | solution.py:30
  46.9 8.3 %collective-permute-start.16 = (f32[8,128]{1,0:T(8,128)S(1)}, f32[8,128]{1,0:T(8,128)S(1)}, u32[]{:S(2)}, u32[]{:S(2)}) collective-permute-start(f32[8,128]{1,0:T(8,128)S(1)} %add.3.refs_5_), channel_id=1, source_target_pairs={{0,4},{1,17},{2,6},{3,19},{4,0},{5,21},{6,2},{7,23},{8,12},{9,25},... | collective-permute-start | bytes 12296 | tf_op jit(solution)/shard_map/ppermute | solution.py:30
  48.3 6.8 %collective-permute-start.17 = (f32[8,128]{1,0:T(8,128)S(1)}, f32[8,128]{1,0:T(8,128)S(1)}, u32[]{:S(2)}, u32[]{:S(2)}) collective-permute-start(f32[8,128]{1,0:T(8,128)S(1)} %add.3.refs_5_), channel_id=1, source_target_pairs={{0,2},{1,9},{2,4},{3,11},{4,6},{5,13},{6,0},{7,15},{8,10},{9,17},{... | collective-permute-start | bytes 12296 | tf_op jit(solution)/shard_map/ppermute | solution.py:30
  49.9 6.8 %collective-permute-start.18 = (f32[8,128]{1,0:T(8,128)S(1)}, f32[8,128]{1,0:T(8,128)S(1)}, u32[]{:S(2)}, u32[]{:S(2)}) collective-permute-start(f32[8,128]{1,0:T(8,128)S(1)} %add.3.refs_5_), channel_id=1, source_target_pairs={{0,6},{1,25},{2,0},{3,27},{4,2},{5,29},{6,4},{7,31},{8,14},{9,1},{... | collective-permute-start | bytes 12296 | tf_op jit(solution)/shard_map/ppermute | solution.py:30
  56.6 11.0 %copy-start.2 = (s32[8]{0:T(128)S(1)}, s32[8]{0:T(128)}, u32[]{:S(2)}) copy-start(s32[8]{0:T(128)} %refs_1_.1) | copy-start | bytes 100
  57.1 11.3 %collective-permute-start.19 = (bf16[32,4736]{1,0:T(8,128)(2,1)S(1)}, bf16[32,4736]{1,0:T(8,128)(2,1)S(1)}, u32[]{:S(2)}, u32[]{:S(2)}) collective-permute-start(bf16[32,4736]{1,0:T(8,128)(2,1)S(1)} %get-tuple-element.61), channel_id=1, source_target_pairs={{0,16},{1,5},{2,18},{3,7},{4,20},{5,1},{6,22},{7,3},{8,24},{9,13},... | collective-permute-start | bytes 909320 | tf_op jit(solution)/shard_map/ppermute | solution.py:30
  58.6 10.1 %collective-permute-start.20 = (bf16[32,4736]{1,0:T(8,128)(2,1)S(1)}, bf16[32,4736]{1,0:T(8,128)(2,1)S(1)}, u32[]{:S(2)}, u32[]{:S(2)}) collective-permute-start(bf16[32,4736]{1,0:T(8,128)(2,1)S(1)} %get-tuple-element.62), channel_id=1, source_target_pairs={{0,8},{1,3},{2,10},{3,5},{4,12},{5,7},{6,14},{7,1},{8,16},{9,11},{... | collective-permute-start | bytes 909320 | tf_op jit(solution)/shard_map/ppermute | solution.py:30
  61.2 8.1 %collective-permute-start.21 = (bf16[32,4736]{1,0:T(8,128)(2,1)S(1)}, bf16[32,4736]{1,0:T(8,128)(2,1)S(1)}, u32[]{:S(2)}, u32[]{:S(2)}) collective-permute-start(bf16[32,4736]{1,0:T(8,128)(2,1)S(1)} %get-tuple-element.63), channel_id=1, source_target_pairs={{0,24},{1,7},{2,26},{3,1},{4,28},{5,3},{6,30},{7,5},{8,0},{9,15},{... | collective-permute-start | bytes 909320 | tf_op jit(solution)/shard_map/ppermute | solution.py:30
  61.8 5.8 %collective-permute-start.10 = (bf16[32,512]{1,0:T(8,128)(2,1)S(1)}, bf16[32,512]{1,0:T(8,128)(2,1)S(1)}, u32[]{:S(2)}, u32[]{:S(2)}) collective-permute-start(bf16[32,512]{1,0:T(8,128)(2,1)S(1)} %get-tuple-element.52), channel_id=1, source_target_pairs={{0,32},{32,64},{64,96},{96,128},{128,160},{160,192},{192,224},{1,3... | collective-permute-start | bytes 98312 | tf_op jit(solution)/shard_map/ppermute | solution.py:55
  (1 other events, 0.7 us)
